TPU v7x, 32 devices: a whole 2x2x4 slice. The times are simulated.
32 devices in a mesh: frame: 4 (over x, core), pixel: 8 (over z, y).
Axes of the slice: x: 2, y: 2, z: 4, core: 2. Of those that a mesh axis runs over, the one named last changes fastest.
Arguments:
- frames: bfloat16 [1024, 16384], P('frame', 'pixel'), may hold values from -6 to 6
- dead_time: float32 [16384], P('pixel'), may hold values from 0.002 to 0.02
- band_width: int32 [16384], P('pixel'), may hold values from 0 to 8
- cycle_label: int32 [16384], P('pixel'), may hold values from 0 to 1, as said below
- valid: int32 [16384], P('pixel'), may hold values from 0 to 1
Outputs:
- two_time: float32 [1024, 2, 1024], P(('frame', 'pixel'))
Inputs may be any that keep to these rules, and one draw needn't show every extreme that they name: `cycle_label`: every cycle holds at least one pixel with valid 1.
All inputs are finite; a program needn't handle non-finite values.
Results may differ from a plain program's by a relative error of at most 0.004.
Values may be sent and summed in bfloat16 or wider, within the bound.
No kernel may reach another device: no remote copies, remote signals or barrier semaphores. Data moves between devices by JAX's collectives and lax.ppermute only.
A program may use at most 64 MiB of HBM per device.

v0:
```python
import jax
import jax.numpy as jnp
from jax import lax
from jax.sharding import PartitionSpec as P

CYCLES = 2
BAND = 8


def band_smooth(running, width_local, nframes):
    npixels = running.shape[1]
    frame_idx = jnp.arange(nframes, dtype=jnp.int32)[:, None]
    total = jnp.zeros((nframes, npixels), jnp.float32)
    divisor = jnp.ones((nframes, npixels), jnp.float32)
    for width in range(BAND + 1):
        if width > 0:
            upper_rows = jnp.concatenate(
                [
                    running[width + 1 :],
                    jnp.broadcast_to(running[nframes : nframes + 1], (width, npixels)),
                ],
                axis=0,
            )
            lower_rows = jnp.concatenate(
                [jnp.broadcast_to(running[0:1], (width, npixels)), running[0 : nframes - width]],
                axis=0,
            )
        else:
            upper_rows = running[1:]
            lower_rows = running[0:nframes]
        span = (
            jnp.minimum(frame_idx + width, nframes - 1) - jnp.maximum(frame_idx - width, 0) + 1
        ).astype(jnp.float32)
        chosen = width_local[None, :] == width
        total = jnp.where(chosen, upper_rows - lower_rows, total)
        divisor = jnp.where(chosen, span, divisor)
    return (total / divisor).astype(jnp.bfloat16)


def shards(frames, dead_time, band_width, cycle_label, valid):
    local = lax.all_to_all(frames, "frame", split_axis=1, concat_axis=0, tiled=True)
    nframes = local.shape[0]
    npixels = local.shape[1]
    offset = lax.axis_index("frame") * npixels
    dead_local = lax.dynamic_slice_in_dim(dead_time, offset, npixels, 0)
    width_local = lax.dynamic_slice_in_dim(band_width, offset, npixels, 0)
    label_local = lax.dynamic_slice_in_dim(cycle_label, offset, npixels, 0)
    valid_local = lax.dynamic_slice_in_dim(valid, offset, npixels, 0)
    count_rate = 4.0 + local.astype(jnp.float32)
    corrected = count_rate / (1.0 - dead_local[None, :] * count_rate)
    running = jnp.concatenate(
        [jnp.zeros((1, npixels), jnp.float32), jnp.cumsum(corrected, axis=0)], axis=0
    )
    smoothed = band_smooth(running, width_local, nframes)
    cycle_ids = jnp.arange(CYCLES, dtype=jnp.int32)[:, None]
    member = ((label_local[None, :] == cycle_ids) & (valid_local[None, :] == 1)).astype(
        jnp.bfloat16
    )
    counts = jnp.sum(member.astype(jnp.float32), axis=1)
    cycle_sum = lax.dot_general(
        smoothed, member, (((1,), (1,)), ((), ())), preferred_element_type=jnp.float32
    )
    cycle_sum, counts = lax.psum((cycle_sum, counts), ("frame", "pixel"))
    own_rows = nframes // lax.axis_size(("frame", "pixel"))
    weighted = (smoothed[:, None, :] * member[None, :, :]).reshape(
        lax.axis_size(("frame", "pixel")) * own_rows * CYCLES, npixels
    )
    product = lax.dot_general(
        weighted, smoothed, (((1,), (1,)), ((), ())), preferred_element_type=jnp.float32
    )
    gram = lax.psum_scatter(
        product.reshape(lax.axis_size(("frame", "pixel")) * own_rows, CYCLES * nframes),
        ("frame", "pixel"),
        scatter_dimension=0,
        tiled=True,
    )
    mean = cycle_sum / counts[None, :]
    row_start = (
        lax.axis_index("frame") * lax.axis_size("pixel") + lax.axis_index("pixel")
    ) * own_rows
    mean_rows = lax.dynamic_slice_in_dim(mean, row_start, own_rows, 0)
    gram = gram.reshape(own_rows, CYCLES, nframes)
    return gram / counts[None, :, None] - mean_rows[:, :, None] * jnp.transpose(mean)[None, :, :]


def solution(mesh):
    in_specs = (P("frame", "pixel"), P("pixel"), P("pixel"), P("pixel"), P("pixel"))
    out_specs = P(("frame", "pixel"), None, None)
    return jax.shard_map(shards, mesh=mesh, in_specs=in_specs, out_specs=out_specs, check_vma=False)
```

profile of v0, /device:TPU:0, one launch (start us, length us, event | category | flops | bytes accessed | tf_op | source)
XLA Modules:
  0.0 273.2 jit_solution(16179887267767051064)
XLA Ops:
  6.5 2.3 copy.15
  8.8 4.2 %all-to-all-start = ((bf16[256,4,512]{0,2,1:T(8,128)(2,1)}), bf16[256,4,512]{0,2,1:T(8,128)(2,1)S(1)}, u32[]{:S(2)}, u32[]{:S(2)}) async-start(bf16[256,4,512]{0,2,1:T(8,128)(2,1)} %bitcast), calls=%async_computation | async-start | bytes 2097152 | tf_op jit(solution)/shard_map/all_to_all | solution.py:41
  13.0 0.8 dynamic_slice.16
  13.8 0.8 dynamic_slice.17
  14.5 0.8 broadcast_compare_fusion.8
  15.4 0.1 convert_reduce_fusion
  15.5 12.0 %all-to-all-done = bf16[256,4,512]{0,2,1:T(8,128)(2,1)S(1)} async-done(((bf16[256,4,512]{0,2,1:T(8,128)(2,1)}), bf16[256,4,512]{0,2,1:T(8,128)(2,1)S(1)}, u32[]{:S(2)}, u32[]{:S(2)}) %all-to-all-start) | async-done | bytes 1048608 | tf_op jit(solution)/shard_map/all_to_all | solution.py:41
  27.5 1.5 add_bitcast_fusion
  29.0 1.9 copy.16
  30.9 0.3 bitcast_divide_fusion
  31.2 1.3 fusion.10
  32.6 0.2 broadcast_add_fusion
  32.8 1.2 copy.18
  34.0 0.5 fusion.62
  34.6 0.7 fusion.63
  35.3 0.7 fusion.64
  36.0 0.7 fusion.65
  36.7 0.7 fusion.66
  37.4 0.7 fusion.67
  38.1 0.7 fusion.68
  38.8 1.8 fusion.61
  40.7 15.8 %fusion.12 = bf16[1024,512]{1,0:T(8,128)(2,1)S(1)} fusion(f32[1024,512]{1,0:T(8,128)S(1)} %bitcast.33, f32[1023,512]{1,0:T(8,128)S(1)} %get-tuple-element.24, f32[1,512]{1,0:T(1,128)S(1)} %slice.90, f32[1023,512]{1,0:T(8,128)S(1)} %get-tuple-element.23, f32[1022,512]{1,0:T(8,128)S(1)} %get-tuple-element.22, f32[2,512]{1,0:T(2,128)S(1)} %broadcast_in_dim.201, ...), kind=kLoop, calls=%fused_computation.23 | loop fusion | flops 19398656 | bytes 36667904 | tf_op jit(solution)/shard_map/convert_element_type | solution.py:37
  56.4 2.2 broadcast_multiply_fusion
  58.6 2.2 mul.53
  60.8 7.2 %fusion.69 = f32[2048,1024]{1,0:T(8,128)} fusion(bf16[2048,512]{1,0:T(8,128)(2,1)} %mul.53, bf16[1024,512]{1,0:T(8,128)(2,1)S(1)} %fusion.12), kind=kOutput, calls=%fused_computation.123 | convolution fusion | flops 2147483648 | bytes 11534336 | tf_op jit(solution)/shard_map/dot_general | solution.py:68
  68.0 9.9 %reshape.258 = f32[1024,2048]{1,0:T(8,128)} reshape(f32[2048,1024]{1,0:T(8,128)} %fusion.69) | data formatting | bytes 16777216 | tf_op jit(solution)/shard_map/reshape | solution.py:72
  78.0 0.4 fusion.56
  78.3 47.0 %all-reduce.9 = (f32[2]{0:T(128)S(1)}, f32[1024,2]{0,1:T(2,128)S(1)}) all-reduce(f32[2]{0:T(128)S(1)} %get-tuple-element.7, f32[1024,2]{0,1:T(2,128)S(1)} %fusion.56), channel_id=1, replica_groups=mesh['frame'=4,'pixel'=8] {'frame','pixel'}, use_global_device_ids=true, to_apply=%region_4.5 | all-reduce | flops 2050 | bytes 16400 | tf_op jit(solution)/shard_map/psum | solution.py:63
  125.5 0.1 copy.19
  125.7 138.6 %reduce-scatter.2.cloned.1.call-done = f32[32,2048]{1,0:T(8,128)} async-done(((f32[1024,2048]{1,0:T(8,128)}), f32[32,2048]{1,0:T(8,128)}) %reduce-scatter.2.cloned.1.call-update) | async-done | bytes 262160 | tf_op jit(solution)/shard_map/reduce_scatter | solution.py:71
  264.3 1.2 reshape.259
  265.5 0.9 divide_subtract_fusion
  (21 shorter events, 0.3 us)
Async XLA Ops:
  8.8 18.7 %all-to-all-start = ((bf16[256,4,512]{0,2,1:T(8,128)(2,1)}), bf16[256,4,512]{0,2,1:T(8,128)(2,1)S(1)}, u32[]{:S(2)}, u32[]{:S(2)}) async-start(bf16[256,4,512]{0,2,1:T(8,128)(2,1)} %bitcast), calls=%async_computation | async-start | bytes 2097152 | tf_op jit(solution)/shard_map/all_to_all | solution.py:41
  13.0 251.3 %reduce-scatter.2.cloned.1.call-start = ((), (), s32[]{:S(2)}) async-start(), calls=%async_computation.2 | async-start | bytes 8650752 | tf_op jit(solution)/shard_map/reduce_scatter | solution.py:71
Sparse Core Ops, SparseCore 0:
  78.1 186.1 reduce-scatter.1
where the time goes:
time: 274 us; the launch traced here: 273 us
  waiting for transfers between devices  151 us (55%)
  blocking collectives  47 us (17%)
  local copies, waits for them, and re-layouts  26.9 us (10%)
  other arithmetic  23.3 us (9%)
  between operations  13.6 us (5%)
  matrix products  7.56 us (3%)
  starting transfers between devices  4.21 us (2%)
    reduce_scatter x1, waiting for transfers between devices, shards(): lax.psum_scatter(product.reshape(lax.axis_size(('frame', 'pixel')) * own_...  139 us
    psum x1, blocking collectives, shards(): cycle_sum, counts = lax.psum((cycle_sum, counts), ('frame', 'pixel'))  47 us
    convert_element_type x1, other arithmetic, band_smooth(): return (total / divisor).astype(jnp.bfloat16)  15.8 us
    all_to_all x1, waiting for transfers between devices, shards(): lax.all_to_all(frames, 'frame', split_axis=1, concat_axis=0, tiled=True)  12 us
    reshape x1, local copies, waits for them, and re-layouts, shards(): product.reshape(lax.axis_size(('frame', 'pixel')) * own_rows, CYCLES * nf...  9.91 us
    dot_general x1, matrix products, shards(): lax.dot_general(weighted, smoothed, (((1,), (1,)), ((), ())), preferred_e...  7.19 us
    slice x8, local copies, waits for them, and re-layouts, band_smooth(): running[width + 1:]  6.52 us
  transfers between devices with their start and end apart: 2, of which 2 were waited for; matrix products, arithmetic and copies ran while one was open for 1% of the time, Pallas kernels for 0%

commit v1 on v0

v1 whole, which is shorter than its diff:
```python
import functools
import jax
import jax.numpy as jnp
from jax import lax
from jax.experimental import pallas as pl
from jax.experimental.pallas import tpu as pltpu
from jax.sharding import PartitionSpec as P

CYCLES = 2
BAND = 8
HALO = 16
LANE = 128
f32 = jnp.float32
bf16 = jnp.bfloat16
NT = (((1,), (1,)), ((), ()))


def cost(flops, nbytes):
    return pl.CostEstimate(flops=flops, bytes_accessed=nbytes, transcendentals=0)


def correct(raw, dead):
    rate = 4.0 + raw.astype(f32)
    return rate / (1.0 - dead * rate)


def band_sum(c_ref, at, n, lanes, width):
    acc = c_ref[pl.ds(at, n), lanes]
    for k in range(1, BAND + 1):
        pair = c_ref[pl.ds(at - k, n), lanes] + c_ref[pl.ds(at + k, n), lanes]
        acc = acc + jnp.where(width >= k, pair, 0.0)
    return acc


def middle_kernel(raw_ref, dead_ref, width_ref, out_ref, c_ref, *, tile):
    rows, px = raw_ref.shape
    quarter = rows // 4
    for col in range(px // LANE):
        lanes = pl.ds(col * LANE, LANE)
        dead = dead_ref[lanes][None, :]
        width = width_ref[lanes][None, :]
        inverse = 1.0 / (2 * width + 1).astype(f32)
        c_ref[:, lanes] = correct(raw_ref[pl.ds(quarter - HALO, 2 * quarter + 2 * HALO), lanes], dead)
        for r in range(2 * quarter // tile):
            acc = band_sum(c_ref, HALO + r * tile, tile, lanes, width)
            out_ref[pl.ds(r * tile, tile), lanes] = (acc * inverse).astype(bf16)


def edge_kernel(raw_ref, up_ref, down_ref, dead_ref, width_ref, out_ref, c_ref, *, tile, nframes):
    rows, px = raw_ref.shape
    quarter = rows // 4
    block = lax.axis_index("frame")
    begin = block * rows
    has_up = (block > 0).astype(f32)
    has_down = ((block + 1) * rows < nframes).astype(f32)
    span = quarter + 2 * HALO
    for col in range(px // LANE):
        lanes = pl.ds(col * LANE, LANE)
        dead = dead_ref[lanes][None, :]
        width = width_ref[lanes][None, :]
        c_ref[pl.ds(0, HALO), lanes] = correct(up_ref[:, lanes], dead) * has_up
        c_ref[pl.ds(HALO, quarter + HALO), lanes] = correct(raw_ref[pl.ds(0, quarter + HALO), lanes], dead)
        c_ref[pl.ds(span, quarter + HALO), lanes] = correct(raw_ref[pl.ds(rows - quarter - HALO, quarter + HALO), lanes], dead)
        c_ref[pl.ds(span + quarter + HALO, HALO), lanes] = correct(down_ref[:, lanes], dead) * has_down
        for half in range(2):
            for r in range(quarter // tile):
                acc = band_sum(c_ref, half * span + HALO + r * tile, tile, lanes, width)
                first = begin + half * (rows - quarter) + r * tile
                t = first + lax.broadcasted_iota(jnp.int32, (tile, LANE), 0)
                terms = jnp.minimum(t + width, nframes - 1) - jnp.maximum(t - width, 0) + 1
                out_ref[pl.ds(half * quarter + r * tile, tile), lanes] = (acc / terms.astype(f32)).astype(bf16)


def smooth_middle(raw, dead, width):
    rows, px = raw.shape
    lanes = min(px, 1024)
    return pl.pallas_call(
        functools.partial(middle_kernel, tile=min(32, rows // 4)),
        grid=(px // lanes,),
        in_specs=[pl.BlockSpec((rows, lanes), lambda i: (0, i))] + [pl.BlockSpec((lanes,), lambda i: (i,))] * 2,
        out_specs=pl.BlockSpec((rows // 2, lanes), lambda i: (0, i)),
        out_shape=jax.ShapeDtypeStruct((rows // 2, px), bf16),
        scratch_shapes=[pltpu.VMEM((rows // 2 + 2 * HALO, lanes), f32)],
        cost_estimate=cost(rows * px * 60, rows * px * 3),
        name="smooth_middle",
    )(raw, dead, width)


def smooth_edges(raw, up, down, dead, width, nframes):
    rows, px = raw.shape
    lanes = min(px, 1024)
    column = lambda i: (0, i)
    return pl.pallas_call(
        functools.partial(edge_kernel, tile=min(32, rows // 4), nframes=nframes),
        grid=(px // lanes,),
        in_specs=[pl.BlockSpec((rows, lanes), column)]
        + [pl.BlockSpec((HALO, lanes), column)] * 2
        + [pl.BlockSpec((lanes,), lambda i: (i,))] * 2,
        out_specs=pl.BlockSpec((rows // 2, lanes), column),
        out_shape=jax.ShapeDtypeStruct((rows // 2, px), bf16),
        scratch_shapes=[pltpu.VMEM((rows // 2 + 4 * HALO, lanes), f32)],
        cost_estimate=cost(rows * px * 60, rows * px * 3),
        name="smooth_edges",
    )(raw, up, down, dead, width)


def gram_kernel(label_ref, valid_ref, mid_ref, edge_ref, *refs, ncols, own):
    cols, rest = refs[:ncols], refs[ncols:]
    out_ref, acc_ref = rest[0], rest[-1]
    half, px = mid_ref.shape
    quarter = half // 2
    rows = 2 * half
    step = pl.program_id(0)
    label = label_ref[...][None, :]
    used = valid_ref[...][None, :] == 1
    member = [((label == q) & used).astype(f32) for q in range(CYCLES)]
    weight = [jnp.broadcast_to(m, (16, px)).astype(bf16) for m in member]
    mid, edge = mid_ref[...], edge_ref[...]
    natural = jnp.concatenate([edge[:quarter], mid, edge[quarter:]], axis=0)
    left = jnp.concatenate([natural * w[:1] for w in weight] + weight, axis=0)
    right = jnp.concatenate([c[...] for c in cols] + [jnp.ones((LANE, px), bf16)], axis=0)
    product = lax.dot_general(left, right, NT, preferred_element_type=f32)

    @pl.when(step == 0)
    def _():
        acc_ref[...] = product

    @pl.when(step > 0)
    def _():
        acc_ref[...] += product

    @pl.when(step == pl.num_programs(0) - 1)
    def _():
        width = out_ref.shape[-1]
        for q in range(CYCLES):
            base = CYCLES * rows + 16 * q
            count = acc_ref[pl.ds(base, 1), pl.ds(width, LANE)]
            mean = acc_ref[pl.ds(base, 1), pl.ds(0, width)] / jnp.maximum(count[:, :1], 1.0)
            total = acc_ref[pl.ds(q * rows, rows), pl.ds(width, LANE)]
            for j in range(width // LANE):
                lanes = pl.ds(j * LANE, LANE)
                block = acc_ref[pl.ds(q * rows, rows), lanes]
                out_ref[q, :, lanes] = (block - total * mean[:, j * LANE : (j + 1) * LANE]).astype(bf16)
            if own:
                rest[1][pl.ds(q, 1), :] = mean[:, :rows]
                rest[1][pl.ds(CYCLES + q, 1), :] = jnp.broadcast_to(count[:, :1], (1, rows))


def gram(label, valid, mid, edge, cols, own):
    half, px = mid.shape
    rows = 2 * half
    lanes = min(px, 1024)
    width = sum(c.shape[0] for c in cols)
    column = lambda i: (0, i)
    whole = lambda *shape: pl.BlockSpec(shape, lambda i: (0,) * len(shape))
    out_shape = [jax.ShapeDtypeStruct((CYCLES, rows, width), bf16)]
    out_specs = [whole(CYCLES, rows, width)]
    if own:
        out_shape.append(jax.ShapeDtypeStruct((2 * CYCLES, rows), f32))
        out_specs.append(whole(2 * CYCLES, rows))
    return pl.pallas_call(
        functools.partial(gram_kernel, ncols=len(cols), own=own),
        grid=(px // lanes,),
        in_specs=[pl.BlockSpec((lanes,), lambda i: (i,))] * 2
        + [pl.BlockSpec((s.shape[0], lanes), column) for s in (mid, edge, *cols)],
        out_specs=out_specs,
        out_shape=out_shape,
        scratch_shapes=[pltpu.VMEM((CYCLES * (rows + 16), width + LANE), f32)],
        cost_estimate=cost(2 * CYCLES * rows * width * px, 2 * (rows + width) * px),
        name="gram_own" if own else "gram_cross",
    )(label, valid, mid, edge, *cols)


def shards(frames, dead_time, band_width, cycle_label, valid):
    nblocks = lax.axis_size("frame")
    ngroups = lax.axis_size("pixel")
    rows = frames.shape[0]
    nframes = rows * nblocks
    half, quarter = rows // 2, rows // 4
    own_rows = rows // ngroups
    me, group = lax.axis_index("frame"), lax.axis_index("pixel")

    def swap(x, axis, bit):
        return lax.ppermute(x, axis, [(i, i ^ bit) for i in range(lax.axis_size(axis))])

    down = lax.ppermute(frames[:HALO], "frame", [(i + 1, i) for i in range(nblocks - 1)])
    up = lax.ppermute(frames[rows - HALO :], "frame", [(i, i + 1) for i in range(nblocks - 1)])
    mid = smooth_middle(frames, dead_time, band_width)
    far_mid = {j: swap(mid, "frame", j) for j in range(2, nblocks, 2)}
    near_mid = swap(mid, "frame", 1)
    edge = smooth_edges(frames, up, down, dead_time, band_width, nframes)
    far_edge = {j: swap(edge, "frame", j) for j in range(2, nblocks, 2)}
    near_edge = swap(edge, "frame", 1)

    def reduce(x, stats):
        x = x.reshape(CYCLES, ngroups, own_rows, x.shape[-1])
        bit = 1
        while bit < ngroups:
            x = x.reshape(CYCLES, -1, 2, own_rows, x.shape[-1])
            mine = (group // bit) % 2
            keep = lax.dynamic_index_in_dim(x, mine, 2, keepdims=False)
            send = lax.dynamic_index_in_dim(x, 1 - mine, 2, keepdims=False)
            x = keep.astype(f32) + swap(send, "pixel", bit).astype(f32)
            if stats is not None:
                stats = jnp.concatenate([stats, swap(stats, "pixel", bit)], axis=0)
            bit *= 2
            if bit < ngroups:
                x = x.astype(bf16)
        return x.reshape(CYCLES, own_rows, x.shape[-1]), stats

    own, stats = gram(cycle_label, valid, mid, edge, (mid, edge, near_mid, near_edge), True)
    own, stats = reduce(own, stats[None])
    mids = [own[..., :half], own[..., rows : rows + half]]
    edges = [own[..., half:rows], own[..., rows + half :]]
    all_stats = [stats, swap(stats, "frame", 1)]
    for j in range(2, nblocks, 2):
        far = swap(stats, "frame", j)
        all_stats += [far, swap(far, "frame", 1)]
        for source, parts in ((far_mid[j], mids), (far_edge[j], edges)):
            part = gram(cycle_label, valid, mid, edge, (source, swap(source, "frame", 1)), False)[0]
            part = reduce(part, None)[0]
            parts += [part[..., :half], part[..., half:]]

    def natural(m, e):
        return jnp.concatenate([e[..., :quarter], m, e[..., quarter:]], axis=-1)

    def in_order(blocks):
        bit = 1
        while bit < nblocks:
            swapped = [blocks[j ^ bit] for j in range(nblocks)]
            flip = (me // bit) % 2 == 1
            blocks = [jnp.where(flip, s, b) for s, b in zip(swapped, blocks)]
            bit *= 2
        return jnp.concatenate(blocks, axis=-1)

    all_stats = [natural(s[..., :half], s[..., half:]) for s in all_stats]
    row_stats = lax.dynamic_slice_in_dim(all_stats[0], group * own_rows, own_rows, 2)
    all_stats = in_order(all_stats)
    number = all_stats[:, CYCLES:, :1]
    counts = jnp.sum(number, axis=0)
    share = number / counts
    grand = jnp.sum(all_stats[:, :CYCLES] * share, axis=0)
    grand_rows = jnp.sum(row_stats[:, :CYCLES] * share, axis=0)
    between = jnp.einsum(
        "dqr,dqc->qrc",
        (row_stats[:, :CYCLES] - grand_rows) * share,
        all_stats[:, :CYCLES] - grand,
        precision=lax.Precision.HIGHEST,
    )
    within = in_order([natural(m, e) for m, e in zip(mids, edges)])
    return jnp.transpose(within / counts[:, :, None] + between, (1, 0, 2))


def solution(mesh):
    in_specs = (P("frame", "pixel"), P("pixel"), P("pixel"), P("pixel"), P("pixel"))
    out_specs = P(("frame", "pixel"), None, None)
    return jax.shard_map(shards, mesh=mesh, in_specs=in_specs, out_specs=out_specs, check_vma=False)
```

time: 274 us -> 88.8 us (0.32)
  waiting for transfers between devices: 151 us -> 23.6 us
  blocking collectives: 47 us -> 0 us
  starting transfers between devices: 4.21 us -> 30.7 us
  Pallas kernels: 0 us -> 21 us
  other arithmetic: 23.3 us -> 2.46 us
  local copies, waits for them, and re-layouts: 26.9 us -> 9.89 us
  between operations: 13.6 us -> 0.37 us
  matrix products: 7.56 us -> 0.42 us
    reduce_scatter x1 -> x0, waiting for transfers between devices: 139 us -> none  [shards(): lax.psum_scatter(product.reshape(lax.axis_size(('frame', 'pixel')) * own_...]
    psum x1 -> x0, blocking collectives: 47 us -> none  [shards(): cycle_sum, counts = lax.psum((cycle_sum, counts), ('frame', 'pixel'))]
    ppermute x0 -> x23, starting transfers between devices: none -> 30.7 us  [the longest x21 27.1 us: swap(): lax.ppermute(x, axis, [(i, i ^ bit) for i in range(lax.axis_size(axis))])]
    ppermute x0 -> x23, waiting for transfers between devices: none -> 23.6 us  [the longest x21 23.6 us: swap(): lax.ppermute(x, axis, [(i, i ^ bit) for i in range(lax.axis_size(axis))])]
    pallas_call x0 -> x5, Pallas kernels: none -> 21 us  [the longest x3 12.3 us: gram(): pl.pallas_call(functools.partial(gram_kernel, ncols=len(cols), own=own),...]
    convert_element_type x6, other arithmetic: 15.8 us -> 0.25 us  [reduce(): x = x.astype(bf16)]
    all_to_all x1 -> x0, waiting for transfers between devices: 12 us -> none  [shards(): lax.all_to_all(frames, 'frame', split_axis=1, concat_axis=0, tiled=True)]
    reshape x2 -> x0, local copies, waits for them, and re-layouts: 11.1 us -> none  [the longest x1 9.91 us: shards(): product.reshape(lax.axis_size(('frame', 'pixel')) * own_rows, CYCLES * nf...]
  transfers between devices with their start and end apart: 2 -> 23, of which waited for: 2 -> 11; matrix products, arithmetic and copies ran while one was open for 1% -> 6% of each run, Pallas kernels for 0% -> 24%
where the time goes in v1:
time: 88.8 us; the launch traced here: 88.4 us
  starting transfers between devices  30.7 us (35%)
  waiting for transfers between devices  23.6 us (27%)
  Pallas kernels  21 us (24%)
  local copies, waits for them, and re-layouts  9.89 us (11%)
  other arithmetic  2.46 us (3%)
    ppermute x21, starting transfers between devices, swap(): lax.ppermute(x, axis, [(i, i ^ bit) for i in range(lax.axis_size(axis))])  27.1 us
    ppermute x21, waiting for transfers between devices, swap(): lax.ppermute(x, axis, [(i, i ^ bit) for i in range(lax.axis_size(axis))])  23.6 us
    pallas_call x3, Pallas kernels, gram(): pl.pallas_call(functools.partial(gram_kernel, ncols=len(cols), own=own),...  12.3 us
    pallas_call x1, Pallas kernels, smooth_edges(): pl.pallas_call(functools.partial(edge_kernel, tile=min(32, rows // 4), nf...  4.57 us
    unnamed x27, local copies, waits for them, and re-layouts  4.48 us
    pallas_call x1, Pallas kernels, smooth_middle(): pl.pallas_call(functools.partial(middle_kernel, tile=min(32, rows // 4)),...  4.08 us
    squeeze x6, local copies, waits for them, and re-layouts, reduce(): send = lax.dynamic_index_in_dim(x, 1 - mine, 2, keepdims=False)  2.88 us
    ppermute x1, starting transfers between devices, shards(): lax.ppermute(frames[rows - HALO:], 'frame', [(i, i + 1) for i in range(nb...  2.36 us
  transfers between devices with their start and end apart: 23, of which 11 were waited for; matrix products, arithmetic and copies ran while one was open for 6% of the time, Pallas kernels for 24%

profile of v1, /device:TPU:0, one launch (start us, length us, event | category | flops | bytes accessed | tf_op | source)
XLA Modules:
  0.0 88.4 jit_solution(892560660165450421)
XLA Ops:
  0.9 2.4 %collective-permute-start = (bf16[16,2048]{1,0:T(8,128)(2,1)S(1)}, bf16[16,2048]{1,0:T(8,128)(2,1)S(1)}, u32[]{:S(2)}, u32[]{:S(2)}) collective-permute-start(bf16[16,2048]{1,0:T(8,128)(2,1)S(1)} %get-tuple-element.20), channel_id=1, source_target_pairs={{0,8},{8,16},{16,24},{1,9},{9,17},{17,25},{2,10},{10,18},{18,26},{... | collective-permute-start | bytes 196616 | tf_op jit(solution)/shard_map/ppermute | solution.py:187
  3.3 1.3 %collective-permute-start.1 = (bf16[16,2048]{1,0:T(8,128)(2,1)S(1)}, bf16[16,2048]{1,0:T(8,128)(2,1)S(1)}, u32[]{:S(2)}, u32[]{:S(2)}) collective-permute-start(bf16[16,2048]{1,0:T(8,128)(2,1)S(1)} %get-tuple-element.19), channel_id=1, source_target_pairs={{8,0},{16,8},{24,16},{9,1},{17,9},{25,17},{10,2},{18,10},{26,18},{... | collective-permute-start | bytes 196616 | tf_op jit(solution)/shard_map/ppermute | solution.py:186
  4.6 4.1 %smooth_middle.1.mid_ref.refs_0_ = bf16[128,2048]{1,0:T(8,128)(2,1)} custom-call(bf16[256,2048]{1,0:T(8,128)(2,1)} %raw_ref.3, f32[2048]{0:T(1024)} %dead_ref.3, s32[2048]{0:T(1024)} %width_ref.3), custom_call_target="tpu_custom_call" | custom-call | flops 31457280 | bytes 1572864 | tf_op jit(solution)/shard_map/smooth_middle/pallas_call | solution.py:77
  8.6 3.2 %collective-permute-start.12 = (bf16[128,2048]{1,0:T(8,128)(2,1)}, bf16[128,2048]{1,0:T(8,128)(2,1)S(1)}, u32[]{:S(2)}, u32[]{:S(2)}) collective-permute-start(bf16[128,2048]{1,0:T(8,128)(2,1)} %smooth_middle.1.mid_ref.refs_0_), channel_id=1, source_target_pairs={{0,8},{8,0},{16,24},{24,16},{1,9},{9,1},{17,25},{25,17},{2,10},{10... | collective-permute-start | bytes 1572872 | tf_op jit(solution)/shard_map/ppermute | solution.py:184
  13.1 4.6 %smooth_edges.1.edge_ref.refs_1_ = bf16[128,2048]{1,0:T(8,128)(2,1)} custom-call(bf16[256,2048]{1,0:T(8,128)(2,1)} %raw_ref.3, bf16[16,2048]{1,0:T(8,128)(2,1)} %copy-done.8, bf16[16,2048]{1,0:T(8,128)(2,1)} %copy-done.9, f32[2048]{0:T(1024)} %dead_ref.3, s32[2048]{0:T(1024)} %width_ref.3), custom_call_target="tpu_custom_call" | custom-call | flops 31457280 | bytes 1572864 | tf_op jit(solution)/shard_map/smooth_edges/pallas_call | solution.py:93
  17.7 2.1 %collective-permute-start.7 = (bf16[128,2048]{1,0:T(8,128)(2,1)S(1)}, bf16[128,2048]{1,0:T(8,128)(2,1)S(1)}, u32[]{:S(2)}, u32[]{:S(2)}) collective-permute-start(bf16[128,2048]{1,0:T(8,128)(2,1)S(1)} %copy-done), channel_id=1, source_target_pairs={{0,16},{8,24},{16,0},{24,8},{1,17},{9,25},{17,1},{25,9},{2,18},{10... | collective-permute-start | bytes 1572872 | tf_op jit(solution)/shard_map/ppermute | solution.py:184
  21.5 4.8 %gram_own.1 = (bf16[2,256,512]{2,1,0:T(8,128)(2,1)}, f32[4,256]{1,0:T(4,128)}) custom-call(s32[2048]{0:T(1024)} %label_ref.5, s32[2048]{0:T(1024)} %valid_ref.5, bf16[128,2048]{1,0:T(8,128)(2,1)} %smooth_middle.1.mid_ref.refs_0_, bf16[128,2048]{1,0:T(8,128)(2,1)} %smooth_edges.1.edge_ref.refs_1_, bf16[128,2048]{1,0:T(8,128)(2,1)} %smooth_middle.1.mid_ref.refs_0_, ...), custom_call_target="tpu_custom_call" | custom-call | flops 1073741824 | bytes 3145728 | tf_op jit(solution)/shard_map/gram_own/pallas_call | solution.py:161
  26.3 1.5 %collective-permute-start.17 = (f32[1,4,256]{2,1,0:T(4,128)}, f32[1,4,256]{2,1,0:T(4,128)S(1)}, u32[]{:S(2)}, u32[]{:S(2)}) collective-permute-start(f32[1,4,256]{2,1,0:T(4,128)} %bitcast.79), channel_id=1, source_target_pairs={{0,1},{1,0},{2,3},{3,2},{4,5},{5,4},{6,7},{7,6},{8,9},{9,8},{10,11... | collective-permute-start | bytes 12296 | tf_op jit(solution)/shard_map/ppermute | solution.py:184
  27.8 2.3 %collective-permute-done.17 = f32[1,4,256]{2,1,0:T(4,128)S(1)} collective-permute-done((f32[1,4,256]{2,1,0:T(4,128)}, f32[1,4,256]{2,1,0:T(4,128)S(1)}, u32[]{:S(2)}, u32[]{:S(2)}) %collective-permute-start.17) | collective-permute-done | bytes 4128 | tf_op jit(solution)/shard_map/ppermute | solution.py:184
  30.8 1.6 %collective-permute-start.18 = (f32[2,4,256]{2,1,0:T(4,128)S(1)}, f32[2,4,256]{2,1,0:T(4,128)S(1)}, u32[]{:S(2)}, u32[]{:S(2)}) collective-permute-start(f32[2,4,256]{2,1,0:T(4,128)S(1)} %pad_maximum_fusion.13), channel_id=1, source_target_pairs={{0,2},{1,3},{2,0},{3,1},{4,6},{5,7},{6,4},{7,5},{8,10},{9,11},{10,... | collective-permute-start | bytes 24584 | tf_op jit(solution)/shard_map/ppermute | solution.py:184
  32.5 1.9 %collective-permute-done.18 = f32[2,4,256]{2,1,0:T(4,128)S(1)} collective-permute-done((f32[2,4,256]{2,1,0:T(4,128)S(1)}, f32[2,4,256]{2,1,0:T(4,128)S(1)}, u32[]{:S(2)}, u32[]{:S(2)}) %collective-permute-start.18) | collective-permute-done | bytes 8224 | tf_op jit(solution)/shard_map/ppermute | solution.py:184
  34.5 2.7 %collective-permute-start.19 = (f32[4,4,256]{2,1,0:T(4,128)S(1)}, f32[4,4,256]{2,1,0:T(4,128)S(1)}, u32[]{:S(2)}, u32[]{:S(2)}) collective-permute-start(f32[4,4,256]{2,1,0:T(4,128)S(1)} %pad_maximum_fusion.12), channel_id=1, source_target_pairs={{0,4},{1,5},{2,6},{3,7},{4,0},{5,1},{6,2},{7,3},{8,12},{9,13},{10,... | collective-permute-start | bytes 49160 | tf_op jit(solution)/shard_map/ppermute | solution.py:184
  37.1 1.0 %dynamic-slice_bitcast_fusion = bf16[2,4,32,512]{3,2,1,0:T(8,128)(2,1)S(1)} fusion(bf16[2,4,2,32,512]{4,3,2,1,0:T(8,128)(2,1)} %bitcast.69, s32[]{:T(128)S(6)} %select_n.181), kind=kLoop, calls=%fused_computation.11 | loop fusion | bytes 524292 | tf_op jit(solution)/shard_map/jit(dynamic_index_in_dim)/squeeze | solution.py:202
  38.1 1.6 %collective-permute-start.14 = (bf16[2,4,32,512]{3,2,1,0:T(8,128)(2,1)S(1)}, bf16[2,4,32,512]{3,2,1,0:T(8,128)(2,1)S(1)}, u32[]{:S(2)}, u32[]{:S(2)}) collective-permute-start(bf16[2,4,32,512]{3,2,1,0:T(8,128)(2,1)S(1)} %dynamic-slice_bitcast_fusion), channel_id=1, source_target_pairs={{0,1},{1,0},{2,3},{3,2},{4,5},{5,4},{6,7},{7,6},{8,9},{9,8},{10,11... | collective-permute-start | bytes 786440 | tf_op jit(solution)/shard_map/ppermute | solution.py:184
  39.7 3.6 %collective-permute-done.2.refs_0_ = bf16[128,2048]{1,0:T(8,128)(2,1)S(1)} collective-permute-done((bf16[128,2048]{1,0:T(8,128)(2,1)}, bf16[128,2048]{1,0:T(8,128)(2,1)S(1)}, u32[]{:S(2)}, u32[]{:S(2)}) %collective-permute-start.2) | collective-permute-done | bytes 524320 | tf_op jit(solution)/shard_map/ppermute | solution.py:184
  43.3 1.8 %collective-permute-start.20 = (f32[8,4,256]{2,1,0:T(4,128)S(1)}, f32[8,4,256]{2,1,0:T(4,128)S(1)}, u32[]{:S(2)}, u32[]{:S(2)}) collective-permute-start(f32[8,4,256]{2,1,0:T(4,128)S(1)} %pad_maximum_fusion.7), channel_id=1, source_target_pairs={{0,16},{8,24},{16,0},{24,8},{1,17},{9,25},{17,1},{25,9},{2,18},{10... | collective-permute-start | bytes 98312 | tf_op jit(solution)/shard_map/ppermute | solution.py:184
  45.4 1.9 %collective-permute-done.20 = f32[8,4,256]{2,1,0:T(4,128)S(1)} collective-permute-done((f32[8,4,256]{2,1,0:T(4,128)S(1)}, f32[8,4,256]{2,1,0:T(4,128)S(1)}, u32[]{:S(2)}, u32[]{:S(2)}) %collective-permute-start.20) | collective-permute-done | bytes 32800 | tf_op jit(solution)/shard_map/ppermute | solution.py:184
  47.5 1.0 %collective-permute-done.21 = f32[8,4,256]{2,1,0:T(4,128)S(1)} collective-permute-done((f32[8,4,256]{2,1,0:T(4,128)S(1)}, f32[8,4,256]{2,1,0:T(4,128)S(1)}, u32[]{:S(2)}, u32[]{:S(2)}) %collective-permute-start.21) | collective-permute-done | bytes 32800 | tf_op jit(solution)/shard_map/ppermute | solution.py:184
  50.0 1.6 %collective-permute-start.15 = (bf16[2,2,32,512]{3,2,0,1:T(8,128)(2,1)S(1)}, bf16[2,2,32,512]{3,2,0,1:T(8,128)(2,1)S(1)}, u32[]{:S(2)}, u32[]{:S(2)}) collective-permute-start(bf16[2,2,32,512]{3,2,0,1:T(8,128)(2,1)S(1)} %bitcast.75), channel_id=1, source_target_pairs={{0,2},{1,3},{2,0},{3,1},{4,6},{5,7},{6,4},{7,5},{8,10},{9,11},{10,... | collective-permute-start | bytes 393224 | tf_op jit(solution)/shard_map/ppermute | solution.py:184
  51.8 3.9 %collective-permute-done.15 = bf16[2,2,32,512]{3,2,0,1:T(8,128)(2,1)S(1)} collective-permute-done((bf16[2,2,32,512]{3,2,0,1:T(8,128)(2,1)S(1)}, bf16[2,2,32,512]{3,2,0,1:T(8,128)(2,1)S(1)}, u32[]{:S(2)}, u32[]{:S(2)}) %collective-permute-start.15) | collective-permute-done | bytes 131104 | tf_op jit(solution)/shard_map/ppermute | solution.py:184
  55.7 2.7 %collective-permute-start.16 = (bf16[2,1,32,512]{3,2,0,1:T(8,128)(2,1)S(1)}, bf16[2,1,32,512]{3,2,0,1:T(8,128)(2,1)S(1)}, u32[]{:S(2)}, u32[]{:S(2)}) collective-permute-start(bf16[2,1,32,512]{3,2,0,1:T(8,128)(2,1)S(1)} %constant_dynamic-slice_fusion), channel_id=1, source_target_pairs={{0,4},{1,5},{2,6},{3,7},{4,0},{5,1},{6,2},{7,3},{8,12},{9,13},{10,... | collective-permute-start | bytes 196616 | tf_op jit(solution)/shard_map/ppermute | solution.py:184
  59.2 3.7 %gram_cross.3 = bf16[2,256,256]{2,1,0:T(8,128)(2,1)} custom-call(s32[2048]{0:T(1024)} %label_ref.5, s32[2048]{0:T(1024)} %valid_ref.5, bf16[128,2048]{1,0:T(8,128)(2,1)} %smooth_middle.1.mid_ref.refs_0_, bf16[128,2048]{1,0:T(8,128)(2,1)} %smooth_edges.1.edge_ref.refs_1_, bf16[128,2048]{1,0:T(8,128)(2,1)} %copy-done.5, bf16[128,2048]{1,0:T(8,128)(2,1)} %copy-done.7), custom_call_target="tpu_custom_call" | custom-call | flops 536870912 | bytes 2097152 | tf_op jit(solution)/shard_map/gram_cross/pallas_call | solution.py:161
  62.9 0.9 %dynamic-slice_bitcast_fusion.1 = bf16[2,4,32,256]{3,2,1,0:T(8,128)(2,1)S(1)} fusion(bf16[2,4,2,32,256]{4,3,2,1,0:T(8,128)(2,1)} %bitcast.64, s32[]{:T(128)S(6)} %select_n.181), kind=kLoop, calls=%fused_computation.19 | loop fusion | bytes 262148 | tf_op jit(solution)/shard_map/jit(dynamic_index_in_dim)/squeeze | solution.py:202
  63.8 1.6 %collective-permute-start.9 = (bf16[2,4,32,256]{3,2,1,0:T(8,128)(2,1)S(1)}, bf16[2,4,32,256]{3,2,1,0:T(8,128)(2,1)S(1)}, u32[]{:S(2)}, u32[]{:S(2)}) collective-permute-start(bf16[2,4,32,256]{3,2,1,0:T(8,128)(2,1)S(1)} %dynamic-slice_bitcast_fusion.1), channel_id=1, source_target_pairs={{0,1},{1,0},{2,3},{3,2},{4,5},{5,4},{6,7},{7,6},{8,9},{9,8},{10,11... | collective-permute-start | bytes 393224 | tf_op jit(solution)/shard_map/ppermute | solution.py:184
  66.4 3.7 %gram_cross.2 = bf16[2,256,256]{2,1,0:T(8,128)(2,1)} custom-call(s32[2048]{0:T(1024)} %label_ref.5, s32[2048]{0:T(1024)} %valid_ref.5, bf16[128,2048]{1,0:T(8,128)(2,1)} %smooth_middle.1.mid_ref.refs_0_, bf16[128,2048]{1,0:T(8,128)(2,1)} %smooth_edges.1.edge_ref.refs_1_, bf16[128,2048]{1,0:T(8,128)(2,1)} %copy-done.4, bf16[128,2048]{1,0:T(8,128)(2,1)} %copy-done.6), custom_call_target="tpu_custom_call" | custom-call | flops 536870912 | bytes 2097152 | tf_op jit(solution)/shard_map/gram_cross/pallas_call | solution.py:161
  70.1 1.0 %dynamic-slice_bitcast_fusion.2 = bf16[2,4,32,256]{3,2,1,0:T(8,128)(2,1)S(1)} fusion(bf16[2,4,2,32,256]{4,3,2,1,0:T(8,128)(2,1)} %bitcast.66, s32[]{:T(128)S(6)} %select_n.181), kind=kLoop, calls=%fused_computation.20 | loop fusion | bytes 262148 | tf_op jit(solution)/shard_map/jit(dynamic_index_in_dim)/squeeze | solution.py:202
  71.7 1.6 %collective-permute-start.10 = (bf16[2,2,32,256]{3,2,0,1:T(8,128)(2,1)S(1)}, bf16[2,2,32,256]{3,2,0,1:T(8,128)(2,1)S(1)}, u32[]{:S(2)}, u32[]{:S(2)}) collective-permute-start(bf16[2,2,32,256]{3,2,0,1:T(8,128)(2,1)S(1)} %bitcast.77), channel_id=1, source_target_pairs={{0,2},{1,3},{2,0},{3,1},{4,6},{5,7},{6,4},{7,5},{8,10},{9,11},{10,... | collective-permute-start | bytes 196616 | tf_op jit(solution)/shard_map/ppermute | solution.py:184
  73.4 2.7 %collective-permute-done.4 = bf16[2,4,32,256]{3,2,1,0:T(8,128)(2,1)S(1)} collective-permute-done((bf16[2,4,32,256]{3,2,1,0:T(8,128)(2,1)S(1)}, bf16[2,4,32,256]{3,2,1,0:T(8,128)(2,1)S(1)}, u32[]{:S(2)}, u32[]{:S(2)}) %collective-permute-start.4) | collective-permute-done | bytes 131104 | tf_op jit(solution)/shard_map/ppermute | solution.py:184
  76.6 1.6 %collective-permute-start.5 = (bf16[2,2,32,256]{3,2,0,1:T(8,128)(2,1)S(1)}, bf16[2,2,32,256]{3,2,0,1:T(8,128)(2,1)S(1)}, u32[]{:S(2)}, u32[]{:S(2)}) collective-permute-start(bf16[2,2,32,256]{3,2,0,1:T(8,128)(2,1)S(1)} %bitcast.78), channel_id=1, source_target_pairs={{0,2},{1,3},{2,0},{3,1},{4,6},{5,7},{6,4},{7,5},{8,10},{9,11},{10,... | collective-permute-start | bytes 196616 | tf_op jit(solution)/shard_map/ppermute | solution.py:184
  78.3 2.9 %collective-permute-done.11 = bf16[2,1,32,256]{3,2,0,1:T(8,128)(2,1)S(1)} collective-permute-done((bf16[2,1,32,256]{3,2,0,1:T(8,128)(2,1)S(1)}, bf16[2,1,32,256]{3,2,0,1:T(8,128)(2,1)S(1)}, u32[]{:S(2)}, u32[]{:S(2)}) %collective-permute-start.11) | collective-permute-done | bytes 32800 | tf_op jit(solution)/shard_map/ppermute | solution.py:184
  81.7 2.2 %collective-permute-start.6 = (bf16[2,1,32,256]{3,2,0,1:T(8,128)(2,1)S(1)}, bf16[2,1,32,256]{3,2,0,1:T(8,128)(2,1)S(1)}, u32[]{:S(2)}, u32[]{:S(2)}) collective-permute-start(bf16[2,1,32,256]{3,2,0,1:T(8,128)(2,1)S(1)} %constant_dynamic-slice_fusion.6), channel_id=1, source_target_pairs={{0,4},{1,5},{2,6},{3,7},{4,0},{5,1},{6,2},{7,3},{8,12},{9,13},{10,... | collective-permute-start | bytes 98312 | tf_op jit(solution)/shard_map/ppermute | solution.py:184
  84.0 2.6 %collective-permute-done.6 = bf16[2,1,32,256]{3,2,0,1:T(8,128)(2,1)S(1)} collective-permute-done((bf16[2,1,32,256]{3,2,0,1:T(8,128)(2,1)S(1)}, bf16[2,1,32,256]{3,2,0,1:T(8,128)(2,1)S(1)}, u32[]{:S(2)}, u32[]{:S(2)}) %collective-permute-start.6) | collective-permute-done | bytes 32800 | tf_op jit(solution)/shard_map/ppermute | solution.py:184
  (100 shorter events, 11.8 us)
Async XLA Ops:
  0.9 11.0 %collective-permute-start = (bf16[16,2048]{1,0:T(8,128)(2,1)S(1)}, bf16[16,2048]{1,0:T(8,128)(2,1)S(1)}, u32[]{:S(2)}, u32[]{:S(2)}) collective-permute-start(bf16[16,2048]{1,0:T(8,128)(2,1)S(1)} %get-tuple-element.20), channel_id=1, source_target_pairs={{0,8},{8,16},{16,24},{1,9},{9,17},{17,25},{2,10},{10,18},{18,26},{... | collective-permute-start | bytes 196616 | tf_op jit(solution)/shard_map/ppermute | solution.py:187
  3.3 8.6 %collective-permute-start.1 = (bf16[16,2048]{1,0:T(8,128)(2,1)S(1)}, bf16[16,2048]{1,0:T(8,128)(2,1)S(1)}, u32[]{:S(2)}, u32[]{:S(2)}) collective-permute-start(bf16[16,2048]{1,0:T(8,128)(2,1)S(1)} %get-tuple-element.19), channel_id=1, source_target_pairs={{8,0},{16,8},{24,16},{9,1},{17,9},{25,17},{10,2},{18,10},{26,18},{... | collective-permute-start | bytes 196616 | tf_op jit(solution)/shard_map/ppermute | solution.py:186
  8.6 9.1 %copy-start = (bf16[128,2048]{1,0:T(8,128)(2,1)S(1)}, bf16[128,2048]{1,0:T(8,128)(2,1)}, u32[]{:S(2)}) copy-start(bf16[128,2048]{1,0:T(8,128)(2,1)} %smooth_middle.1.mid_ref.refs_0_) | copy-start | bytes 1572868
  8.6 11.2 %collective-permute-start.12 = (bf16[128,2048]{1,0:T(8,128)(2,1)}, bf16[128,2048]{1,0:T(8,128)(2,1)S(1)}, u32[]{:S(2)}, u32[]{:S(2)}) collective-permute-start(bf16[128,2048]{1,0:T(8,128)(2,1)} %smooth_middle.1.mid_ref.refs_0_), channel_id=1, source_target_pairs={{0,8},{8,0},{16,24},{24,16},{1,9},{9,1},{17,25},{25,17},{2,10},{10... | collective-permute-start | bytes 1572872 | tf_op jit(solution)/shard_map/ppermute | solution.py:184
  17.7 2.2 %collective-permute-start.13 = (bf16[128,2048]{1,0:T(8,128)(2,1)}, bf16[128,2048]{1,0:T(8,128)(2,1)S(1)}, u32[]{:S(2)}, u32[]{:S(2)}) collective-permute-start(bf16[128,2048]{1,0:T(8,128)(2,1)} %smooth_edges.1.edge_ref.refs_1_), channel_id=1, source_target_pairs={{0,8},{8,0},{16,24},{24,16},{1,9},{9,1},{17,25},{25,17},{2,10},{10... | collective-permute-start | bytes 1572872 | tf_op jit(solution)/shard_map/ppermute | solution.py:184
  17.7 14.8 %collective-permute-start.7 = (bf16[128,2048]{1,0:T(8,128)(2,1)S(1)}, bf16[128,2048]{1,0:T(8,128)(2,1)S(1)}, u32[]{:S(2)}, u32[]{:S(2)}) collective-permute-start(bf16[128,2048]{1,0:T(8,128)(2,1)S(1)} %copy-done), channel_id=1, source_target_pairs={{0,16},{8,24},{16,0},{24,8},{1,17},{9,25},{17,1},{25,9},{2,18},{10... | collective-permute-start | bytes 1572872 | tf_op jit(solution)/shard_map/ppermute | solution.py:184
  19.8 23.4 %collective-permute-start.2 = (bf16[128,2048]{1,0:T(8,128)(2,1)}, bf16[128,2048]{1,0:T(8,128)(2,1)S(1)}, u32[]{:S(2)}, u32[]{:S(2)}) collective-permute-start(bf16[128,2048]{1,0:T(8,128)(2,1)} %smooth_edges.1.edge_ref.refs_1_), channel_id=1, source_target_pairs={{0,16},{8,24},{16,0},{24,8},{1,17},{9,25},{17,1},{25,9},{2,18},{10... | collective-permute-start | bytes 1572872 | tf_op jit(solution)/shard_map/ppermute | solution.py:184
  26.3 3.8 %collective-permute-start.17 = (f32[1,4,256]{2,1,0:T(4,128)}, f32[1,4,256]{2,1,0:T(4,128)S(1)}, u32[]{:S(2)}, u32[]{:S(2)}) collective-permute-start(f32[1,4,256]{2,1,0:T(4,128)} %bitcast.79), channel_id=1, source_target_pairs={{0,1},{1,0},{2,3},{3,2},{4,5},{5,4},{6,7},{7,6},{8,9},{9,8},{10,11... | collective-permute-start | bytes 12296 | tf_op jit(solution)/shard_map/ppermute | solution.py:184
  30.8 3.7 %collective-permute-start.18 = (f32[2,4,256]{2,1,0:T(4,128)S(1)}, f32[2,4,256]{2,1,0:T(4,128)S(1)}, u32[]{:S(2)}, u32[]{:S(2)}) collective-permute-start(f32[2,4,256]{2,1,0:T(4,128)S(1)} %pad_maximum_fusion.13), channel_id=1, source_target_pairs={{0,2},{1,3},{2,0},{3,1},{4,6},{5,7},{6,4},{7,5},{8,10},{9,11},{10,... | collective-permute-start | bytes 24584 | tf_op jit(solution)/shard_map/ppermute | solution.py:184
  32.4 2.1 %copy-start.10 = (f32[4,256]{1,0:T(4,128)S(1)}, f32[4,256]{1,0:T(4,128)}, u32[]{:S(2)}) copy-start(f32[4,256]{1,0:T(4,128)} %get-tuple-element.8) | copy-start | bytes 12292
  32.5 16.2 %copy-start.5 = (bf16[128,2048]{1,0:T(8,128)(2,1)}, bf16[128,2048]{1,0:T(8,128)(2,1)S(1)}, u32[]{:S(2)}) copy-start(bf16[128,2048]{1,0:T(8,128)(2,1)S(1)} %collective-permute-done.7.refs_0_) | copy-start | bytes 1572868
  32.5 25.8 %collective-permute-start.8 = (bf16[128,2048]{1,0:T(8,128)(2,1)S(1)}, bf16[128,2048]{1,0:T(8,128)(2,1)S(1)}, u32[]{:S(2)}, u32[]{:S(2)}) collective-permute-start(bf16[128,2048]{1,0:T(8,128)(2,1)S(1)} %collective-permute-done.7.refs_0_), channel_id=1, source_target_pairs={{0,8},{8,0},{16,24},{24,16},{1,9},{9,1},{17,25},{25,17},{2,10},{10... | collective-permute-start | bytes 1572872 | tf_op jit(solution)/shard_map/ppermute | solution.py:184
  34.5 8.8 %collective-permute-start.19 = (f32[4,4,256]{2,1,0:T(4,128)S(1)}, f32[4,4,256]{2,1,0:T(4,128)S(1)}, u32[]{:S(2)}, u32[]{:S(2)}) collective-permute-start(f32[4,4,256]{2,1,0:T(4,128)S(1)} %pad_maximum_fusion.12), channel_id=1, source_target_pairs={{0,4},{1,5},{2,6},{3,7},{4,0},{5,1},{6,2},{7,3},{8,12},{9,13},{10,... | collective-permute-start | bytes 49160 | tf_op jit(solution)/shard_map/ppermute | solution.py:184
  38.1 11.8 %collective-permute-start.14 = (bf16[2,4,32,512]{3,2,1,0:T(8,128)(2,1)S(1)}, bf16[2,4,32,512]{3,2,1,0:T(8,128)(2,1)S(1)}, u32[]{:S(2)}, u32[]{:S(2)}) collective-permute-start(bf16[2,4,32,512]{3,2,1,0:T(8,128)(2,1)S(1)} %dynamic-slice_bitcast_fusion), channel_id=1, source_target_pairs={{0,1},{1,0},{2,3},{3,2},{4,5},{5,4},{6,7},{7,6},{8,9},{9,8},{10,11... | collective-permute-start | bytes 786440 | tf_op jit(solution)/shard_map/ppermute | solution.py:184
  43.3 5.8 %copy-start.4 = (bf16[128,2048]{1,0:T(8,128)(2,1)}, bf16[128,2048]{1,0:T(8,128)(2,1)S(1)}, u32[]{:S(2)}) copy-start(bf16[128,2048]{1,0:T(8,128)(2,1)S(1)} %collective-permute-done.2.refs_0_) | copy-start | bytes 1572868
  43.3 22.3 %collective-permute-start.3 = (bf16[128,2048]{1,0:T(8,128)(2,1)S(1)}, bf16[128,2048]{1,0:T(8,128)(2,1)S(1)}, u32[]{:S(2)}, u32[]{:S(2)}) collective-permute-start(bf16[128,2048]{1,0:T(8,128)(2,1)S(1)} %collective-permute-done.2.refs_0_), channel_id=1, source_target_pairs={{0,8},{8,0},{16,24},{24,16},{1,9},{9,1},{17,25},{25,17},{2,10},{10... | collective-permute-start | bytes 1572872 | tf_op jit(solution)/shard_map/ppermute | solution.py:184
  43.3 4.0 %collective-permute-start.20 = (f32[8,4,256]{2,1,0:T(4,128)S(1)}, f32[8,4,256]{2,1,0:T(4,128)S(1)}, u32[]{:S(2)}, u32[]{:S(2)}) collective-permute-start(f32[8,4,256]{2,1,0:T(4,128)S(1)} %pad_maximum_fusion.7), channel_id=1, source_target_pairs={{0,16},{8,24},{16,0},{24,8},{1,17},{9,25},{17,1},{25,9},{2,18},{10... | collective-permute-start | bytes 98312 | tf_op jit(solution)/shard_map/ppermute | solution.py:184
  45.1 2.3 %collective-permute-start.22 = (f32[8,4,256]{2,1,0:T(4,128)S(1)}, f32[8,4,256]{2,1,0:T(4,128)S(1)}, u32[]{:S(2)}, u32[]{:S(2)}) collective-permute-start(f32[8,4,256]{2,1,0:T(4,128)S(1)} %pad_maximum_fusion.7), channel_id=1, source_target_pairs={{0,8},{8,0},{16,24},{24,16},{1,9},{9,1},{17,25},{25,17},{2,10},{10... | collective-permute-start | bytes 98312 | tf_op jit(solution)/shard_map/ppermute | solution.py:184
  47.3 1.2 %collective-permute-start.21 = (f32[8,4,256]{2,1,0:T(4,128)S(1)}, f32[8,4,256]{2,1,0:T(4,128)S(1)}, u32[]{:S(2)}, u32[]{:S(2)}) collective-permute-start(f32[8,4,256]{2,1,0:T(4,128)S(1)} %collective-permute-done.20), channel_id=1, source_target_pairs={{0,8},{8,0},{16,24},{24,16},{1,9},{9,1},{17,25},{25,17},{2,10},{10... | collective-permute-start | bytes 98312 | tf_op jit(solution)/shard_map/ppermute | solution.py:184
  48.8 1.1 %copy-start.3 = (bf16[2,256,512]{2,1,0:T(8,128)(2,1)S(1)}, bf16[2,256,512]{2,1,0:T(8,128)(2,1)}, u32[]{:S(2)}) copy-start(bf16[2,256,512]{2,1,0:T(8,128)(2,1)} %get-tuple-element.7) | copy-start | bytes 1572868
  50.0 5.6 %collective-permute-start.15 = (bf16[2,2,32,512]{3,2,0,1:T(8,128)(2,1)S(1)}, bf16[2,2,32,512]{3,2,0,1:T(8,128)(2,1)S(1)}, u32[]{:S(2)}, u32[]{:S(2)}) collective-permute-start(bf16[2,2,32,512]{3,2,0,1:T(8,128)(2,1)S(1)} %bitcast.75), channel_id=1, source_target_pairs={{0,2},{1,3},{2,0},{3,1},{4,6},{5,7},{6,4},{7,5},{8,10},{9,11},{10,... | collective-permute-start | bytes 393224 | tf_op jit(solution)/shard_map/ppermute | solution.py:184
  55.7 9.7 %collective-permute-start.16 = (bf16[2,1,32,512]{3,2,0,1:T(8,128)(2,1)S(1)}, bf16[2,1,32,512]{3,2,0,1:T(8,128)(2,1)S(1)}, u32[]{:S(2)}, u32[]{:S(2)}) collective-permute-start(bf16[2,1,32,512]{3,2,0,1:T(8,128)(2,1)S(1)} %constant_dynamic-slice_fusion), channel_id=1, source_target_pairs={{0,4},{1,5},{2,6},{3,7},{4,0},{5,1},{6,2},{7,3},{8,12},{9,13},{10,... | collective-permute-start | bytes 196616 | tf_op jit(solution)/shard_map/ppermute | solution.py:184
  58.4 0.8 copy-start.7
  63.8 7.8 %collective-permute-start.9 = (bf16[2,4,32,256]{3,2,1,0:T(8,128)(2,1)S(1)}, bf16[2,4,32,256]{3,2,1,0:T(8,128)(2,1)S(1)}, u32[]{:S(2)}, u32[]{:S(2)}) collective-permute-start(bf16[2,4,32,256]{3,2,1,0:T(8,128)(2,1)S(1)} %dynamic-slice_bitcast_fusion.1), channel_id=1, source_target_pairs={{0,1},{1,0},{2,3},{3,2},{4,5},{5,4},{6,7},{7,6},{8,9},{9,8},{10,11... | collective-permute-start | bytes 393224 | tf_op jit(solution)/shard_map/ppermute | solution.py:184
  65.6 0.8 copy-start.6
  70.1 1.5 %copy-start.1 = (bf16[2,256,256]{2,1,0:T(8,128)(2,1)S(1)}, bf16[2,256,256]{2,1,0:T(8,128)(2,1)}, u32[]{:S(2)}) copy-start(bf16[2,256,256]{2,1,0:T(8,128)(2,1)} %gram_cross.3) | copy-start | bytes 786436
  71.1 5.0 %collective-permute-start.4 = (bf16[2,4,32,256]{3,2,1,0:T(8,128)(2,1)S(1)}, bf16[2,4,32,256]{3,2,1,0:T(8,128)(2,1)S(1)}, u32[]{:S(2)}, u32[]{:S(2)}) collective-permute-start(bf16[2,4,32,256]{3,2,1,0:T(8,128)(2,1)S(1)} %dynamic-slice_bitcast_fusion.2), channel_id=1, source_target_pairs={{0,1},{1,0},{2,3},{3,2},{4,5},{5,4},{6,7},{7,6},{8,9},{9,8},{10,11... | collective-permute-start | bytes 393224 | tf_op jit(solution)/shard_map/ppermute | solution.py:184
  71.7 4.4 %copy-start.2 = (bf16[2,256,256]{2,1,0:T(8,128)(2,1)S(1)}, bf16[2,256,256]{2,1,0:T(8,128)(2,1)}, u32[]{:S(2)}) copy-start(bf16[2,256,256]{2,1,0:T(8,128)(2,1)} %gram_cross.2) | copy-start | bytes 786436
  71.7 4.4 %collective-permute-start.10 = (bf16[2,2,32,256]{3,2,0,1:T(8,128)(2,1)S(1)}, bf16[2,2,32,256]{3,2,0,1:T(8,128)(2,1)S(1)}, u32[]{:S(2)}, u32[]{:S(2)}) collective-permute-start(bf16[2,2,32,256]{3,2,0,1:T(8,128)(2,1)S(1)} %bitcast.77), channel_id=1, source_target_pairs={{0,2},{1,3},{2,0},{3,1},{4,6},{5,7},{6,4},{7,5},{8,10},{9,11},{10,... | collective-permute-start | bytes 196616 | tf_op jit(solution)/shard_map/ppermute | solution.py:184
  76.2 5.0 %collective-permute-start.11 = (bf16[2,1,32,256]{3,2,0,1:T(8,128)(2,1)S(1)}, bf16[2,1,32,256]{3,2,0,1:T(8,128)(2,1)S(1)}, u32[]{:S(2)}, u32[]{:S(2)}) collective-permute-start(bf16[2,1,32,256]{3,2,0,1:T(8,128)(2,1)S(1)} %constant_dynamic-slice_fusion.3), channel_id=1, source_target_pairs={{0,4},{1,5},{2,6},{3,7},{4,0},{5,1},{6,2},{7,3},{8,12},{9,13},{10,... | collective-permute-start | bytes 98312 | tf_op jit(solution)/shard_map/ppermute | solution.py:184
  76.6 5.0 %collective-permute-start.5 = (bf16[2,2,32,256]{3,2,0,1:T(8,128)(2,1)S(1)}, bf16[2,2,32,256]{3,2,0,1:T(8,128)(2,1)S(1)}, u32[]{:S(2)}, u32[]{:S(2)}) collective-permute-start(bf16[2,2,32,256]{3,2,0,1:T(8,128)(2,1)S(1)} %bitcast.78), channel_id=1, source_target_pairs={{0,2},{1,3},{2,0},{3,1},{4,6},{5,7},{6,4},{7,5},{8,10},{9,11},{10,... | collective-permute-start | bytes 196616 | tf_op jit(solution)/shard_map/ppermute | solution.py:184
  81.7 4.9 %collective-permute-start.6 = (bf16[2,1,32,256]{3,2,0,1:T(8,128)(2,1)S(1)}, bf16[2,1,32,256]{3,2,0,1:T(8,128)(2,1)S(1)}, u32[]{:S(2)}, u32[]{:S(2)}) collective-permute-start(bf16[2,1,32,256]{3,2,0,1:T(8,128)(2,1)S(1)} %constant_dynamic-slice_fusion.6), channel_id=1, source_target_pairs={{0,4},{1,5},{2,6},{3,7},{4,0},{5,1},{6,2},{7,3},{8,12},{9,13},{10,... | collective-permute-start | bytes 98312 | tf_op jit(solution)/shard_map/ppermute | solution.py:184
  (4 other events, 2.9 us)

commit v2 on v0

v2 whole, which is shorter than its diff:
```python
import functools
import jax
import jax.numpy as jnp
from jax import lax
from jax.experimental import pallas as pl
from jax.experimental.pallas import tpu as pltpu
from jax.sharding import PartitionSpec as P

CYCLES = 2
BAND = 8
HALO = 16
EDGE_PART = 4
STAT = 8
STAT_ROWS = 16
LANE = 128
f32 = jnp.float32
bf16 = jnp.bfloat16
NT = (((1,), (1,)), ((), ()))
NN = (((1,), (0,)), ((), ()))
EXACT = lax.Precision.HIGHEST


def kernel_call(body, name, args, outs, scratch=(), in_specs=None, mib=4):
    vmem = pl.BlockSpec(memory_space=pltpu.VMEM)
    return pl.pallas_call(
        body,
        in_specs=in_specs or [vmem] * len(args),
        out_specs=[vmem] * len(outs),
        out_shape=[jax.ShapeDtypeStruct(shape, dtype) for shape, dtype in outs],
        scratch_shapes=list(scratch),
        compiler_params=pltpu.CompilerParams(vmem_limit_bytes=mib * 2**20),
        cost_estimate=pl.CostEstimate(flops=0, bytes_accessed=2**18, transcendentals=0),
        name=name,
    )(*args)


def correct(raw, dead):
    rate = 4.0 + raw.astype(f32)
    return rate / (1.0 - dead * rate)


def band_sum(c_ref, at, n, width):
    acc = c_ref[pl.ds(at, n), :]
    for k in range(1, BAND + 1):
        pair = c_ref[pl.ds(at - k, n), :] + c_ref[pl.ds(at + k, n), :]
        acc = acc + jnp.where(width >= k, pair, 0.0)
    return acc


def halo_kernel(frames_ref, near_ref, far_ref, ends_ref, sems):
    rows = frames_ref.shape[0]
    copies = [
        pltpu.make_async_copy(frames_ref.at[pl.ds(at, HALO)], ends_ref.at[i], sems.at[i])
        for i, at in enumerate((0, rows - HALO))
    ]
    for copy in copies:
        copy.start()
    for copy in copies:
        copy.wait()
    even = lax.axis_index("frame") % 2 == 0
    first, last = ends_ref[0], ends_ref[1]
    far_ref[...] = jnp.where(even, first, last)
    near_ref[...] = jnp.where(even, last, first)


def halos(frames):
    rows, px = frames.shape
    return kernel_call(
        halo_kernel,
        "halos",
        (frames,),
        [((HALO, px), bf16)] * 2,
        [pltpu.VMEM((2, HALO, px), bf16), pltpu.SemaphoreType.DMA((2,))],
        in_specs=[pl.BlockSpec(memory_space=pltpu.HBM)],
    )


def middle_kernel(frames_ref, dead_hbm, width_hbm, mid_ref, rim_ref, dead_ref, width_ref, raw_ref, c_ref, sems):
    rows, px = frames_ref.shape
    edge = rim_ref.shape[0] // 2 - HALO
    tile = 32
    chunk = min(512, px)
    small = [pltpu.make_async_copy(dead_hbm, dead_ref, sems.at[0]), pltpu.make_async_copy(width_hbm, width_ref, sems.at[1])]
    large = [
        pltpu.make_async_copy(frames_ref.at[:, pl.ds(i * chunk, chunk)], raw_ref.at[:, pl.ds(i * chunk, chunk)], sems.at[2 + i])
        for i in range(px // chunk)
    ]
    for copy in small + large:
        copy.start()
    for copy in small:
        copy.wait()
    for i, copy in enumerate(large):
        copy.wait()
        part = pl.ds(i * chunk, chunk)
        rim_ref[pl.ds(0, edge + HALO), part] = raw_ref[pl.ds(0, edge + HALO), part]
        rim_ref[pl.ds(edge + HALO, edge + HALO), part] = raw_ref[pl.ds(rows - edge - HALO, edge + HALO), part]
        for col in range(chunk // LANE):
            lanes = pl.ds(i * chunk + col * LANE, LANE)
            dead = dead_ref[lanes][None, :]
            width = width_ref[lanes][None, :]
            inverse = 1.0 / (2 * width + 1).astype(f32)
            c_ref[...] = correct(raw_ref[pl.ds(edge - HALO, rows - 2 * edge + 2 * HALO), lanes], dead)
            for r in range((rows - 2 * edge) // tile):
                acc = band_sum(c_ref, HALO + r * tile, tile, width)
                mid_ref[pl.ds(r * tile, tile), lanes] = (acc * inverse).astype(bf16)


def edge_kernel(rim_ref, near_ref, far_ref, dead_ref, width_ref, out_ref, c_ref, *, nframes):
    px = rim_ref.shape[1]
    edge = out_ref.shape[0] // 2
    rows = nframes // lax.axis_size("frame")
    tile = 32
    block = lax.axis_index("frame")
    even = block % 2 == 0
    begin = block * rows
    has_up = (block > 0).astype(f32)
    has_down = ((block + 1) * rows < nframes).astype(f32)
    span = edge + 2 * HALO
    for col in range(px // LANE):
        lanes = pl.ds(col * LANE, LANE)
        dead = dead_ref[lanes][None, :]
        width = width_ref[lanes][None, :]
        near, far = near_ref[:, lanes], far_ref[:, lanes]
        c_ref[pl.ds(0, HALO), :] = correct(jnp.where(even, far, near), dead) * has_up
        c_ref[pl.ds(HALO, edge + HALO), :] = correct(rim_ref[pl.ds(0, edge + HALO), lanes], dead)
        c_ref[pl.ds(span, edge + HALO), :] = correct(rim_ref[pl.ds(edge + HALO, edge + HALO), lanes], dead)
        c_ref[pl.ds(span + edge + HALO, HALO), :] = correct(jnp.where(even, near, far), dead) * has_down
        for half in range(2):
            for r in range(edge // tile):
                acc = band_sum(c_ref, half * span + HALO + r * tile, tile, width)
                first = begin + half * (rows - edge) + r * tile
                t = first + lax.broadcasted_iota(jnp.int32, (tile, LANE), 0)
                terms = jnp.minimum(t + width, nframes - 1) - jnp.maximum(t - width, 0) + 1
                out_ref[pl.ds(half * edge + r * tile, tile), lanes] = (acc / terms.astype(f32)).astype(bf16)


def smooth_middle(frames, dead, width, edge):
    rows, px = frames.shape
    mid = rows - 2 * edge
    return kernel_call(
        middle_kernel,
        "smooth_middle",
        (frames, dead, width),
        [((mid, px), bf16), ((2 * (edge + HALO), px), bf16), ((px,), f32), ((px,), jnp.int32)],
        [pltpu.VMEM((rows, px), bf16), pltpu.VMEM((mid + 2 * HALO, LANE), f32), pltpu.SemaphoreType.DMA((2 + px // min(512, px),))],
        in_specs=[pl.BlockSpec(memory_space=pltpu.HBM)] * 3,
    )


def smooth_edges(rim, near, far, dead, width, nframes):
    edge = rim.shape[0] // 2 - HALO
    return kernel_call(
        functools.partial(edge_kernel, nframes=nframes),
        "smooth_edges",
        (rim, near, far, dead, width),
        [((2 * edge, rim.shape[1]), bf16)],
        [pltpu.VMEM((2 * (edge + 2 * HALO), LANE), f32)],
    )[0]


def hold_kernel(*refs):
    pass


def hold(x, *tokens):
    anywhere = pl.BlockSpec(memory_space=pl.ANY)
    return pl.pallas_call(
        hold_kernel,
        in_specs=[anywhere] * (1 + len(tokens)),
        out_specs=anywhere,
        out_shape=jax.ShapeDtypeStruct(x.shape, x.dtype),
        input_output_aliases={0: 0},
        compiler_params=pltpu.CompilerParams(vmem_limit_bytes=2**20),
        cost_estimate=pl.CostEstimate(flops=0, bytes_accessed=0, transcendentals=0),
        name="hold",
    )(x, *tokens)


def tree_order(n):
    return [0] if n == 1 else [2 * s + bit for bit in range(2) for s in tree_order(n // 2)]


def centre(product_ref, total_ref, mean, keep_ref, send_ref, groups):
    rows = product_ref.shape[0] // CYCLES - 16
    size = rows // groups
    me = lax.axis_index("pixel")
    for at, slot in enumerate(tree_order(groups)):
        out_ref = send_ref if slot % 2 else keep_ref
        place = (at % (groups // 2)) * CYCLES * size
        for q in range(CYCLES):
            begin = pl.multiple_of(q * rows + (me ^ slot) * size, size)
            total = total_ref[pl.ds(begin, size), :]
            for j in range(keep_ref.shape[1] // LANE):
                lanes = pl.ds(j * LANE, LANE)
                centred = product_ref[pl.ds(begin, size), lanes] - total * mean[q][:, j * LANE : (j + 1) * LANE]
                out_ref[pl.ds(place + q * size, size), lanes] = centred.astype(bf16)


def means(product_ref, total_ref, width):
    base = product_ref.shape[0] - 16 * CYCLES
    count = [total_ref[pl.ds(base + 16 * q, 1), :][:, :1] for q in range(CYCLES)]
    mean = [product_ref[pl.ds(base + 16 * q, 1), pl.ds(0, width)] / jnp.maximum(count[q], 1.0) for q in range(CYCLES)]
    return mean, count


def split(x, pieces):
    out = []
    for _ in range(pieces):
        out.append(x.astype(bf16).astype(f32))
        x = x - out[-1]
    return out


def stat_rows(mean, count=None):
    width = mean[0].shape[1]
    rows = [piece for m in zip(*[split(m, 3) for m in mean]) for piece in m]
    zero = jnp.zeros((1, width), f32)
    if count is None:
        rows += [zero] * 2
    else:
        lane = lax.broadcasted_iota(jnp.int32, (1, width), 1) // (LANE // 2)
        for part in zip(*[split(c, 2) for c in count]):
            rows.append(sum(jnp.where(lane == q, p, 0.0) for q, p in enumerate(part)))
    return jnp.concatenate(rows + [zero] * (STAT_ROWS - len(rows)), axis=0).astype(bf16)


def gram_own_kernel(label_ref, valid_ref, mid_ref, edge_ref, *refs, groups):
    near_refs, (out_ref, left_ref, total_ref, acc_ref) = refs[:-4], refs[-4:]
    px = mid_ref.shape[1]
    rim = edge_ref.shape[0] // 2
    rows = mid_ref.shape[0] + 2 * rim
    width = 2 * rows
    label = label_ref[...][None, :]
    used = valid_ref[...][None, :] == 1
    for q in range(CYCLES):
        weight = jnp.broadcast_to(((label == q) & used).astype(f32), (16, px)).astype(bf16)
        left_ref[pl.ds(q * rows, rim), :] = edge_ref[pl.ds(0, rim), :] * weight[:1]
        left_ref[pl.ds(q * rows + rim, rows - 2 * rim), :] = mid_ref[...] * weight[:1]
        left_ref[pl.ds((q + 1) * rows - rim, rim), :] = edge_ref[pl.ds(rim, rim), :] * weight[:1]
        left_ref[pl.ds(CYCLES * rows + 16 * q, 16), :] = weight
    right = jnp.concatenate([ref[...] for ref in (mid_ref, edge_ref, *near_refs)] + [jnp.ones((LANE, px), bf16)], axis=0)
    acc_ref[...] = lax.dot_general(left_ref[...], right, NT, preferred_element_type=f32)
    total_ref[...] = acc_ref[:, pl.ds(width, LANE)]
    mean, count = means(acc_ref, total_ref, width)
    size = rows // groups
    stats = stat_rows(mean, count)
    for group in range(groups):
        for q in range(CYCLES):
            here = pl.ds(q * rows + group * size, size)
            for j in range(width // LANE):
                lanes = pl.ds(j * LANE, LANE)
                centred = acc_ref[here, lanes] - total_ref[here, :] * mean[q][:, j * LANE : (j + 1) * LANE]
                out_ref[group, pl.ds(q * size, size), lanes] = centred.astype(bf16)
        out_ref[group, pl.ds(CYCLES * size, STAT_ROWS), :] = stats


def part_outs(rows, width, stat_rows):
    return [((rows, width), bf16), ((rows + stat_rows, width), bf16), ((stat_rows, width), bf16)]


def gram_own(label, valid, mid, edge, near, groups):
    px = mid.shape[1]
    rows = mid.shape[0] + edge.shape[0]
    tall = CYCLES * (rows + 16)
    return kernel_call(
        functools.partial(gram_own_kernel, groups=groups),
        "gram_own",
        (label, valid, mid, edge, *near),
        [((groups, CYCLES * rows // groups + STAT_ROWS, 2 * rows), bf16), ((tall, px), bf16), ((tall, LANE), f32)],
        [pltpu.VMEM((tall, 2 * rows + LANE), f32)],
        mib=10,
    )


def gram_cross_kernel(left_ref, total_ref, *refs, groups):
    col_refs, (keep_ref, send_ref, stat_ref, acc_ref) = refs[:-4], refs[-4:]
    right = jnp.concatenate([ref[...] for ref in col_refs], axis=0)
    acc_ref[...] = lax.dot_general(left_ref[...], right, NT, preferred_element_type=f32)
    mean, _ = means(acc_ref, total_ref, acc_ref.shape[1])
    stats = stat_rows(mean)
    stat_ref[...] = stats
    send_ref[pl.ds(send_ref.shape[0] - STAT_ROWS, STAT_ROWS), :] = stats
    centre(acc_ref, total_ref, mean, keep_ref, send_ref, groups)


def gram_cross(left, total, cols, groups):
    tall, width = left.shape[0], sum(c.shape[0] for c in cols)
    return kernel_call(
        functools.partial(gram_cross_kernel, groups=groups),
        "gram_cross",
        (left, total, *cols),
        part_outs(tall // 2 - 16, width, STAT_ROWS),
        [pltpu.VMEM((tall, width), f32)],
        mib=8,
    )


def join_stats(mine_ref, got_ref, groups):
    mine = mine_ref[...].astype(f32)
    got = got_ref[pl.ds(got_ref.shape[0] - mine.shape[0], mine.shape[0]), :].astype(f32)
    return jnp.concatenate([mine[: groups * STAT], got[: groups * STAT]], axis=0)


def merge_kernel(keep_ref, got_ref, stat_ref, next_keep_ref, next_send_ref, next_stat_ref, *, groups):
    half = next_keep_ref.shape[0]
    total = keep_ref[...].astype(f32) + got_ref[pl.ds(0, 2 * half), :].astype(f32)
    next_keep_ref[...] = total[:half].astype(bf16)
    next_send_ref[pl.ds(0, half), :] = total[half:].astype(bf16)
    stats = join_stats(stat_ref, got_ref, groups).astype(bf16)
    next_stat_ref[...] = stats
    next_send_ref[pl.ds(half, stats.shape[0]), :] = stats


def merge(keep, got, stat, groups):
    outs = part_outs(keep.shape[0] // 2, keep.shape[1], 2 * groups * STAT)
    return kernel_call(functools.partial(merge_kernel, groups=groups), "merge", (keep, got, stat), outs)


def whole_means(stats):
    n = stats.shape[0]
    return stats + pltpu.roll(stats, n - CYCLES, 0) + pltpu.roll(stats, n - 2 * CYCLES, 0)


def own_part_kernel(got_ref, out_ref, side_ref, share_ref, *, edge):
    groups, _, width = got_ref.shape
    size = out_ref.shape[0] // CYCLES
    rows = width // 2
    mid = rows - 2 * edge
    me = lax.axis_index("pixel")
    stats = [got_ref[me ^ i, pl.ds(CYCLES * size, STAT_ROWS), :].astype(f32)[:STAT] for i in range(groups)]
    stats = jnp.concatenate(stats, axis=0)
    entries = stats.shape[0]
    kind = lax.broadcasted_iota(jnp.int32, (entries, 1), 0) % STAT
    n = me * size + lax.broadcasted_iota(jnp.int32, (size, rows), 0)
    packed = jnp.where(n < edge, n + mid, jnp.where(n < edge + mid, n - edge, n))
    pick = (packed == lax.broadcasted_iota(jnp.int32, (size, rows), 1)).astype(f32)
    counted = stats + pltpu.roll(stats, entries - 1, 0)
    mean = whole_means(stats)
    for q in range(CYCLES):
        number = pltpu.roll(counted, entries - 3 * CYCLES + q, 0)[:, q * LANE // 2 : q * LANE // 2 + 1]
        number = jnp.where(kind == q, number, 0.0)
        count = jnp.sum(number, axis=0, keepdims=True)
        share = number / count
        share_ref[pl.ds(q * entries, entries), :] = jnp.broadcast_to(share, (entries, LANE))
        share_ref[pl.ds(CYCLES * entries + 8 * q, 8), :] = jnp.broadcast_to(1.0 / count, (8, LANE))
        apart = mean[:, :rows] - jnp.sum(mean[:, :rows] * share, axis=0, keepdims=True)
        side = lax.dot_general(pick, apart * share, NT, precision=EXACT, preferred_element_type=f32)
        here = pl.ds(q * size, size)
        side_ref[here, :] = side
        within = got_ref[0, here, :].astype(f32)
        for group in range(1, groups):
            within += got_ref[group, here, :].astype(f32)
        out_ref[here, :] = within * (1.0 / count) + part_between(mean, side, share)


def part_between(mean, side, share):
    apart = mean - jnp.sum(mean * share, axis=0, keepdims=True)
    return lax.dot_general(side, apart, NN, precision=EXACT, preferred_element_type=f32)


def part_sum(keep_ref, got_ref, mean, side, share, inverse, q):
    size = keep_ref.shape[0] // CYCLES
    rows = pl.ds(q * size, size)
    within = keep_ref[rows, :].astype(f32) + got_ref[rows, :].astype(f32)
    return within * inverse + part_between(mean, side, share)


def part_sums(keep_ref, got_ref, stat_ref, side_ref, share_ref, groups):
    stats = join_stats(stat_ref, got_ref, groups // 2)
    entries = stats.shape[0]
    mean = whole_means(stats)
    size = keep_ref.shape[0] // CYCLES
    return [
        part_sum(
            keep_ref,
            got_ref,
            mean,
            side_ref[pl.ds(q * size, size), :],
            share_ref[pl.ds(q * entries, entries), :][:, :1],
            share_ref[pl.ds(CYCLES * entries + 8 * q, 1), :][:, :1],
            q,
        )
        for q in range(CYCLES)
    ]


def own_part(got, edge):
    groups, tall, width = got.shape
    size = (tall - STAT_ROWS) // CYCLES
    entries = groups * STAT
    outs = [((CYCLES * size, width), f32), ((CYCLES * size, entries), f32), ((CYCLES * (entries + 8), LANE), f32)]
    return kernel_call(functools.partial(own_part_kernel, edge=edge), "own_part", (got,), outs)


def finish_kernel(own_ref, side_ref, share_ref, *refs, parts, rows, edge, groups):
    refs, out_ref = refs[:-1], refs[-1]
    size = out_ref.shape[0]
    mid = rows - 2 * edge
    me = lax.axis_index("frame")
    sums = [[ref[pl.ds(q * size, size), :] for q in range(CYCLES)] for ref in (own_ref,)]
    sums += [part_sums(*refs[i : i + 3], side_ref, share_ref, groups) for i in range(0, len(refs), 3)]
    for q in range(CYCLES):
        for j, ((mid_part, mid_at), (edge_part, edge_at)) in enumerate(parts):
            mids = sums[mid_part][q][:, mid_at : mid_at + mid]
            edges = sums[edge_part][q][:, edge_at : edge_at + 2 * edge]
            natural = jnp.concatenate([edges[:, :edge], mids, edges[:, edge:]], axis=1)
            out_ref[:, q, pl.ds(pl.multiple_of((me ^ j) * rows, rows), rows)] = natural


def swap(x, axis, bit):
    return lax.ppermute(x, axis, [(i, i ^ bit) for i in range(lax.axis_size(axis))])


def swap_pieces(x, n):
    size = x.shape[0] // n
    return [swap(x[i * size : (i + 1) * size], "frame", 1) for i in range(n)]


def shards(frames, dead_time, band_width, cycle_label, valid):
    nblocks = lax.axis_size("frame")
    ngroups = lax.axis_size("pixel")
    rows = frames.shape[0]
    nframes = rows * nblocks
    own_rows = rows // ngroups
    edge_rows = max(rows // EDGE_PART, 32)
    mid_rows = rows - 2 * edge_rows
    chip = lax.axis_index("frame") // 2
    even = lax.axis_index("frame") % 2 == 0

    near_halo, far_halo = halos(frames)
    mid, rim, dead, width = smooth_middle(frames, dead_time, band_width, edge_rows)
    halo = far_halo
    for bit in sorted({x ^ (x + 1) for x in range(nblocks // 2 - 1)}):
        got = swap(far_halo, "frame", 2 * bit)
        wanted = (chip ^ bit) == jnp.where(even, chip + 1, chip - 1)
        halo = got if bit == 1 else jnp.where(wanted, got, halo)
    mid = hold(mid, halo)
    far_mid = {j: swap(mid, "frame", j) for j in range(2, nblocks, 2)}
    near_halo = swap(near_halo, "frame", 1)
    halo = swap(halo, "frame", 1)
    near = swap_pieces(mid, 4)
    edge = smooth_edges(rim, near_halo, halo, dead, width, nframes)
    far_edge = {j: swap(edge, "frame", j) for j in range(2, nblocks, 2)}
    near += swap_pieces(edge, 4)

    def exchange(send, level):
        return swap(send, "pixel", 2**level)

    levels = ngroups.bit_length() - 1
    own, left, total = gram_own(cycle_label, valid, mid, edge, near, ngroups)
    wait = [total]
    own, side, share = own_part(lax.all_to_all(own, "pixel", 0, 0, tiled=True), edge_rows)

    others, places = [], []
    later = []
    for j in range(2, nblocks, 2):
        for source, n in ((far_mid[j], 4), (far_edge[j], 1)):
            source = hold(source, *wait)
            keep, send, stat = gram_cross(left, total, [source, *swap_pieces(source, n)], ngroups)
            wait = [stat]
            for level in range(levels):
                got = exchange(send, level)
                if level + 1 < levels:
                    keep, send, stat = merge(keep, got, stat, 2**level)
            later = [own, send]
            places.append((1 + len(others) // 3, source.shape[0]))
            others += [keep, got, stat]
    parts = [((0, 0), (0, mid_rows)), ((0, rows), (0, rows + mid_rows))]
    for pair in zip(places[::2], places[1::2]):
        parts += [tuple((p, i * n) for p, n in pair) for i in range(2)]
    return kernel_call(
        functools.partial(finish_kernel, parts=parts, rows=rows, edge=edge_rows, groups=ngroups),
        "finish",
        (own, side, share, *others),
        [((own_rows, CYCLES, nframes), f32)],
    )[0]


def solution(mesh):
    in_specs = (P("frame", "pixel"), P("pixel"), P("pixel"), P("pixel"), P("pixel"))
    out_specs = P(("frame", "pixel"), None, None)
    return jax.shard_map(shards, mesh=mesh, in_specs=in_specs, out_specs=out_specs, check_vma=False)
```

time: 274 us -> 55.8 us (0.20)
  waiting for transfers between devices: 151 us -> 10.5 us
  blocking collectives: 47 us -> 0 us
  other arithmetic: 23.3 us -> 0 us
  starting transfers between devices: 4.21 us -> 26.9 us
  local copies, waits for them, and re-layouts: 26.9 us -> 4.69 us
  between operations: 13.6 us -> 0.17 us
  Pallas kernels: 0 us -> 13.1 us
  matrix products: 7.56 us -> 0 us
    reduce_scatter x1 -> x0, waiting for transfers between devices: 139 us -> none  [shards(): lax.psum_scatter(product.reshape(lax.axis_size(('frame', 'pixel')) * own_...]
    psum x1 -> x0, blocking collectives: 47 us -> none  [shards(): cycle_sum, counts = lax.psum((cycle_sum, counts), ('frame', 'pixel'))]
    ppermute x0 -> x24, starting transfers between devices: none -> 21.1 us  [swap(): lax.ppermute(x, axis, [(i, i ^ bit) for i in range(lax.axis_size(axis))])]
    convert_element_type x6 -> x0, other arithmetic: 15.8 us -> none  [the longest x1 15.8 us: band_smooth(): return (total / divisor).astype(jnp.bfloat16)]
    pallas_call x0 -> x15, Pallas kernels: none -> 13.1 us  [the longest x12 13.1 us: kernel_call(): pl.pallas_call(body, in_specs=in_specs or [vmem] * len(args), out_specs=[...]
    all_to_all x1, waiting for transfers between devices: 12 us -> 0.01 us  [shards(): lax.all_to_all(own, 'pixel', 0, 0, tiled=True)]
    reshape x2 -> x0, local copies, waits for them, and re-layouts: 11.1 us -> none  [the longest x1 9.91 us: shards(): product.reshape(lax.axis_size(('frame', 'pixel')) * own_rows, CYCLES * nf...]
    ppermute x0 -> x24, waiting for transfers between devices: none -> 10.5 us  [swap(): lax.ppermute(x, axis, [(i, i ^ bit) for i in range(lax.axis_size(axis))])]
  transfers between devices with their start and end apart: 2 -> 25, of which waited for: 2 -> 10; matrix products, arithmetic and copies ran while one was open for 1% -> 2% of each run, Pallas kernels for 0% -> 21%
where the time goes in v2:
time: 55.8 us; the launch traced here: 55.3 us
  starting transfers between devices  26.9 us (48%)
  Pallas kernels  13.1 us (23%)
  waiting for transfers between devices  10.5 us (19%)
  local copies, waits for them, and re-layouts  4.69 us (8%)
    ppermute x24, starting transfers between devices, swap(): lax.ppermute(x, axis, [(i, i ^ bit) for i in range(lax.axis_size(axis))])  21.1 us
    pallas_call x12, Pallas kernels, kernel_call(): pl.pallas_call(body, in_specs=in_specs or [vmem] * len(args), out_specs=[...  13.1 us
    ppermute x24, waiting for transfers between devices, swap(): lax.ppermute(x, axis, [(i, i ^ bit) for i in range(lax.axis_size(axis))])  10.5 us
    all_to_all x1, starting transfers between devices, shards(): lax.all_to_all(own, 'pixel', 0, 0, tiled=True)  5.83 us
    unnamed x12, local copies, waits for them, and re-layouts  3.47 us
    slice x3, local copies, waits for them, and re-layouts, swap_pieces(): return [swap(x[i * size:(i + 1) * size], 'frame', 1) for i in range(n)]  1.21 us
  transfers between devices with their start and end apart: 25, of which 10 were waited for; matrix products, arithmetic and copies ran while one was open for 2% of the time, Pallas kernels for 21%

profile of v2, /device:TPU:0, one launch (start us, length us, event | category | flops | bytes accessed | tf_op | source)
XLA Modules:
  0.0 55.3 jit_solution(16801902884548893533)
XLA Ops:
  0.0 1.2 %copy-done = bf16[256,2048]{1,0:T(8,128)(2,1)S(1)} copy-done((bf16[256,2048]{1,0:T(8,128)(2,1)S(1)}, bf16[256,2048]{1,0:T(8,128)(2,1)}, u32[]{:S(2)}) %copy-start) | copy-done | bytes 1048600
  1.4 3.0 %collective-permute-start = (bf16[16,2048]{1,0:T(8,128)(2,1)S(1)}, bf16[16,2048]{1,0:T(8,128)(2,1)S(1)}, u32[]{:S(2)}, u32[]{:S(2)}) collective-permute-start(bf16[16,2048]{1,0:T(8,128)(2,1)S(1)} %get-tuple-element.36), channel_id=1, source_target_pairs={{0,16},{8,24},{16,0},{24,8},{1,17},{9,25},{17,1},{25,9},{2,18},{10... | collective-permute-start | bytes 196616 | tf_op jit(solution)/shard_map/ppermute | solution.py:411
  4.4 0.7 %copy-done.2 = f32[2048]{0:T(1024)S(1)} copy-done((f32[2048]{0:T(1024)S(1)}, f32[2048]{0:T(1024)}, u32[]{:S(2)}) %copy-start.2) | copy-done | bytes 8216
  5.1 0.7 %copy-done.3 = s32[2048]{0:T(1024)S(1)} copy-done((s32[2048]{0:T(1024)S(1)}, s32[2048]{0:T(1024)}, u32[]{:S(2)}) %copy-start.3) | copy-done | bytes 8216
  5.8 1.5 %smooth_middle.1 = (bf16[128,2048]{1,0:T(8,128)(2,1)S(1)}, bf16[160,2048]{1,0:T(8,128)(2,1)S(1)}, f32[2048]{0:T(1024)S(1)}, s32[2048]{0:T(1024)S(1)}) custom-call(bf16[256,2048]{1,0:T(8,128)(2,1)S(1)} %copy-done, f32[2048]{0:T(1024)S(1)} %copy-done.2, s32[2048]{0:T(1024)S(1)} %copy-done.3), custom_call_target="tpu_custom_call" | custom-call | bytes 262144 | tf_op jit(solution)/shard_map/smooth_middle/pallas_call | solution.py:25
  7.3 0.6 %collective-permute-start.2 = (bf16[16,2048]{1,0:T(8,128)(2,1)S(1)}, bf16[16,2048]{1,0:T(8,128)(2,1)S(1)}, u32[]{:S(2)}, u32[]{:S(2)}) collective-permute-start(bf16[16,2048]{1,0:T(8,128)(2,1)S(1)} %collective-permute-done.refs_1_), channel_id=1, source_target_pairs={{0,8},{8,0},{16,24},{24,16},{1,9},{9,1},{17,25},{25,17},{2,10},{10... | collective-permute-start | bytes 196616 | tf_op jit(solution)/shard_map/ppermute | solution.py:411
  7.9 0.9 %collective-permute-start.11 = (bf16[128,2048]{1,0:T(8,128)(2,1)S(1)}, bf16[128,2048]{1,0:T(8,128)(2,1)S(1)}, u32[]{:S(2)}, u32[]{:S(2)}) collective-permute-start(bf16[128,2048]{1,0:T(8,128)(2,1)S(1)} %hold.3.mid_ref), channel_id=1, source_target_pairs={{0,16},{8,24},{16,0},{24,8},{1,17},{9,25},{17,1},{25,9},{2,18},{10... | collective-permute-start | bytes 1572872 | tf_op jit(solution)/shard_map/ppermute | solution.py:411
  9.8 2.4 %smooth_edges.1.edge_ref = bf16[128,2048]{1,0:T(8,128)(2,1)} custom-call(bf16[160,2048]{1,0:T(8,128)(2,1)S(1)} %get-tuple-element.37.rim_ref, bf16[16,2048]{1,0:T(8,128)(2,1)S(1)} %collective-permute-done.1.near_ref, bf16[16,2048]{1,0:T(8,128)(2,1)S(1)} %collective-permute-done.2.far_ref, f32[2048]{0:T(1024)S(1)} %get-tuple-element.39.dead_ref, ...), custom_call_target="tpu_custom_call" | custom-call | bytes 262144 | tf_op jit(solution)/shard_map/smooth_edges/pallas_call | solution.py:25
  12.3 1.1 %fusion.1 = (bf16[32,2048]{1,0:T(8,128)(2,1)S(1)}, bf16[32,2048]{1,0:T(8,128)(2,1)S(1)}, bf16[32,2048]{1,0:T(8,128)(2,1)S(1)}, bf16[32,2048]{1,0:T(8,128)(2,1)S(1)}) fusion(bf16[128,2048]{1,0:T(8,128)(2,1)} %smooth_edges.1.edge_ref), kind=kLoop, calls=%fused_computation.1 | loop fusion | bytes 1048576 | tf_op jit(solution)/shard_map/slice | solution.py:416
  14.8 1.2 %collective-permute-start.19 = (bf16[128,2048]{1,0:T(8,128)(2,1)}, bf16[128,2048]{1,0:T(8,128)(2,1)}, u32[]{:S(2)}, u32[]{:S(2)}) collective-permute-start(bf16[128,2048]{1,0:T(8,128)(2,1)} %smooth_edges.1.edge_ref), channel_id=1, source_target_pairs={{0,16},{8,24},{16,0},{24,8},{1,17},{9,25},{17,1},{25,9},{2,18},{10... | collective-permute-start | bytes 1572872 | tf_op jit(solution)/shard_map/ppermute | solution.py:411
  16.1 3.3 %gram_own.1 = (bf16[8,80,512]{2,1,0:T(8,128)(2,1)S(1)}, bf16[544,2048]{1,0:T(8,128)(2,1)S(1)}, f32[544,128]{1,0:T(8,128)S(1)}) custom-call(s32[2048]{0:T(1024)S(1)} %copy-done.4, s32[2048]{0:T(1024)S(1)} %copy-done.5, bf16[128,2048]{1,0:T(8,128)(2,1)S(1)} %hold.3.mid_ref, bf16[128,2048]{1,0:T(8,128)(2,1)} %smooth_edges.1.edge_ref, ...), custom_call_target="tpu_custom_call" | custom-call | bytes 262144 | tf_op jit(solution)/shard_map/gram_own/pallas_call | solution.py:25
  19.4 0.8 %copy-done.1 = bf16[8,80,512]{2,1,0:T(8,128)(2,1)} copy-done((bf16[8,80,512]{2,1,0:T(8,128)(2,1)}, bf16[8,80,512]{2,1,0:T(8,128)(2,1)S(1)}, u32[]{:S(2)}) %copy-start.1) | copy-done | bytes 655384
  20.2 5.8 %all-to-all-start = ((bf16[8,80,512]{2,1,0:T(8,128)(2,1)}), bf16[8,80,512]{2,1,0:T(8,128)(2,1)}, u32[]{:S(2)}, u32[]{:S(2)}) async-start(bf16[8,80,512]{2,1,0:T(8,128)(2,1)} %copy-done.1), calls=%async_computation | async-start | bytes 1310720 | tf_op jit(solution)/shard_map/all_to_all | solution.py:452
  26.2 0.5 collective-permute-start.13
  26.8 0.4 collective-permute-start.15
  27.2 0.3 collective-permute-done.12.refs_1_
  27.7 0.3 collective-permute-done.14.refs_3_
  28.2 0.8 %gram_cross.2 = (bf16[256,256]{1,0:T(8,128)(2,1)S(1)}, bf16[272,256]{1,0:T(8,128)(2,1)S(1)}, bf16[16,256]{1,0:T(8,128)(2,1)S(1)}) custom-call(bf16[544,2048]{1,0:T(8,128)(2,1)S(1)} %get-tuple-element.45.left_ref, f32[544,128]{1,0:T(8,128)S(1)} %get-tuple-element.46.refs_1_.total_ref, bf16[128,2048]{1,0:T(8,128)(2,1)S(1)} %hold.4.refs_0_, ...), custom_call_target="tpu_custom_call" | custom-call | bytes 262144 | tf_op jit(solution)/shard_map/gram_cross/pallas_call | solution.py:25
  29.1 4.1 %collective-permute-done.19.refs_0_ = bf16[128,2048]{1,0:T(8,128)(2,1)} collective-permute-done((bf16[128,2048]{1,0:T(8,128)(2,1)}, bf16[128,2048]{1,0:T(8,128)(2,1)}, u32[]{:S(2)}, u32[]{:S(2)}) %collective-permute-start.19) | collective-permute-done | bytes 524320 | tf_op jit(solution)/shard_map/ppermute | solution.py:411
  33.2 1.5 %collective-permute-start.16 = (bf16[272,256]{1,0:T(8,128)(2,1)S(1)}, bf16[272,256]{1,0:T(8,128)(2,1)S(1)}, u32[]{:S(2)}, u32[]{:S(2)}) collective-permute-start(bf16[272,256]{1,0:T(8,128)(2,1)S(1)} %get-tuple-element.48), channel_id=1, source_target_pairs={{0,1},{1,0},{2,3},{3,2},{4,5},{5,4},{6,7},{7,6},{8,9},{9,8},{10,11... | collective-permute-start | bytes 417800 | tf_op jit(solution)/shard_map/ppermute | solution.py:411
  34.8 0.6 %collective-permute-done.20.refs_1_ = bf16[128,2048]{1,0:T(8,128)(2,1)S(1)} collective-permute-done((bf16[128,2048]{1,0:T(8,128)(2,1)}, bf16[128,2048]{1,0:T(8,128)(2,1)S(1)}, u32[]{:S(2)}, u32[]{:S(2)}) %collective-permute-start.20) | collective-permute-done | bytes 524320 | tf_op jit(solution)/shard_map/ppermute | solution.py:411
  35.3 1.9 %gram_cross.3 = (bf16[256,256]{1,0:T(8,128)(2,1)S(1)}, bf16[272,256]{1,0:T(8,128)(2,1)S(1)}, bf16[16,256]{1,0:T(8,128)(2,1)S(1)}) custom-call(bf16[544,2048]{1,0:T(8,128)(2,1)S(1)} %get-tuple-element.45.left_ref, f32[544,128]{1,0:T(8,128)S(1)} %get-tuple-element.46.refs_1_.total_ref, bf16[128,2048]{1,0:T(8,128)(2,1)} %hold.5.refs_0_, ...), custom_call_target="tpu_custom_call" | custom-call | bytes 262144 | tf_op jit(solution)/shard_map/gram_cross/pallas_call | solution.py:25
  37.2 1.6 %collective-permute-start.21 = (bf16[272,256]{1,0:T(8,128)(2,1)S(1)}, bf16[272,256]{1,0:T(8,128)(2,1)S(1)}, u32[]{:S(2)}, u32[]{:S(2)}) collective-permute-start(bf16[272,256]{1,0:T(8,128)(2,1)S(1)} %get-tuple-element.57), channel_id=1, source_target_pairs={{0,1},{1,0},{2,3},{3,2},{4,5},{5,4},{6,7},{7,6},{8,9},{9,8},{10,11... | collective-permute-start | bytes 417800 | tf_op jit(solution)/shard_map/ppermute | solution.py:411
  38.8 2.5 %collective-permute-done.16.got_ref = bf16[272,256]{1,0:T(8,128)(2,1)S(1)} collective-permute-done((bf16[272,256]{1,0:T(8,128)(2,1)S(1)}, bf16[272,256]{1,0:T(8,128)(2,1)S(1)}, u32[]{:S(2)}, u32[]{:S(2)}) %collective-permute-start.16) | collective-permute-done | bytes 139296 | tf_op jit(solution)/shard_map/ppermute | solution.py:411
  41.4 1.2 %collective-permute-start.17 = (bf16[144,256]{1,0:T(8,128)(2,1)S(1)}, bf16[144,256]{1,0:T(8,128)(2,1)S(1)}, u32[]{:S(2)}, u32[]{:S(2)}) collective-permute-start(bf16[144,256]{1,0:T(8,128)(2,1)S(1)} %get-tuple-element.51), channel_id=1, source_target_pairs={{0,2},{1,3},{2,0},{3,1},{4,6},{5,7},{6,4},{7,5},{8,10},{9,11},{10,... | collective-permute-start | bytes 221192 | tf_op jit(solution)/shard_map/ppermute | solution.py:411
  42.5 1.5 %collective-permute-done.21.got_ref = bf16[272,256]{1,0:T(8,128)(2,1)S(1)} collective-permute-done((bf16[272,256]{1,0:T(8,128)(2,1)S(1)}, bf16[272,256]{1,0:T(8,128)(2,1)S(1)}, u32[]{:S(2)}, u32[]{:S(2)}) %collective-permute-start.21) | collective-permute-done | bytes 139296 | tf_op jit(solution)/shard_map/ppermute | solution.py:411
  44.1 1.9 %collective-permute-start.22 = (bf16[144,256]{1,0:T(8,128)(2,1)S(1)}, bf16[144,256]{1,0:T(8,128)(2,1)S(1)}, u32[]{:S(2)}, u32[]{:S(2)}) collective-permute-start(bf16[144,256]{1,0:T(8,128)(2,1)S(1)} %get-tuple-element.60), channel_id=1, source_target_pairs={{0,2},{1,3},{2,0},{3,1},{4,6},{5,7},{6,4},{7,5},{8,10},{9,11},{10,... | collective-permute-start | bytes 221192 | tf_op jit(solution)/shard_map/ppermute | solution.py:411
  46.0 3.1 %collective-permute-start.18 = (bf16[96,256]{1,0:T(8,128)(2,1)S(1)}, bf16[96,256]{1,0:T(8,128)(2,1)S(1)}, u32[]{:S(2)}, u32[]{:S(2)}) collective-permute-start(bf16[96,256]{1,0:T(8,128)(2,1)S(1)} %get-tuple-element.54), channel_id=1, source_target_pairs={{0,4},{1,5},{2,6},{3,7},{4,0},{5,1},{6,2},{7,3},{8,12},{9,13},{10,... | collective-permute-start | bytes 147464 | tf_op jit(solution)/shard_map/ppermute | solution.py:411
  49.1 3.0 %collective-permute-start.23 = (bf16[96,256]{1,0:T(8,128)(2,1)S(1)}, bf16[96,256]{1,0:T(8,128)(2,1)S(1)}, u32[]{:S(2)}, u32[]{:S(2)}) collective-permute-start(bf16[96,256]{1,0:T(8,128)(2,1)S(1)} %get-tuple-element.63), channel_id=1, source_target_pairs={{0,4},{1,5},{2,6},{3,7},{4,0},{5,1},{6,2},{7,3},{8,12},{9,13},{10,... | collective-permute-start | bytes 147464 | tf_op jit(solution)/shard_map/ppermute | solution.py:411
  52.1 1.7 %own_part.1 = (f32[64,512]{1,0:T(8,128)S(1)}, f32[64,64]{1,0:T(8,128)S(1)}, f32[144,128]{1,0:T(8,128)S(1)}) custom-call(bf16[8,80,512]{2,1,0:T(8,128)(2,1)} %all-to-all-done.got_ref), custom_call_target="tpu_custom_call" | custom-call | bytes 262144 | tf_op jit(solution)/shard_map/own_part/pallas_call | solution.py:25
  53.8 0.3 collective-permute-done.23.refs_4_
  54.2 1.1 %finish.1 = f32[32,2,1024]{2,1,0:T(2,128)} custom-call(f32[64,512]{1,0:T(8,128)S(1)} %get-tuple-element.42.own_ref, f32[64,64]{1,0:T(8,128)S(1)} %get-tuple-element.43.side_ref, f32[144,128]{1,0:T(8,128)S(1)} %get-tuple-element.44.share_ref, bf16[64,256]{1,0:T(8,128)(2,1)S(1)} %get-tuple-element.53.refs_0_, ...), custom_call_target="tpu_custom_call" | custom-call | bytes 262144 | tf_op jit(solution)/shard_map/finish/pallas_call | solution.py:25
  (48 shorter events, 3.4 us)
Async XLA Ops:
  0.0 1.2 %copy-start = (bf16[256,2048]{1,0:T(8,128)(2,1)S(1)}, bf16[256,2048]{1,0:T(8,128)(2,1)}, u32[]{:S(2)}) copy-start(bf16[256,2048]{1,0:T(8,128)(2,1)} %frames_ref.3) | copy-start | bytes 3145732
  1.4 5.9 %collective-permute-start = (bf16[16,2048]{1,0:T(8,128)(2,1)S(1)}, bf16[16,2048]{1,0:T(8,128)(2,1)S(1)}, u32[]{:S(2)}, u32[]{:S(2)}) collective-permute-start(bf16[16,2048]{1,0:T(8,128)(2,1)S(1)} %get-tuple-element.36), channel_id=1, source_target_pairs={{0,16},{8,24},{16,0},{24,8},{1,17},{9,25},{17,1},{25,9},{2,18},{10... | collective-permute-start | bytes 196616 | tf_op jit(solution)/shard_map/ppermute | solution.py:411
  4.4 4.9 %collective-permute-start.1 = (bf16[16,2048]{1,0:T(8,128)(2,1)S(1)}, bf16[16,2048]{1,0:T(8,128)(2,1)S(1)}, u32[]{:S(2)}, u32[]{:S(2)}) collective-permute-start(bf16[16,2048]{1,0:T(8,128)(2,1)S(1)} %get-tuple-element.38), channel_id=1, source_target_pairs={{0,8},{8,0},{16,24},{24,16},{1,9},{9,1},{17,25},{25,17},{2,10},{10... | collective-permute-start | bytes 196616 | tf_op jit(solution)/shard_map/ppermute | solution.py:411
  4.4 0.7 %copy-start.2 = (f32[2048]{0:T(1024)S(1)}, f32[2048]{0:T(1024)}, u32[]{:S(2)}) copy-start(f32[2048]{0:T(1024)} %dead_hbm.1) | copy-start | bytes 24580
  5.1 0.7 %copy-start.3 = (s32[2048]{0:T(1024)S(1)}, s32[2048]{0:T(1024)}, u32[]{:S(2)}) copy-start(s32[2048]{0:T(1024)} %width_hbm.1) | copy-start | bytes 24580
  7.3 2.2 %collective-permute-start.2 = (bf16[16,2048]{1,0:T(8,128)(2,1)S(1)}, bf16[16,2048]{1,0:T(8,128)(2,1)S(1)}, u32[]{:S(2)}, u32[]{:S(2)}) collective-permute-start(bf16[16,2048]{1,0:T(8,128)(2,1)S(1)} %collective-permute-done.refs_1_), channel_id=1, source_target_pairs={{0,8},{8,0},{16,24},{24,16},{1,9},{9,1},{17,25},{25,17},{2,10},{10... | collective-permute-start | bytes 196616 | tf_op jit(solution)/shard_map/ppermute | solution.py:411
  7.9 8.2 %copy-start.4 = (s32[2048]{0:T(1024)S(1)}, s32[2048]{0:T(1024)}, u32[]{:S(2)}) copy-start(s32[2048]{0:T(1024)} %label_ref.1) | copy-start | bytes 24580
  7.9 8.2 %copy-start.5 = (s32[2048]{0:T(1024)S(1)}, s32[2048]{0:T(1024)}, u32[]{:S(2)}) copy-start(s32[2048]{0:T(1024)} %valid_ref.1) | copy-start | bytes 24580
  7.9 18.1 %collective-permute-start.11 = (bf16[128,2048]{1,0:T(8,128)(2,1)S(1)}, bf16[128,2048]{1,0:T(8,128)(2,1)S(1)}, u32[]{:S(2)}, u32[]{:S(2)}) collective-permute-start(bf16[128,2048]{1,0:T(8,128)(2,1)S(1)} %hold.3.mid_ref), channel_id=1, source_target_pairs={{0,16},{8,24},{16,0},{24,8},{1,17},{9,25},{17,1},{25,9},{2,18},{10... | collective-permute-start | bytes 1572872 | tf_op jit(solution)/shard_map/ppermute | solution.py:411
  8.8 4.6 %collective-permute-start.3 = (bf16[32,2048]{1,0:T(8,128)(2,1)S(1)}, bf16[32,2048]{1,0:T(8,128)(2,1)S(1)}, u32[]{:S(2)}, u32[]{:S(2)}) collective-permute-start(bf16[32,2048]{1,0:T(8,128)(2,1)S(1)} %get-tuple-element.76), channel_id=1, source_target_pairs={{0,8},{8,0},{16,24},{24,16},{1,9},{9,1},{17,25},{25,17},{2,10},{10... | collective-permute-start | bytes 393224 | tf_op jit(solution)/shard_map/ppermute | solution.py:411
  9.0 4.7 %collective-permute-start.4 = (bf16[32,2048]{1,0:T(8,128)(2,1)S(1)}, bf16[32,2048]{1,0:T(8,128)(2,1)S(1)}, u32[]{:S(2)}, u32[]{:S(2)}) collective-permute-start(bf16[32,2048]{1,0:T(8,128)(2,1)S(1)} %get-tuple-element.75), channel_id=1, source_target_pairs={{0,8},{8,0},{16,24},{24,16},{1,9},{9,1},{17,25},{25,17},{2,10},{10... | collective-permute-start | bytes 393224 | tf_op jit(solution)/shard_map/ppermute | solution.py:411
  9.3 4.7 %collective-permute-start.5 = (bf16[32,2048]{1,0:T(8,128)(2,1)S(1)}, bf16[32,2048]{1,0:T(8,128)(2,1)S(1)}, u32[]{:S(2)}, u32[]{:S(2)}) collective-permute-start(bf16[32,2048]{1,0:T(8,128)(2,1)S(1)} %get-tuple-element.74), channel_id=1, source_target_pairs={{0,8},{8,0},{16,24},{24,16},{1,9},{9,1},{17,25},{25,17},{2,10},{10... | collective-permute-start | bytes 393224 | tf_op jit(solution)/shard_map/ppermute | solution.py:411
  9.6 4.7 %collective-permute-start.6 = (bf16[32,2048]{1,0:T(8,128)(2,1)S(1)}, bf16[32,2048]{1,0:T(8,128)(2,1)S(1)}, u32[]{:S(2)}, u32[]{:S(2)}) collective-permute-start(bf16[32,2048]{1,0:T(8,128)(2,1)S(1)} %get-tuple-element.73), channel_id=1, source_target_pairs={{0,8},{8,0},{16,24},{24,16},{1,9},{9,1},{17,25},{25,17},{2,10},{10... | collective-permute-start | bytes 393224 | tf_op jit(solution)/shard_map/ppermute | solution.py:411
  13.4 1.4 %collective-permute-start.10 = (bf16[32,2048]{1,0:T(8,128)(2,1)S(1)}, bf16[32,2048]{1,0:T(8,128)(2,1)S(1)}, u32[]{:S(2)}, u32[]{:S(2)}) collective-permute-start(bf16[32,2048]{1,0:T(8,128)(2,1)S(1)} %get-tuple-element.69), channel_id=1, source_target_pairs={{0,8},{8,0},{16,24},{24,16},{1,9},{9,1},{17,25},{25,17},{2,10},{10... | collective-permute-start | bytes 393224 | tf_op jit(solution)/shard_map/ppermute | solution.py:411
  13.7 2.4 %collective-permute-start.7 = (bf16[32,2048]{1,0:T(8,128)(2,1)S(1)}, bf16[32,2048]{1,0:T(8,128)(2,1)S(1)}, u32[]{:S(2)}, u32[]{:S(2)}) collective-permute-start(bf16[32,2048]{1,0:T(8,128)(2,1)S(1)} %get-tuple-element.72), channel_id=1, source_target_pairs={{0,8},{8,0},{16,24},{24,16},{1,9},{9,1},{17,25},{25,17},{2,10},{10... | collective-permute-start | bytes 393224 | tf_op jit(solution)/shard_map/ppermute | solution.py:411
  14.0 2.1 %collective-permute-start.8 = (bf16[32,2048]{1,0:T(8,128)(2,1)S(1)}, bf16[32,2048]{1,0:T(8,128)(2,1)S(1)}, u32[]{:S(2)}, u32[]{:S(2)}) collective-permute-start(bf16[32,2048]{1,0:T(8,128)(2,1)S(1)} %get-tuple-element.71), channel_id=1, source_target_pairs={{0,8},{8,0},{16,24},{24,16},{1,9},{9,1},{17,25},{25,17},{2,10},{10... | collective-permute-start | bytes 393224 | tf_op jit(solution)/shard_map/ppermute | solution.py:411
  14.2 1.8 %collective-permute-start.9 = (bf16[32,2048]{1,0:T(8,128)(2,1)S(1)}, bf16[32,2048]{1,0:T(8,128)(2,1)S(1)}, u32[]{:S(2)}, u32[]{:S(2)}) collective-permute-start(bf16[32,2048]{1,0:T(8,128)(2,1)S(1)} %get-tuple-element.70), channel_id=1, source_target_pairs={{0,8},{8,0},{16,24},{24,16},{1,9},{9,1},{17,25},{25,17},{2,10},{10... | collective-permute-start | bytes 393224 | tf_op jit(solution)/shard_map/ppermute | solution.py:411
  14.8 18.4 %collective-permute-start.19 = (bf16[128,2048]{1,0:T(8,128)(2,1)}, bf16[128,2048]{1,0:T(8,128)(2,1)}, u32[]{:S(2)}, u32[]{:S(2)}) collective-permute-start(bf16[128,2048]{1,0:T(8,128)(2,1)} %smooth_edges.1.edge_ref), channel_id=1, source_target_pairs={{0,16},{8,24},{16,0},{24,8},{1,17},{9,25},{17,1},{25,9},{2,18},{10... | collective-permute-start | bytes 1572872 | tf_op jit(solution)/shard_map/ppermute | solution.py:411
  19.4 0.9 %copy-start.1 = (bf16[8,80,512]{2,1,0:T(8,128)(2,1)}, bf16[8,80,512]{2,1,0:T(8,128)(2,1)S(1)}, u32[]{:S(2)}) copy-start(bf16[8,80,512]{2,1,0:T(8,128)(2,1)S(1)} %get-tuple-element.41) | copy-start | bytes 1966084
  20.2 31.9 %all-to-all-start = ((bf16[8,80,512]{2,1,0:T(8,128)(2,1)}), bf16[8,80,512]{2,1,0:T(8,128)(2,1)}, u32[]{:S(2)}, u32[]{:S(2)}) async-start(bf16[8,80,512]{2,1,0:T(8,128)(2,1)} %copy-done.1), calls=%async_computation | async-start | bytes 1310720 | tf_op jit(solution)/shard_map/all_to_all | solution.py:452
  26.1 1.4 %collective-permute-start.12 = (bf16[32,2048]{1,0:T(8,128)(2,1)S(1)}, bf16[32,2048]{1,0:T(8,128)(2,1)S(1)}, u32[]{:S(2)}, u32[]{:S(2)}) collective-permute-start(bf16[32,2048]{1,0:T(8,128)(2,1)S(1)} %get-tuple-element.68), channel_id=1, source_target_pairs={{0,8},{8,0},{16,24},{24,16},{1,9},{9,1},{17,25},{25,17},{2,10},{10... | collective-permute-start | bytes 393224 | tf_op jit(solution)/shard_map/ppermute | solution.py:411
  26.2 1.5 %collective-permute-start.13 = (bf16[32,2048]{1,0:T(8,128)(2,1)S(1)}, bf16[32,2048]{1,0:T(8,128)(2,1)S(1)}, u32[]{:S(2)}, u32[]{:S(2)}) collective-permute-start(bf16[32,2048]{1,0:T(8,128)(2,1)S(1)} %get-tuple-element.67), channel_id=1, source_target_pairs={{0,8},{8,0},{16,24},{24,16},{1,9},{9,1},{17,25},{25,17},{2,10},{10... | collective-permute-start | bytes 393224 | tf_op jit(solution)/shard_map/ppermute | solution.py:411
  26.7 1.3 %collective-permute-start.14 = (bf16[32,2048]{1,0:T(8,128)(2,1)S(1)}, bf16[32,2048]{1,0:T(8,128)(2,1)S(1)}, u32[]{:S(2)}, u32[]{:S(2)}) collective-permute-start(bf16[32,2048]{1,0:T(8,128)(2,1)S(1)} %get-tuple-element.66), channel_id=1, source_target_pairs={{0,8},{8,0},{16,24},{24,16},{1,9},{9,1},{17,25},{25,17},{2,10},{10... | collective-permute-start | bytes 393224 | tf_op jit(solution)/shard_map/ppermute | solution.py:411
  26.8 1.5 %collective-permute-start.15 = (bf16[32,2048]{1,0:T(8,128)(2,1)S(1)}, bf16[32,2048]{1,0:T(8,128)(2,1)S(1)}, u32[]{:S(2)}, u32[]{:S(2)}) collective-permute-start(bf16[32,2048]{1,0:T(8,128)(2,1)S(1)} %get-tuple-element.65), channel_id=1, source_target_pairs={{0,8},{8,0},{16,24},{24,16},{1,9},{9,1},{17,25},{25,17},{2,10},{10... | collective-permute-start | bytes 393224 | tf_op jit(solution)/shard_map/ppermute | solution.py:411
  33.2 2.1 %collective-permute-start.20 = (bf16[128,2048]{1,0:T(8,128)(2,1)}, bf16[128,2048]{1,0:T(8,128)(2,1)S(1)}, u32[]{:S(2)}, u32[]{:S(2)}) collective-permute-start(bf16[128,2048]{1,0:T(8,128)(2,1)} %hold.5.refs_0_), channel_id=1, source_target_pairs={{0,8},{8,0},{16,24},{24,16},{1,9},{9,1},{17,25},{25,17},{2,10},{10... | collective-permute-start | bytes 1572872 | tf_op jit(solution)/shard_map/ppermute | solution.py:411
  33.2 8.1 %collective-permute-start.16 = (bf16[272,256]{1,0:T(8,128)(2,1)S(1)}, bf16[272,256]{1,0:T(8,128)(2,1)S(1)}, u32[]{:S(2)}, u32[]{:S(2)}) collective-permute-start(bf16[272,256]{1,0:T(8,128)(2,1)S(1)} %get-tuple-element.48), channel_id=1, source_target_pairs={{0,1},{1,0},{2,3},{3,2},{4,5},{5,4},{6,7},{7,6},{8,9},{9,8},{10,11... | collective-permute-start | bytes 417800 | tf_op jit(solution)/shard_map/ppermute | solution.py:411
  37.2 6.8 %collective-permute-start.21 = (bf16[272,256]{1,0:T(8,128)(2,1)S(1)}, bf16[272,256]{1,0:T(8,128)(2,1)S(1)}, u32[]{:S(2)}, u32[]{:S(2)}) collective-permute-start(bf16[272,256]{1,0:T(8,128)(2,1)S(1)} %get-tuple-element.57), channel_id=1, source_target_pairs={{0,1},{1,0},{2,3},{3,2},{4,5},{5,4},{6,7},{7,6},{8,9},{9,8},{10,11... | collective-permute-start | bytes 417800 | tf_op jit(solution)/shard_map/ppermute | solution.py:411
  41.4 4.6 %collective-permute-start.17 = (bf16[144,256]{1,0:T(8,128)(2,1)S(1)}, bf16[144,256]{1,0:T(8,128)(2,1)S(1)}, u32[]{:S(2)}, u32[]{:S(2)}) collective-permute-start(bf16[144,256]{1,0:T(8,128)(2,1)S(1)} %get-tuple-element.51), channel_id=1, source_target_pairs={{0,2},{1,3},{2,0},{3,1},{4,6},{5,7},{6,4},{7,5},{8,10},{9,11},{10,... | collective-permute-start | bytes 221192 | tf_op jit(solution)/shard_map/ppermute | solution.py:411
  44.1 5.0 %collective-permute-start.22 = (bf16[144,256]{1,0:T(8,128)(2,1)S(1)}, bf16[144,256]{1,0:T(8,128)(2,1)S(1)}, u32[]{:S(2)}, u32[]{:S(2)}) collective-permute-start(bf16[144,256]{1,0:T(8,128)(2,1)S(1)} %get-tuple-element.60), channel_id=1, source_target_pairs={{0,2},{1,3},{2,0},{3,1},{4,6},{5,7},{6,4},{7,5},{8,10},{9,11},{10,... | collective-permute-start | bytes 221192 | tf_op jit(solution)/shard_map/ppermute | solution.py:411
  46.0 7.8 %collective-permute-start.18 = (bf16[96,256]{1,0:T(8,128)(2,1)S(1)}, bf16[96,256]{1,0:T(8,128)(2,1)S(1)}, u32[]{:S(2)}, u32[]{:S(2)}) collective-permute-start(bf16[96,256]{1,0:T(8,128)(2,1)S(1)} %get-tuple-element.54), channel_id=1, source_target_pairs={{0,4},{1,5},{2,6},{3,7},{4,0},{5,1},{6,2},{7,3},{8,12},{9,13},{10,... | collective-permute-start | bytes 147464 | tf_op jit(solution)/shard_map/ppermute | solution.py:411
  49.1 5.1 %collective-permute-start.23 = (bf16[96,256]{1,0:T(8,128)(2,1)S(1)}, bf16[96,256]{1,0:T(8,128)(2,1)S(1)}, u32[]{:S(2)}, u32[]{:S(2)}) collective-permute-start(bf16[96,256]{1,0:T(8,128)(2,1)S(1)} %get-tuple-element.63), channel_id=1, source_target_pairs={{0,4},{1,5},{2,6},{3,7},{4,0},{5,1},{6,2},{7,3},{8,12},{9,13},{10,... | collective-permute-start | bytes 147464 | tf_op jit(solution)/shard_map/ppermute | solution.py:411

commit v3 on v2

--- a/solution.py
+++ b/solution.py
@@ -10,8 +10,10 @@
 BAND = 8
 HALO = 16
 EDGE_PART = 4
+FORWARDS = ((4, 8, 12), (12,), ())
 STAT = 8
-STAT_ROWS = 16
+STAT_ROWS = 8
+TURNS = (0, 0)
 LANE = 128
 f32 = jnp.float32
 bf16 = jnp.bfloat16
@@ -20,7 +22,7 @@
 EXACT = lax.Precision.HIGHEST
 
 
-def kernel_call(body, name, args, outs, scratch=(), in_specs=None, mib=4):
+def kernel_call(body, name, args, outs, scratch=(), in_specs=None, mib=4, aliases={}):
     vmem = pl.BlockSpec(memory_space=pltpu.VMEM)
     return pl.pallas_call(
         body,
@@ -28,6 +30,7 @@
         out_specs=[vmem] * len(outs),
         out_shape=[jax.ShapeDtypeStruct(shape, dtype) for shape, dtype in outs],
         scratch_shapes=list(scratch),
+        input_output_aliases=aliases,
         compiler_params=pltpu.CompilerParams(vmem_limit_bytes=mib * 2**20),
         cost_estimate=pl.CostEstimate(flops=0, bytes_accessed=2**18, transcendentals=0),
         name=name,
@@ -105,7 +108,7 @@
                 mid_ref[pl.ds(r * tile, tile), lanes] = (acc * inverse).astype(bf16)
 
 
-def edge_kernel(rim_ref, near_ref, far_ref, dead_ref, width_ref, out_ref, c_ref, *, nframes):
+def edge_kernel(rim_ref, near_ref, far_ref, dead_ref, width_ref, out_ref, top_ref, bottom_ref, c_ref, *, nframes):
     px = rim_ref.shape[1]
     edge = out_ref.shape[0] // 2
     rows = nframes // lax.axis_size("frame")
@@ -131,7 +134,9 @@
                 first = begin + half * (rows - edge) + r * tile
                 t = first + lax.broadcasted_iota(jnp.int32, (tile, LANE), 0)
                 terms = jnp.minimum(t + width, nframes - 1) - jnp.maximum(t - width, 0) + 1
-                out_ref[pl.ds(half * edge + r * tile, tile), lanes] = (acc / terms.astype(f32)).astype(bf16)
+                smoothed = (acc / terms.astype(f32)).astype(bf16)
+                out_ref[pl.ds(half * edge + r * tile, tile), lanes] = smoothed
+                (top_ref, bottom_ref)[half][pl.ds(r * tile, tile), lanes] = smoothed
 
 
 def smooth_middle(frames, dead, width, edge):
@@ -153,9 +158,9 @@
         functools.partial(edge_kernel, nframes=nframes),
         "smooth_edges",
         (rim, near, far, dead, width),
-        [((2 * edge, rim.shape[1]), bf16)],
+        [((2 * edge, rim.shape[1]), bf16)] + [((edge, rim.shape[1]), bf16)] * 2,
         [pltpu.VMEM((2 * (edge + 2 * HALO), LANE), f32)],
-    )[0]
+    )
 
 
 def hold_kernel(*refs):
@@ -176,17 +181,18 @@
     )(x, *tokens)
 
 
-def tree_order(n):
-    return [0] if n == 1 else [2 * s + bit for bit in range(2) for s in tree_order(n // 2)]
-
-
-def centre(product_ref, total_ref, mean, keep_ref, send_ref, groups):
+def tree_order(bits):
+    return [(high << bits[0]) + slot for high in range(2) for slot in tree_order(bits[1:])] if bits else [0]
+
+
+def centre(product_ref, total_ref, mean, keep_ref, send_ref, bits):
     rows = product_ref.shape[0] // CYCLES - 16
-    size = rows // groups
+    half = 2 ** len(bits) // 2
+    size = rows // (2 * half)
     me = lax.axis_index("pixel")
-    for at, slot in enumerate(tree_order(groups)):
-        out_ref = send_ref if slot % 2 else keep_ref
-        place = (at % (groups // 2)) * CYCLES * size
+    for at, slot in enumerate(tree_order(bits)):
+        out_ref = send_ref if at >= half else keep_ref
+        place = (at % half) * CYCLES * size
         for q in range(CYCLES):
             begin = pl.multiple_of(q * rows + (me ^ slot) * size, size)
             total = total_ref[pl.ds(begin, size), :]
@@ -272,26 +278,28 @@
     )
 
 
-def gram_cross_kernel(left_ref, total_ref, *refs, groups):
-    col_refs, (keep_ref, send_ref, stat_ref, acc_ref) = refs[:-4], refs[-4:]
-    right = jnp.concatenate([ref[...] for ref in col_refs], axis=0)
+def gram_cross_kernel(left_ref, total_ref, *refs, bits, cols, at):
+    keep_ref, send_ref, stat_ref, acc_ref = refs[-4:]
+    right = jnp.concatenate([ref[...] for ref in refs[:cols]], axis=0)
     acc_ref[...] = lax.dot_general(left_ref[...], right, NT, preferred_element_type=f32)
     mean, _ = means(acc_ref, total_ref, acc_ref.shape[1])
+    here = pl.ds(at, acc_ref.shape[1])
     stats = stat_rows(mean)
-    stat_ref[...] = stats
-    send_ref[pl.ds(send_ref.shape[0] - STAT_ROWS, STAT_ROWS), :] = stats
-    centre(acc_ref, total_ref, mean, keep_ref, send_ref, groups)
-
-
-def gram_cross(left, total, cols, groups):
-    tall, width = left.shape[0], sum(c.shape[0] for c in cols)
+    stat_ref[:, here] = stats
+    send_ref[pl.ds(send_ref.shape[0] - STAT_ROWS, STAT_ROWS), here] = stats
+    centre(acc_ref, total_ref, mean, keep_ref.at[:, here], send_ref.at[:, here], bits)
+
+
+def gram_cross(left, total, cols, width, at, part, bits):
+    tall = left.shape[0]
     return kernel_call(
-        functools.partial(gram_cross_kernel, groups=groups),
+        functools.partial(gram_cross_kernel, bits=bits, cols=len(cols), at=at),
         "gram_cross",
-        (left, total, *cols),
+        (left, total, *cols, *part),
         part_outs(tall // 2 - 16, width, STAT_ROWS),
-        [pltpu.VMEM((tall, width), f32)],
-        mib=8,
+        [pltpu.VMEM((tall, sum(c.shape[0] for c in cols)), f32)],
+        mib=10,
+        aliases={2 + len(cols) + i: i for i in range(len(part))},
     )
 
 
@@ -327,7 +335,7 @@
     rows = width // 2
     mid = rows - 2 * edge
     me = lax.axis_index("pixel")
-    stats = [got_ref[me ^ i, pl.ds(CYCLES * size, STAT_ROWS), :].astype(f32)[:STAT] for i in range(groups)]
+    stats = [got_ref[me ^ i, pl.ds(CYCLES * size, STAT), :].astype(f32) for i in range(groups)]
     stats = jnp.concatenate(stats, axis=0)
     entries = stats.shape[0]
     kind = lax.broadcasted_iota(jnp.int32, (entries, 1), 0) % STAT
@@ -365,8 +373,10 @@
     return within * inverse + part_between(mean, side, share)
 
 
-def part_sums(keep_ref, got_ref, stat_ref, side_ref, share_ref, groups):
-    stats = join_stats(stat_ref, got_ref, groups // 2)
+def part_sums(keep_ref, got_ref, stat_ref, side_ref, share_ref, bits):
+    stats = join_stats(stat_ref, got_ref, 2 ** len(bits) // 2)
+    spots = [sum((group >> bit & 1) << level for level, bit in enumerate(bits)) for group in range(2 ** len(bits))]
+    stats = jnp.concatenate([stats[STAT * spot : STAT * (spot + 1)] for spot in spots], axis=0)
     entries = stats.shape[0]
     mean = whole_means(stats)
     size = keep_ref.shape[0] // CYCLES
@@ -392,18 +402,17 @@
     return kernel_call(functools.partial(own_part_kernel, edge=edge), "own_part", (got,), outs)
 
 
-def finish_kernel(own_ref, side_ref, share_ref, *refs, parts, rows, edge, groups):
+def finish_kernel(own_ref, side_ref, share_ref, *refs, parts, rows, edge, orders):
     refs, out_ref = refs[:-1], refs[-1]
     size = out_ref.shape[0]
     mid = rows - 2 * edge
     me = lax.axis_index("frame")
     sums = [[ref[pl.ds(q * size, size), :] for q in range(CYCLES)] for ref in (own_ref,)]
-    sums += [part_sums(*refs[i : i + 3], side_ref, share_ref, groups) for i in range(0, len(refs), 3)]
+    sums += [part_sums(*refs[i : i + 3], side_ref, share_ref, orders[i // 3 % 2]) for i in range(0, len(refs), 3)]
     for q in range(CYCLES):
-        for j, ((mid_part, mid_at), (edge_part, edge_at)) in enumerate(parts):
-            mids = sums[mid_part][q][:, mid_at : mid_at + mid]
-            edges = sums[edge_part][q][:, edge_at : edge_at + 2 * edge]
-            natural = jnp.concatenate([edges[:, :edge], mids, edges[:, edge:]], axis=1)
+        for j, places in enumerate(parts):
+            pieces = [sums[part][q][:, at : at + n] for (part, at), n in zip(places, (mid, edge, edge))]
+            natural = jnp.concatenate([pieces[1], pieces[0], pieces[2]], axis=1)
             out_ref[:, q, pl.ds(pl.multiple_of((me ^ j) * rows, rows), rows)] = natural
 
 
@@ -411,9 +420,9 @@
     return lax.ppermute(x, axis, [(i, i ^ bit) for i in range(lax.axis_size(axis))])
 
 
-def swap_pieces(x, n):
-    size = x.shape[0] // n
-    return [swap(x[i * size : (i + 1) * size], "frame", 1) for i in range(n)]
+def swap_pieces(x, *cuts):
+    at = [0] + [x.shape[0] * cut // 16 for cut in cuts] + [x.shape[0]]
+    return [swap(x[i:j], "frame", 1) for i, j in zip(at, at[1:])]
 
 
 def shards(frames, dead_time, band_width, cycle_label, valid):
@@ -438,38 +447,48 @@
     far_mid = {j: swap(mid, "frame", j) for j in range(2, nblocks, 2)}
     near_halo = swap(near_halo, "frame", 1)
     halo = swap(halo, "frame", 1)
-    near = swap_pieces(mid, 4)
-    edge = smooth_edges(rim, near_halo, halo, dead, width, nframes)
-    far_edge = {j: swap(edge, "frame", j) for j in range(2, nblocks, 2)}
-    near += swap_pieces(edge, 4)
-
-    def exchange(send, level):
-        return swap(send, "pixel", 2**level)
+    near = swap_pieces(mid, 8)
+    edge, top, bottom = smooth_edges(rim, near_halo, halo, dead, width, nframes)
+    far_ends = {j: [swap(x, "frame", j) for x in (top, bottom)] for j in range(2, nblocks, 2)}
+    near += swap_pieces(edge, 8)
 
     levels = ngroups.bit_length() - 1
+    orders = [tuple((level + turn) % levels for level in range(levels)) for turn in TURNS]
     own, left, total = gram_own(cycle_label, valid, mid, edge, near, ngroups)
     wait = [total]
     own, side, share = own_part(lax.all_to_all(own, "pixel", 0, 0, tiled=True), edge_rows)
 
-    others, places = [], []
-    later = []
+    sizes = (mid_rows, edge_rows, edge_rows)
+    split = [[(0,)], [(1,), (2,)] if 2 * edge_rows % LANE == 0 else [(1, 2)]]
+    others = []
+    parts = [[(0, i * rows), (0, i * rows + mid_rows), (0, i * rows + mid_rows + edge_rows)] for i in range(2)]
     for j in range(2, nblocks, 2):
-        for source, n in ((far_mid[j], 4), (far_edge[j], 1)):
-            source = hold(source, *wait)
-            keep, send, stat = gram_cross(left, total, [source, *swap_pieces(source, n)], ngroups)
-            wait = [stat]
+        places = [[None] * 3, [None] * 3]
+        pieces = [far_mid[j], *far_ends[j]]
+        for part in split:
+            width = 2 * sum(sizes[k] for group in part for k in group)
+            at, done = 0, ()
+            bits = orders[len(others) // 3 % 2]
+            for group in part:
+                group_rows = sum(sizes[k] for k in group)
+                far, near = [], []
+                for k in group:
+                    for i in range(2):
+                        places[i][k] = (1 + len(others) // 3, at + i * group_rows + sum(x.shape[0] for x in far))
+                    far.append(hold(pieces[k], *wait))
+                    near += swap_pieces(far[-1], *FORWARDS[k])
+                done = gram_cross(left, total, far + near, width, at, done, bits)
+                at += 2 * group_rows
+                wait = [done[2]]
+            keep, send, stat = done
             for level in range(levels):
-                got = exchange(send, level)
+                got = swap(send, "pixel", 1 << bits[level])
                 if level + 1 < levels:
                     keep, send, stat = merge(keep, got, stat, 2**level)
-            later = [own, send]
-            places.append((1 + len(others) // 3, source.shape[0]))
             others += [keep, got, stat]
-    parts = [((0, 0), (0, mid_rows)), ((0, rows), (0, rows + mid_rows))]
-    for pair in zip(places[::2], places[1::2]):
-        parts += [tuple((p, i * n) for p, n in pair) for i in range(2)]
+        parts += places
     return kernel_call(
-        functools.partial(finish_kernel, parts=parts, rows=rows, edge=edge_rows, groups=ngroups),
+        functools.partial(finish_kernel, parts=parts, rows=rows, edge=edge_rows, orders=orders),
         "finish",
         (own, side, share, *others),
         [((own_rows, CYCLES, nframes), f32)],

time: 55.8 us -> 53.7 us (0.962)
  waiting for transfers between devices: 10.5 us -> 7.76 us
  local copies, waits for them, and re-layouts: 4.69 us -> 5.37 us
  Pallas kernels: 13.1 us -> 12.5 us
    ppermute x24 -> x23, waiting for transfers between devices: 10.5 us -> 7.76 us  [swap(): lax.ppermute(x, axis, [(i, i ^ bit) for i in range(lax.axis_size(axis))])]
    slice x3 -> x5, local copies, waits for them, and re-layouts: 1.21 us -> 1.9 us  [swap_pieces(): return [swap(x[i:j], 'frame', 1) for i, j in zip(at, at[1:])]]
    pallas_call x12 -> x13, Pallas kernels: 13.1 us -> 12.5 us  [kernel_call(): pl.pallas_call(body, in_specs=in_specs or [vmem] * len(args), out_specs=[...]
    ppermute x24 -> x23, starting transfers between devices: 21.1 us -> 21.6 us  [swap(): lax.ppermute(x, axis, [(i, i ^ bit) for i in range(lax.axis_size(axis))])]
    unnamed x12 -> x16, local copies, waits for them, and re-layouts: 3.47 us -> 3.47 us
  transfers between devices with their start and end apart: 25 -> 24, of which waited for: 10 -> 9; matrix products, arithmetic and copies ran while one was open for 2% -> 4% of each run, Pallas kernels for 21% -> 21%
where the time goes in v3:
time: 53.7 us; the launch traced here: 53.2 us
  starting transfers between devices  27.4 us (51%)
  Pallas kernels  12.5 us (23%)
  waiting for transfers between devices  7.76 us (14%)
  local copies, waits for them, and re-layouts  5.37 us (10%)
    ppermute x23, starting transfers between devices, swap(): lax.ppermute(x, axis, [(i, i ^ bit) for i in range(lax.axis_size(axis))])  21.6 us
    pallas_call x13, Pallas kernels, kernel_call(): pl.pallas_call(body, in_specs=in_specs or [vmem] * len(args), out_specs=[...  12.5 us
    ppermute x23, waiting for transfers between devices, swap(): lax.ppermute(x, axis, [(i, i ^ bit) for i in range(lax.axis_size(axis))])  7.76 us
    all_to_all x1, starting transfers between devices, shards(): lax.all_to_all(own, 'pixel', 0, 0, tiled=True)  5.83 us
    unnamed x16, local copies, waits for them, and re-layouts  3.47 us
    slice x5, local copies, waits for them, and re-layouts, swap_pieces(): return [swap(x[i:j], 'frame', 1) for i, j in zip(at, at[1:])]  1.9 us
  transfers between devices with their start and end apart: 24, of which 9 were waited for; matrix products, arithmetic and copies ran while one was open for 4% of the time, Pallas kernels for 21%

profile of v3, /device:TPU:0, one launch (start us, length us, event | category | flops | bytes accessed | tf_op | source)
XLA Modules:
  0.0 53.2 jit_solution(12526327070113463188)
XLA Ops:
  0.0 1.2 %copy-done = bf16[256,2048]{1,0:T(8,128)(2,1)S(1)} copy-done((bf16[256,2048]{1,0:T(8,128)(2,1)S(1)}, bf16[256,2048]{1,0:T(8,128)(2,1)}, u32[]{:S(2)}) %copy-start) | copy-done | bytes 1048600
  1.4 3.0 %collective-permute-start = (bf16[16,2048]{1,0:T(8,128)(2,1)S(1)}, bf16[16,2048]{1,0:T(8,128)(2,1)S(1)}, u32[]{:S(2)}, u32[]{:S(2)}) collective-permute-start(bf16[16,2048]{1,0:T(8,128)(2,1)S(1)} %get-tuple-element.42), channel_id=1, source_target_pairs={{0,16},{8,24},{16,0},{24,8},{1,17},{9,25},{17,1},{25,9},{2,18},{10... | collective-permute-start | bytes 196616 | tf_op jit(solution)/shard_map/ppermute | solution.py:420
  4.4 0.7 %copy-done.2 = f32[2048]{0:T(1024)S(1)} copy-done((f32[2048]{0:T(1024)S(1)}, f32[2048]{0:T(1024)}, u32[]{:S(2)}) %copy-start.2) | copy-done | bytes 8216
  5.1 0.7 %copy-done.3 = s32[2048]{0:T(1024)S(1)} copy-done((s32[2048]{0:T(1024)S(1)}, s32[2048]{0:T(1024)}, u32[]{:S(2)}) %copy-start.3) | copy-done | bytes 8216
  5.8 1.4 %smooth_middle.1 = (bf16[128,2048]{1,0:T(8,128)(2,1)S(1)}, bf16[160,2048]{1,0:T(8,128)(2,1)S(1)}, f32[2048]{0:T(1024)S(1)}, s32[2048]{0:T(1024)S(1)}) custom-call(bf16[256,2048]{1,0:T(8,128)(2,1)S(1)} %copy-done, f32[2048]{0:T(1024)S(1)} %copy-done.2, s32[2048]{0:T(1024)S(1)} %copy-done.3), custom_call_target="tpu_custom_call" | custom-call | bytes 262144 | tf_op jit(solution)/shard_map/smooth_middle/pallas_call | solution.py:27
  7.3 0.6 %collective-permute-start.2 = (bf16[16,2048]{1,0:T(8,128)(2,1)S(1)}, bf16[16,2048]{1,0:T(8,128)(2,1)S(1)}, u32[]{:S(2)}, u32[]{:S(2)}) collective-permute-start(bf16[16,2048]{1,0:T(8,128)(2,1)S(1)} %collective-permute-done.refs_1_), channel_id=1, source_target_pairs={{0,8},{8,0},{16,24},{24,16},{1,9},{9,1},{17,25},{25,17},{2,10},{10... | collective-permute-start | bytes 196616 | tf_op jit(solution)/shard_map/ppermute | solution.py:420
  7.9 0.9 %collective-permute-start.7 = (bf16[128,2048]{1,0:T(8,128)(2,1)S(1)}, bf16[128,2048]{1,0:T(8,128)(2,1)S(1)}, u32[]{:S(2)}, u32[]{:S(2)}) collective-permute-start(bf16[128,2048]{1,0:T(8,128)(2,1)S(1)} %hold.4.mid_ref), channel_id=1, source_target_pairs={{0,16},{8,24},{16,0},{24,8},{1,17},{9,25},{17,1},{25,9},{2,18},{10... | collective-permute-start | bytes 1572872 | tf_op jit(solution)/shard_map/ppermute | solution.py:420
  9.3 2.3 %smooth_edges.1 = (bf16[128,2048]{1,0:T(8,128)(2,1)S(1)}, bf16[64,2048]{1,0:T(8,128)(2,1)}, bf16[64,2048]{1,0:T(8,128)(2,1)S(1)}) custom-call(bf16[160,2048]{1,0:T(8,128)(2,1)S(1)} %get-tuple-element.43.rim_ref, bf16[16,2048]{1,0:T(8,128)(2,1)S(1)} %collective-permute-done.1.near_ref, bf16[16,2048]{1,0:T(8,128)(2,1)S(1)} %collective-permute-done.2.far_ref, ...), custom_call_target="tpu_custom_call" | custom-call | bytes 262144 | tf_op jit(solution)/shard_map/smooth_edges/pallas_call | solution.py:27
  12.2 1.2 %collective-permute-start.16 = (bf16[64,2048]{1,0:T(8,128)(2,1)}, bf16[64,2048]{1,0:T(8,128)(2,1)}, u32[]{:S(2)}, u32[]{:S(2)}) collective-permute-start(bf16[64,2048]{1,0:T(8,128)(2,1)} %get-tuple-element.64), channel_id=1, source_target_pairs={{0,16},{8,24},{16,0},{24,8},{1,17},{9,25},{17,1},{25,9},{2,18},{10... | collective-permute-start | bytes 786440 | tf_op jit(solution)/shard_map/ppermute | solution.py:420
  13.6 2.2 %gram_own.1 = (bf16[8,72,512]{2,1,0:T(8,128)(2,1)S(1)}, bf16[544,2048]{1,0:T(8,128)(2,1)S(1)}, f32[544,128]{1,0:T(8,128)S(1)}) custom-call(s32[2048]{0:T(1024)S(1)} %copy-done.4, s32[2048]{0:T(1024)S(1)} %copy-done.5, bf16[128,2048]{1,0:T(8,128)(2,1)S(1)} %hold.4.mid_ref, bf16[128,2048]{1,0:T(8,128)(2,1)S(1)} %get-tuple-element.47.edge_ref, ...), custom_call_target="tpu_custom_call" | custom-call | bytes 262144 | tf_op jit(solution)/shard_map/gram_own/pallas_call | solution.py:27
  15.8 0.8 %copy-done.1 = bf16[8,72,512]{2,1,0:T(8,128)(2,1)} copy-done((bf16[8,72,512]{2,1,0:T(8,128)(2,1)}, bf16[8,72,512]{2,1,0:T(8,128)(2,1)S(1)}, u32[]{:S(2)}) %copy-start.1) | copy-done | bytes 589848
  16.7 5.8 %all-to-all-start = ((bf16[8,72,512]{2,1,0:T(8,128)(2,1)}), bf16[8,72,512]{2,1,0:T(8,128)(2,1)}, u32[]{:S(2)}, u32[]{:S(2)}) async-start(bf16[8,72,512]{2,1,0:T(8,128)(2,1)} %copy-done.1), calls=%async_computation | async-start | bytes 1179648 | tf_op jit(solution)/shard_map/all_to_all | solution.py:459
  22.9 0.5 collective-permute-start.11
  24.2 1.0 %collective-permute-start.15 = (bf16[64,2048]{1,0:T(8,128)(2,1)S(1)}, bf16[64,2048]{1,0:T(8,128)(2,1)S(1)}, u32[]{:S(2)}, u32[]{:S(2)}) collective-permute-start(bf16[64,2048]{1,0:T(8,128)(2,1)S(1)} %copy-done.7), channel_id=1, source_target_pairs={{0,16},{8,24},{16,0},{24,8},{1,17},{9,25},{17,1},{25,9},{2,18},{10... | collective-permute-start | bytes 786440 | tf_op jit(solution)/shard_map/ppermute | solution.py:420
  25.2 0.9 %gram_cross.3 = (bf16[256,256]{1,0:T(8,128)(2,1)S(1)}, bf16[264,256]{1,0:T(8,128)(2,1)S(1)}, bf16[8,256]{1,0:T(8,128)(2,1)S(1)}) custom-call(bf16[544,2048]{1,0:T(8,128)(2,1)S(1)} %get-tuple-element.52.left_ref, f32[544,128]{1,0:T(8,128)S(1)} %get-tuple-element.53.refs_1_.total_ref, bf16[128,2048]{1,0:T(8,128)(2,1)S(1)} %hold.5.refs_0_, ...), custom_call_target="tpu_custom_call" | custom-call | bytes 262144 | tf_op jit(solution)/shard_map/gram_cross/pallas_call | solution.py:27
  26.1 1.9 %collective-permute-done.16.refs_0_ = bf16[64,2048]{1,0:T(8,128)(2,1)} collective-permute-done((bf16[64,2048]{1,0:T(8,128)(2,1)}, bf16[64,2048]{1,0:T(8,128)(2,1)}, u32[]{:S(2)}, u32[]{:S(2)}) %collective-permute-start.16) | collective-permute-done | bytes 262176 | tf_op jit(solution)/shard_map/ppermute | solution.py:420
  28.0 0.9 %slice.46 = bf16[48,2048]{1,0:T(8,128)(2,1)S(1)} slice(bf16[64,2048]{1,0:T(8,128)(2,1)} %hold.6.refs_0_), slice={[0:48], [0:2048]} | slice | bytes 393216 | tf_op jit(solution)/shard_map/slice | solution.py:425
  29.0 0.8 %slice.47 = bf16[16,2048]{1,0:T(8,128)(2,1)S(1)} slice(bf16[64,2048]{1,0:T(8,128)(2,1)} %hold.6.refs_0_), slice={[48:64], [0:2048]} | slice | bytes 131072 | tf_op jit(solution)/shard_map/slice | solution.py:425
  29.8 0.5 collective-permute-start.18
  30.3 0.9 %collective-permute-done.18.refs_2_ = bf16[16,2048]{1,0:T(8,128)(2,1)S(1)} collective-permute-done((bf16[16,2048]{1,0:T(8,128)(2,1)S(1)}, bf16[16,2048]{1,0:T(8,128)(2,1)S(1)}, u32[]{:S(2)}, u32[]{:S(2)}) %collective-permute-start.18) | collective-permute-done | bytes 65568 | tf_op jit(solution)/shard_map/ppermute | solution.py:420
  31.2 1.7 %gram_cross.4 = (bf16[256,256]{1,0:T(8,128)(2,1)S(1)}, bf16[264,256]{1,0:T(8,128)(2,1)S(1)}, bf16[8,256]{1,0:T(8,128)(2,1)S(1)}) custom-call(bf16[544,2048]{1,0:T(8,128)(2,1)S(1)} %get-tuple-element.52.left_ref, f32[544,128]{1,0:T(8,128)S(1)} %get-tuple-element.53.refs_1_.total_ref, bf16[64,2048]{1,0:T(8,128)(2,1)} %hold.6.refs_0_, ...), custom_call_target="tpu_custom_call" | custom-call | bytes 262144 | tf_op jit(solution)/shard_map/gram_cross/pallas_call | solution.py:27
  33.4 1.3 %collective-permute-start.12 = (bf16[264,256]{1,0:T(8,128)(2,1)S(1)}, bf16[264,256]{1,0:T(8,128)(2,1)S(1)}, u32[]{:S(2)}, u32[]{:S(2)}) collective-permute-start(bf16[264,256]{1,0:T(8,128)(2,1)S(1)} %get-tuple-element.55), channel_id=1, source_target_pairs={{0,1},{1,0},{2,3},{3,2},{4,5},{5,4},{6,7},{7,6},{8,9},{9,8},{10,11... | collective-permute-start | bytes 405512 | tf_op jit(solution)/shard_map/ppermute | solution.py:420
  34.7 0.8 %gram_cross.5 = (bf16[256,256]{1,0:T(8,128)(2,1)S(1)}, bf16[264,256]{1,0:T(8,128)(2,1)S(1)}, bf16[8,256]{1,0:T(8,128)(2,1)S(1)}) custom-call(bf16[544,2048]{1,0:T(8,128)(2,1)S(1)} %get-tuple-element.52.left_ref, f32[544,128]{1,0:T(8,128)S(1)} %get-tuple-element.53.refs_1_.total_ref, ...), custom_call_target="tpu_custom_call", output_to_operand_aliasing={{0}: (4, {}), {1}: (5, {}), {2}: (6, {})} | custom-call | bytes 262144 | tf_op jit(solution)/shard_map/gram_cross/pallas_call | solution.py:27
  35.5 1.5 %collective-permute-start.20 = (bf16[264,256]{1,0:T(8,128)(2,1)S(1)}, bf16[264,256]{1,0:T(8,128)(2,1)S(1)}, u32[]{:S(2)}, u32[]{:S(2)}) collective-permute-start(bf16[264,256]{1,0:T(8,128)(2,1)S(1)} %get-tuple-element.69), channel_id=1, source_target_pairs={{0,1},{1,0},{2,3},{3,2},{4,5},{5,4},{6,7},{7,6},{8,9},{9,8},{10,11... | collective-permute-start | bytes 405512 | tf_op jit(solution)/shard_map/ppermute | solution.py:420
  37.0 2.9 %collective-permute-done.12.got_ref = bf16[264,256]{1,0:T(8,128)(2,1)S(1)} collective-permute-done((bf16[264,256]{1,0:T(8,128)(2,1)S(1)}, bf16[264,256]{1,0:T(8,128)(2,1)S(1)}, u32[]{:S(2)}, u32[]{:S(2)}) %collective-permute-start.12) | collective-permute-done | bytes 135200 | tf_op jit(solution)/shard_map/ppermute | solution.py:420
  39.9 2.1 %collective-permute-start.13 = (bf16[144,256]{1,0:T(8,128)(2,1)S(1)}, bf16[144,256]{1,0:T(8,128)(2,1)S(1)}, u32[]{:S(2)}, u32[]{:S(2)}) collective-permute-start(bf16[144,256]{1,0:T(8,128)(2,1)S(1)} %get-tuple-element.58), channel_id=1, source_target_pairs={{0,2},{1,3},{2,0},{3,1},{4,6},{5,7},{6,4},{7,5},{8,10},{9,11},{10,... | collective-permute-start | bytes 221192 | tf_op jit(solution)/shard_map/ppermute | solution.py:420
  42.4 2.1 %collective-permute-start.21 = (bf16[144,256]{1,0:T(8,128)(2,1)S(1)}, bf16[144,256]{1,0:T(8,128)(2,1)S(1)}, u32[]{:S(2)}, u32[]{:S(2)}) collective-permute-start(bf16[144,256]{1,0:T(8,128)(2,1)S(1)} %get-tuple-element.72), channel_id=1, source_target_pairs={{0,2},{1,3},{2,0},{3,1},{4,6},{5,7},{6,4},{7,5},{8,10},{9,11},{10,... | collective-permute-start | bytes 221192 | tf_op jit(solution)/shard_map/ppermute | solution.py:420
  44.5 2.5 %collective-permute-start.14 = (bf16[96,256]{1,0:T(8,128)(2,1)S(1)}, bf16[96,256]{1,0:T(8,128)(2,1)S(1)}, u32[]{:S(2)}, u32[]{:S(2)}) collective-permute-start(bf16[96,256]{1,0:T(8,128)(2,1)S(1)} %get-tuple-element.61), channel_id=1, source_target_pairs={{0,4},{1,5},{2,6},{3,7},{4,0},{5,1},{6,2},{7,3},{8,12},{9,13},{10,... | collective-permute-start | bytes 147464 | tf_op jit(solution)/shard_map/ppermute | solution.py:420
  47.0 2.4 %collective-permute-start.22 = (bf16[96,256]{1,0:T(8,128)(2,1)S(1)}, bf16[96,256]{1,0:T(8,128)(2,1)S(1)}, u32[]{:S(2)}, u32[]{:S(2)}) collective-permute-start(bf16[96,256]{1,0:T(8,128)(2,1)S(1)} %get-tuple-element.75), channel_id=1, source_target_pairs={{0,4},{1,5},{2,6},{3,7},{4,0},{5,1},{6,2},{7,3},{8,12},{9,13},{10,... | collective-permute-start | bytes 147464 | tf_op jit(solution)/shard_map/ppermute | solution.py:420
  49.4 1.7 %own_part.1 = (f32[64,512]{1,0:T(8,128)S(1)}, f32[64,64]{1,0:T(8,128)S(1)}, f32[144,128]{1,0:T(8,128)S(1)}) custom-call(bf16[8,72,512]{2,1,0:T(8,128)(2,1)} %all-to-all-done.got_ref), custom_call_target="tpu_custom_call" | custom-call | bytes 262144 | tf_op jit(solution)/shard_map/own_part/pallas_call | solution.py:27
  51.2 0.9 %collective-permute-done.22.refs_4_ = bf16[96,256]{1,0:T(8,128)(2,1)S(1)} collective-permute-done((bf16[96,256]{1,0:T(8,128)(2,1)S(1)}, bf16[96,256]{1,0:T(8,128)(2,1)S(1)}, u32[]{:S(2)}, u32[]{:S(2)}) %collective-permute-start.22) | collective-permute-done | bytes 49184 | tf_op jit(solution)/shard_map/ppermute | solution.py:420
  52.1 1.2 %finish.1 = f32[32,2,1024]{2,1,0:T(2,128)} custom-call(f32[64,512]{1,0:T(8,128)S(1)} %get-tuple-element.49.own_ref, f32[64,64]{1,0:T(8,128)S(1)} %get-tuple-element.50.side_ref, f32[144,128]{1,0:T(8,128)S(1)} %get-tuple-element.51.share_ref, bf16[64,256]{1,0:T(8,128)(2,1)S(1)} %get-tuple-element.60.refs_0_, ...), custom_call_target="tpu_custom_call" | custom-call | bytes 262144 | tf_op jit(solution)/shard_map/finish/pallas_call | solution.py:27
  (54 shorter events, 3.7 us)
Async XLA Ops:
  0.0 1.2 %copy-start = (bf16[256,2048]{1,0:T(8,128)(2,1)S(1)}, bf16[256,2048]{1,0:T(8,128)(2,1)}, u32[]{:S(2)}) copy-start(bf16[256,2048]{1,0:T(8,128)(2,1)} %frames_ref.3) | copy-start | bytes 3145732
  1.4 5.9 %collective-permute-start = (bf16[16,2048]{1,0:T(8,128)(2,1)S(1)}, bf16[16,2048]{1,0:T(8,128)(2,1)S(1)}, u32[]{:S(2)}, u32[]{:S(2)}) collective-permute-start(bf16[16,2048]{1,0:T(8,128)(2,1)S(1)} %get-tuple-element.42), channel_id=1, source_target_pairs={{0,16},{8,24},{16,0},{24,8},{1,17},{9,25},{17,1},{25,9},{2,18},{10... | collective-permute-start | bytes 196616 | tf_op jit(solution)/shard_map/ppermute | solution.py:420
  4.4 4.9 %collective-permute-start.1 = (bf16[16,2048]{1,0:T(8,128)(2,1)S(1)}, bf16[16,2048]{1,0:T(8,128)(2,1)S(1)}, u32[]{:S(2)}, u32[]{:S(2)}) collective-permute-start(bf16[16,2048]{1,0:T(8,128)(2,1)S(1)} %get-tuple-element.44), channel_id=1, source_target_pairs={{0,8},{8,0},{16,24},{24,16},{1,9},{9,1},{17,25},{25,17},{2,10},{10... | collective-permute-start | bytes 196616 | tf_op jit(solution)/shard_map/ppermute | solution.py:420
  4.4 0.7 %copy-start.2 = (f32[2048]{0:T(1024)S(1)}, f32[2048]{0:T(1024)}, u32[]{:S(2)}) copy-start(f32[2048]{0:T(1024)} %dead_hbm.1) | copy-start | bytes 24580
  5.1 0.7 %copy-start.3 = (s32[2048]{0:T(1024)S(1)}, s32[2048]{0:T(1024)}, u32[]{:S(2)}) copy-start(s32[2048]{0:T(1024)} %width_hbm.1) | copy-start | bytes 24580
  7.3 6.4 %copy-start.4 = (s32[2048]{0:T(1024)S(1)}, s32[2048]{0:T(1024)}, u32[]{:S(2)}) copy-start(s32[2048]{0:T(1024)} %label_ref.1) | copy-start | bytes 24580
  7.3 6.3 %copy-start.5 = (s32[2048]{0:T(1024)S(1)}, s32[2048]{0:T(1024)}, u32[]{:S(2)}) copy-start(s32[2048]{0:T(1024)} %valid_ref.1) | copy-start | bytes 24580
  7.3 2.0 %collective-permute-start.2 = (bf16[16,2048]{1,0:T(8,128)(2,1)S(1)}, bf16[16,2048]{1,0:T(8,128)(2,1)S(1)}, u32[]{:S(2)}, u32[]{:S(2)}) collective-permute-start(bf16[16,2048]{1,0:T(8,128)(2,1)S(1)} %collective-permute-done.refs_1_), channel_id=1, source_target_pairs={{0,8},{8,0},{16,24},{24,16},{1,9},{9,1},{17,25},{25,17},{2,10},{10... | collective-permute-start | bytes 196616 | tf_op jit(solution)/shard_map/ppermute | solution.py:420
  7.9 14.8 %collective-permute-start.7 = (bf16[128,2048]{1,0:T(8,128)(2,1)S(1)}, bf16[128,2048]{1,0:T(8,128)(2,1)S(1)}, u32[]{:S(2)}, u32[]{:S(2)}) collective-permute-start(bf16[128,2048]{1,0:T(8,128)(2,1)S(1)} %hold.4.mid_ref), channel_id=1, source_target_pairs={{0,16},{8,24},{16,0},{24,8},{1,17},{9,25},{17,1},{25,9},{2,18},{10... | collective-permute-start | bytes 1572872 | tf_op jit(solution)/shard_map/ppermute | solution.py:420
  8.8 3.4 %collective-permute-start.3 = (bf16[64,2048]{1,0:T(8,128)(2,1)S(1)}, bf16[64,2048]{1,0:T(8,128)(2,1)S(1)}, u32[]{:S(2)}, u32[]{:S(2)}) collective-permute-start(bf16[64,2048]{1,0:T(8,128)(2,1)S(1)} %get-tuple-element.84), channel_id=1, source_target_pairs={{0,8},{8,0},{16,24},{24,16},{1,9},{9,1},{17,25},{25,17},{2,10},{10... | collective-permute-start | bytes 786440 | tf_op jit(solution)/shard_map/ppermute | solution.py:420
  9.0 4.4 %collective-permute-start.4 = (bf16[64,2048]{1,0:T(8,128)(2,1)S(1)}, bf16[64,2048]{1,0:T(8,128)(2,1)S(1)}, u32[]{:S(2)}, u32[]{:S(2)}) collective-permute-start(bf16[64,2048]{1,0:T(8,128)(2,1)S(1)} %get-tuple-element.83), channel_id=1, source_target_pairs={{0,8},{8,0},{16,24},{24,16},{1,9},{9,1},{17,25},{25,17},{2,10},{10... | collective-permute-start | bytes 786440 | tf_op jit(solution)/shard_map/ppermute | solution.py:420
  11.6 1.8 %copy-start.6 = (bf16[64,2048]{1,0:T(8,128)(2,1)}, bf16[64,2048]{1,0:T(8,128)(2,1)S(1)}, u32[]{:S(2)}) copy-start(bf16[64,2048]{1,0:T(8,128)(2,1)S(1)} %get-tuple-element.63) | copy-start | bytes 786436
  11.6 1.8 %collective-permute-start.5 = (bf16[64,2048]{1,0:T(8,128)(2,1)S(1)}, bf16[64,2048]{1,0:T(8,128)(2,1)S(1)}, u32[]{:S(2)}, u32[]{:S(2)}) collective-permute-start(bf16[64,2048]{1,0:T(8,128)(2,1)S(1)} %get-tuple-element.82), channel_id=1, source_target_pairs={{0,8},{8,0},{16,24},{24,16},{1,9},{9,1},{17,25},{25,17},{2,10},{10... | collective-permute-start | bytes 786440 | tf_op jit(solution)/shard_map/ppermute | solution.py:420
  11.9 1.7 %collective-permute-start.6 = (bf16[64,2048]{1,0:T(8,128)(2,1)S(1)}, bf16[64,2048]{1,0:T(8,128)(2,1)S(1)}, u32[]{:S(2)}, u32[]{:S(2)}) collective-permute-start(bf16[64,2048]{1,0:T(8,128)(2,1)S(1)} %get-tuple-element.81), channel_id=1, source_target_pairs={{0,8},{8,0},{16,24},{24,16},{1,9},{9,1},{17,25},{25,17},{2,10},{10... | collective-permute-start | bytes 786440 | tf_op jit(solution)/shard_map/ppermute | solution.py:420
  12.2 15.7 %collective-permute-start.16 = (bf16[64,2048]{1,0:T(8,128)(2,1)}, bf16[64,2048]{1,0:T(8,128)(2,1)}, u32[]{:S(2)}, u32[]{:S(2)}) collective-permute-start(bf16[64,2048]{1,0:T(8,128)(2,1)} %get-tuple-element.64), channel_id=1, source_target_pairs={{0,16},{8,24},{16,0},{24,8},{1,17},{9,25},{17,1},{25,9},{2,18},{10... | collective-permute-start | bytes 786440 | tf_op jit(solution)/shard_map/ppermute | solution.py:420
  15.8 0.8 %copy-start.1 = (bf16[8,72,512]{2,1,0:T(8,128)(2,1)}, bf16[8,72,512]{2,1,0:T(8,128)(2,1)S(1)}, u32[]{:S(2)}) copy-start(bf16[8,72,512]{2,1,0:T(8,128)(2,1)S(1)} %get-tuple-element.48) | copy-start | bytes 1769476
  16.7 32.8 %all-to-all-start = ((bf16[8,72,512]{2,1,0:T(8,128)(2,1)}), bf16[8,72,512]{2,1,0:T(8,128)(2,1)}, u32[]{:S(2)}, u32[]{:S(2)}) async-start(bf16[8,72,512]{2,1,0:T(8,128)(2,1)} %copy-done.1), calls=%async_computation | async-start | bytes 1179648 | tf_op jit(solution)/shard_map/all_to_all | solution.py:459
  22.5 1.7 %copy-start.7 = (bf16[64,2048]{1,0:T(8,128)(2,1)S(1)}, bf16[64,2048]{1,0:T(8,128)(2,1)}, u32[]{:S(2)}) copy-start(bf16[64,2048]{1,0:T(8,128)(2,1)} %copy-done.6) | copy-start | bytes 786436
  22.8 1.4 %collective-permute-start.10 = (bf16[32,2048]{1,0:T(8,128)(2,1)S(1)}, bf16[32,2048]{1,0:T(8,128)(2,1)S(1)}, u32[]{:S(2)}, u32[]{:S(2)}) collective-permute-start(bf16[32,2048]{1,0:T(8,128)(2,1)S(1)} %get-tuple-element.78), channel_id=1, source_target_pairs={{0,8},{8,0},{16,24},{24,16},{1,9},{9,1},{17,25},{25,17},{2,10},{10... | collective-permute-start | bytes 393224 | tf_op jit(solution)/shard_map/ppermute | solution.py:420
  22.9 2.3 %collective-permute-start.11 = (bf16[32,2048]{1,0:T(8,128)(2,1)S(1)}, bf16[32,2048]{1,0:T(8,128)(2,1)S(1)}, u32[]{:S(2)}, u32[]{:S(2)}) collective-permute-start(bf16[32,2048]{1,0:T(8,128)(2,1)S(1)} %get-tuple-element.77), channel_id=1, source_target_pairs={{0,8},{8,0},{16,24},{24,16},{1,9},{9,1},{17,25},{25,17},{2,10},{10... | collective-permute-start | bytes 393224 | tf_op jit(solution)/shard_map/ppermute | solution.py:420
  23.4 1.8 %collective-permute-start.8 = (bf16[32,2048]{1,0:T(8,128)(2,1)S(1)}, bf16[32,2048]{1,0:T(8,128)(2,1)S(1)}, u32[]{:S(2)}, u32[]{:S(2)}) collective-permute-start(bf16[32,2048]{1,0:T(8,128)(2,1)S(1)} %get-tuple-element.80), channel_id=1, source_target_pairs={{0,8},{8,0},{16,24},{24,16},{1,9},{9,1},{17,25},{25,17},{2,10},{10... | collective-permute-start | bytes 393224 | tf_op jit(solution)/shard_map/ppermute | solution.py:420
  23.5 1.8 %collective-permute-start.9 = (bf16[32,2048]{1,0:T(8,128)(2,1)S(1)}, bf16[32,2048]{1,0:T(8,128)(2,1)S(1)}, u32[]{:S(2)}, u32[]{:S(2)}) collective-permute-start(bf16[32,2048]{1,0:T(8,128)(2,1)S(1)} %get-tuple-element.79), channel_id=1, source_target_pairs={{0,8},{8,0},{16,24},{24,16},{1,9},{9,1},{17,25},{25,17},{2,10},{10... | collective-permute-start | bytes 393224 | tf_op jit(solution)/shard_map/ppermute | solution.py:420
  24.2 8.8 %collective-permute-start.15 = (bf16[64,2048]{1,0:T(8,128)(2,1)S(1)}, bf16[64,2048]{1,0:T(8,128)(2,1)S(1)}, u32[]{:S(2)}, u32[]{:S(2)}) collective-permute-start(bf16[64,2048]{1,0:T(8,128)(2,1)S(1)} %copy-done.7), channel_id=1, source_target_pairs={{0,16},{8,24},{16,0},{24,8},{1,17},{9,25},{17,1},{25,9},{2,18},{10... | collective-permute-start | bytes 786440 | tf_op jit(solution)/shard_map/ppermute | solution.py:420
  28.9 2.3 %collective-permute-start.17 = (bf16[48,2048]{1,0:T(8,128)(2,1)S(1)}, bf16[48,2048]{1,0:T(8,128)(2,1)S(1)}, u32[]{:S(2)}, u32[]{:S(2)}) collective-permute-start(bf16[48,2048]{1,0:T(8,128)(2,1)S(1)} %slice.46), channel_id=1, source_target_pairs={{0,8},{8,0},{16,24},{24,16},{1,9},{9,1},{17,25},{25,17},{2,10},{10... | collective-permute-start | bytes 589832 | tf_op jit(solution)/shard_map/ppermute | solution.py:420
  29.8 1.4 %collective-permute-start.18 = (bf16[16,2048]{1,0:T(8,128)(2,1)S(1)}, bf16[16,2048]{1,0:T(8,128)(2,1)S(1)}, u32[]{:S(2)}, u32[]{:S(2)}) collective-permute-start(bf16[16,2048]{1,0:T(8,128)(2,1)S(1)} %slice.47), channel_id=1, source_target_pairs={{0,8},{8,0},{16,24},{24,16},{1,9},{9,1},{17,25},{25,17},{2,10},{10... | collective-permute-start | bytes 196616 | tf_op jit(solution)/shard_map/ppermute | solution.py:420
  33.1 1.6 %collective-permute-start.19 = (bf16[64,2048]{1,0:T(8,128)(2,1)S(1)}, bf16[64,2048]{1,0:T(8,128)(2,1)S(1)}, u32[]{:S(2)}, u32[]{:S(2)}) collective-permute-start(bf16[64,2048]{1,0:T(8,128)(2,1)S(1)} %hold.7.refs_0_), channel_id=1, source_target_pairs={{0,8},{8,0},{16,24},{24,16},{1,9},{9,1},{17,25},{25,17},{2,10},{10... | collective-permute-start | bytes 786440 | tf_op jit(solution)/shard_map/ppermute | solution.py:420
  33.4 6.4 %collective-permute-start.12 = (bf16[264,256]{1,0:T(8,128)(2,1)S(1)}, bf16[264,256]{1,0:T(8,128)(2,1)S(1)}, u32[]{:S(2)}, u32[]{:S(2)}) collective-permute-start(bf16[264,256]{1,0:T(8,128)(2,1)S(1)} %get-tuple-element.55), channel_id=1, source_target_pairs={{0,1},{1,0},{2,3},{3,2},{4,5},{5,4},{6,7},{7,6},{8,9},{9,8},{10,11... | collective-permute-start | bytes 405512 | tf_op jit(solution)/shard_map/ppermute | solution.py:420
  35.5 6.9 %collective-permute-start.20 = (bf16[264,256]{1,0:T(8,128)(2,1)S(1)}, bf16[264,256]{1,0:T(8,128)(2,1)S(1)}, u32[]{:S(2)}, u32[]{:S(2)}) collective-permute-start(bf16[264,256]{1,0:T(8,128)(2,1)S(1)} %get-tuple-element.69), channel_id=1, source_target_pairs={{0,1},{1,0},{2,3},{3,2},{4,5},{5,4},{6,7},{7,6},{8,9},{9,8},{10,11... | collective-permute-start | bytes 405512 | tf_op jit(solution)/shard_map/ppermute | solution.py:420
  39.9 4.6 %collective-permute-start.13 = (bf16[144,256]{1,0:T(8,128)(2,1)S(1)}, bf16[144,256]{1,0:T(8,128)(2,1)S(1)}, u32[]{:S(2)}, u32[]{:S(2)}) collective-permute-start(bf16[144,256]{1,0:T(8,128)(2,1)S(1)} %get-tuple-element.58), channel_id=1, source_target_pairs={{0,2},{1,3},{2,0},{3,1},{4,6},{5,7},{6,4},{7,5},{8,10},{9,11},{10,... | collective-permute-start | bytes 221192 | tf_op jit(solution)/shard_map/ppermute | solution.py:420
  42.4 4.6 %collective-permute-start.21 = (bf16[144,256]{1,0:T(8,128)(2,1)S(1)}, bf16[144,256]{1,0:T(8,128)(2,1)S(1)}, u32[]{:S(2)}, u32[]{:S(2)}) collective-permute-start(bf16[144,256]{1,0:T(8,128)(2,1)S(1)} %get-tuple-element.72), channel_id=1, source_target_pairs={{0,2},{1,3},{2,0},{3,1},{4,6},{5,7},{6,4},{7,5},{8,10},{9,11},{10,... | collective-permute-start | bytes 221192 | tf_op jit(solution)/shard_map/ppermute | solution.py:420
  44.5 6.7 %collective-permute-start.14 = (bf16[96,256]{1,0:T(8,128)(2,1)S(1)}, bf16[96,256]{1,0:T(8,128)(2,1)S(1)}, u32[]{:S(2)}, u32[]{:S(2)}) collective-permute-start(bf16[96,256]{1,0:T(8,128)(2,1)S(1)} %get-tuple-element.61), channel_id=1, source_target_pairs={{0,4},{1,5},{2,6},{3,7},{4,0},{5,1},{6,2},{7,3},{8,12},{9,13},{10,... | collective-permute-start | bytes 147464 | tf_op jit(solution)/shard_map/ppermute | solution.py:420
  47.0 5.1 %collective-permute-start.22 = (bf16[96,256]{1,0:T(8,128)(2,1)S(1)}, bf16[96,256]{1,0:T(8,128)(2,1)S(1)}, u32[]{:S(2)}, u32[]{:S(2)}) collective-permute-start(bf16[96,256]{1,0:T(8,128)(2,1)S(1)} %get-tuple-element.75), channel_id=1, source_target_pairs={{0,4},{1,5},{2,6},{3,7},{4,0},{5,1},{6,2},{7,3},{8,12},{9,13},{10,... | collective-permute-start | bytes 147464 | tf_op jit(solution)/shard_map/ppermute | solution.py:420

commit v4 on v3

--- a/solution.py
+++ b/solution.py
@@ -13,7 +13,6 @@
 FORWARDS = ((4, 8, 12), (12,), ())
 STAT = 8
 STAT_ROWS = 8
-TURNS = (0, 0)
 LANE = 128
 f32 = jnp.float32
 bf16 = jnp.bfloat16
@@ -50,62 +49,34 @@
     return acc
 
 
-def halo_kernel(frames_ref, near_ref, far_ref, ends_ref, sems):
+def halo_kernel(frames_ref, near_ref, far_ref):
     rows = frames_ref.shape[0]
-    copies = [
-        pltpu.make_async_copy(frames_ref.at[pl.ds(at, HALO)], ends_ref.at[i], sems.at[i])
-        for i, at in enumerate((0, rows - HALO))
-    ]
-    for copy in copies:
-        copy.start()
-    for copy in copies:
-        copy.wait()
     even = lax.axis_index("frame") % 2 == 0
-    first, last = ends_ref[0], ends_ref[1]
+    first, last = frames_ref[pl.ds(0, HALO), :], frames_ref[pl.ds(rows - HALO, HALO), :]
     far_ref[...] = jnp.where(even, first, last)
     near_ref[...] = jnp.where(even, last, first)
 
 
 def halos(frames):
-    rows, px = frames.shape
-    return kernel_call(
-        halo_kernel,
-        "halos",
-        (frames,),
-        [((HALO, px), bf16)] * 2,
-        [pltpu.VMEM((2, HALO, px), bf16), pltpu.SemaphoreType.DMA((2,))],
-        in_specs=[pl.BlockSpec(memory_space=pltpu.HBM)],
-    )
-
-
-def middle_kernel(frames_ref, dead_hbm, width_hbm, mid_ref, rim_ref, dead_ref, width_ref, raw_ref, c_ref, sems):
+    px = frames.shape[1]
+    return kernel_call(halo_kernel, "halos", (frames,), [((HALO, px), bf16)] * 2)
+
+
+def middle_kernel(frames_ref, dead_ref, width_ref, mid_ref, rim_ref, c_ref):
     rows, px = frames_ref.shape
     edge = rim_ref.shape[0] // 2 - HALO
     tile = 32
-    chunk = min(512, px)
-    small = [pltpu.make_async_copy(dead_hbm, dead_ref, sems.at[0]), pltpu.make_async_copy(width_hbm, width_ref, sems.at[1])]
-    large = [
-        pltpu.make_async_copy(frames_ref.at[:, pl.ds(i * chunk, chunk)], raw_ref.at[:, pl.ds(i * chunk, chunk)], sems.at[2 + i])
-        for i in range(px // chunk)
-    ]
-    for copy in small + large:
-        copy.start()
-    for copy in small:
-        copy.wait()
-    for i, copy in enumerate(large):
-        copy.wait()
-        part = pl.ds(i * chunk, chunk)
-        rim_ref[pl.ds(0, edge + HALO), part] = raw_ref[pl.ds(0, edge + HALO), part]
-        rim_ref[pl.ds(edge + HALO, edge + HALO), part] = raw_ref[pl.ds(rows - edge - HALO, edge + HALO), part]
-        for col in range(chunk // LANE):
-            lanes = pl.ds(i * chunk + col * LANE, LANE)
-            dead = dead_ref[lanes][None, :]
-            width = width_ref[lanes][None, :]
-            inverse = 1.0 / (2 * width + 1).astype(f32)
-            c_ref[...] = correct(raw_ref[pl.ds(edge - HALO, rows - 2 * edge + 2 * HALO), lanes], dead)
-            for r in range((rows - 2 * edge) // tile):
-                acc = band_sum(c_ref, HALO + r * tile, tile, width)
-                mid_ref[pl.ds(r * tile, tile), lanes] = (acc * inverse).astype(bf16)
+    rim_ref[pl.ds(0, edge + HALO), :] = frames_ref[pl.ds(0, edge + HALO), :]
+    rim_ref[pl.ds(edge + HALO, edge + HALO), :] = frames_ref[pl.ds(rows - edge - HALO, edge + HALO), :]
+    for col in range(px // LANE):
+        lanes = pl.ds(col * LANE, LANE)
+        dead = dead_ref[lanes][None, :]
+        width = width_ref[lanes][None, :]
+        inverse = 1.0 / (2 * width + 1).astype(f32)
+        c_ref[...] = correct(frames_ref[pl.ds(edge - HALO, rows - 2 * edge + 2 * HALO), lanes], dead)
+        for r in range((rows - 2 * edge) // tile):
+            acc = band_sum(c_ref, HALO + r * tile, tile, width)
+            mid_ref[pl.ds(r * tile, tile), lanes] = (acc * inverse).astype(bf16)
 
 
 def edge_kernel(rim_ref, near_ref, far_ref, dead_ref, width_ref, out_ref, top_ref, bottom_ref, c_ref, *, nframes):
@@ -146,9 +117,8 @@
         middle_kernel,
         "smooth_middle",
         (frames, dead, width),
-        [((mid, px), bf16), ((2 * (edge + HALO), px), bf16), ((px,), f32), ((px,), jnp.int32)],
-        [pltpu.VMEM((rows, px), bf16), pltpu.VMEM((mid + 2 * HALO, LANE), f32), pltpu.SemaphoreType.DMA((2 + px // min(512, px),))],
-        in_specs=[pl.BlockSpec(memory_space=pltpu.HBM)] * 3,
+        [((mid, px), bf16), ((2 * (edge + HALO), px), bf16)],
+        [pltpu.VMEM((mid + 2 * HALO, LANE), f32)],
     )
 
 
@@ -437,7 +407,7 @@
     even = lax.axis_index("frame") % 2 == 0
 
     near_halo, far_halo = halos(frames)
-    mid, rim, dead, width = smooth_middle(frames, dead_time, band_width, edge_rows)
+    mid, rim = smooth_middle(frames, dead_time, band_width, edge_rows)
     halo = far_halo
     for bit in sorted({x ^ (x + 1) for x in range(nblocks // 2 - 1)}):
         got = swap(far_halo, "frame", 2 * bit)
@@ -448,12 +418,13 @@
     near_halo = swap(near_halo, "frame", 1)
     halo = swap(halo, "frame", 1)
     near = swap_pieces(mid, 8)
-    edge, top, bottom = smooth_edges(rim, near_halo, halo, dead, width, nframes)
+    edge, top, bottom = smooth_edges(rim, near_halo, halo, dead_time, band_width, nframes)
     far_ends = {j: [swap(x, "frame", j) for x in (top, bottom)] for j in range(2, nblocks, 2)}
     near += swap_pieces(edge, 8)
 
     levels = ngroups.bit_length() - 1
-    orders = [tuple((level + turn) % levels for level in range(levels)) for turn in TURNS]
+    straight = tuple(range(levels))
+    orders = [straight, (straight[:2][::-1] + straight[2:])]
     own, left, total = gram_own(cycle_label, valid, mid, edge, near, ngroups)
     wait = [total]
     own, side, share = own_part(lax.all_to_all(own, "pixel", 0, 0, tiled=True), edge_rows)

time: 53.7 us -> 52.7 us (0.981)
  starting transfers between devices: 27.4 us -> 26.2 us
  waiting for transfers between devices: 7.76 us -> 8.31 us
    ppermute x23, starting transfers between devices: 21.6 us -> 20.4 us  [swap(): lax.ppermute(x, axis, [(i, i ^ bit) for i in range(lax.axis_size(axis))])]
    ppermute x23, waiting for transfers between devices: 7.76 us -> 8.3 us  [swap(): lax.ppermute(x, axis, [(i, i ^ bit) for i in range(lax.axis_size(axis))])]
  transfers between devices with their start and end apart: 24 -> 24, of which waited for: 9 -> 10; matrix products, arithmetic and copies ran while one was open for 4% -> 4% of each run, Pallas kernels for 21% -> 21%
where the time goes in v4:
time: 52.7 us; the launch traced here: 52.2 us
  starting transfers between devices  26.2 us (50%)
  Pallas kernels  12.2 us (23%)
  waiting for transfers between devices  8.31 us (16%)
  local copies, waits for them, and re-layouts  5.37 us (10%)
    ppermute x23, starting transfers between devices, swap(): lax.ppermute(x, axis, [(i, i ^ bit) for i in range(lax.axis_size(axis))])  20.4 us
    pallas_call x13, Pallas kernels, kernel_call(): pl.pallas_call(body, in_specs=in_specs or [vmem] * len(args), out_specs=[...  12.2 us
    ppermute x23, waiting for transfers between devices, swap(): lax.ppermute(x, axis, [(i, i ^ bit) for i in range(lax.axis_size(axis))])  8.3 us
    all_to_all x1, starting transfers between devices, shards(): lax.all_to_all(own, 'pixel', 0, 0, tiled=True)  5.84 us
    unnamed x16, local copies, waits for them, and re-layouts  3.47 us
    slice x5, local copies, waits for them, and re-layouts, swap_pieces(): return [swap(x[i:j], 'frame', 1) for i, j in zip(at, at[1:])]  1.9 us
  transfers between devices with their start and end apart: 24, of which 10 were waited for; matrix products, arithmetic and copies ran while one was open for 4% of the time, Pallas kernels for 21%

profile of v4, /device:TPU:0, one launch (start us, length us, event | category | flops | bytes accessed | tf_op | source)
XLA Modules:
  0.0 52.2 jit_solution(7450379155119546972)
XLA Ops:
  0.0 1.2 %copy-done = bf16[256,2048]{1,0:T(8,128)(2,1)S(1)} copy-done((bf16[256,2048]{1,0:T(8,128)(2,1)S(1)}, bf16[256,2048]{1,0:T(8,128)(2,1)}, u32[]{:S(2)}) %copy-start) | copy-done | bytes 1048600
  1.2 3.0 %collective-permute-start = (bf16[16,2048]{1,0:T(8,128)(2,1)S(1)}, bf16[16,2048]{1,0:T(8,128)(2,1)S(1)}, u32[]{:S(2)}, u32[]{:S(2)}) collective-permute-start(bf16[16,2048]{1,0:T(8,128)(2,1)S(1)} %get-tuple-element.40), channel_id=1, source_target_pairs={{0,16},{8,24},{16,0},{24,8},{1,17},{9,25},{17,1},{25,9},{2,18},{10... | collective-permute-start | bytes 196616 | tf_op jit(solution)/shard_map/ppermute | solution.py:390
  4.3 0.7 %copy-done.2 = f32[2048]{0:T(1024)S(1)} copy-done((f32[2048]{0:T(1024)S(1)}, f32[2048]{0:T(1024)}, u32[]{:S(2)}) %copy-start.2) | copy-done | bytes 8216
  5.0 0.7 %copy-done.3 = s32[2048]{0:T(1024)S(1)} copy-done((s32[2048]{0:T(1024)S(1)}, s32[2048]{0:T(1024)}, u32[]{:S(2)}) %copy-start.3) | copy-done | bytes 8216
  5.6 1.3 %smooth_middle.1 = (bf16[128,2048]{1,0:T(8,128)(2,1)S(1)}, bf16[160,2048]{1,0:T(8,128)(2,1)S(1)}) custom-call(bf16[256,2048]{1,0:T(8,128)(2,1)S(1)} %copy-done, f32[2048]{0:T(1024)S(1)} %copy-done.2, s32[2048]{0:T(1024)S(1)} %copy-done.3), custom_call_target="tpu_custom_call" | custom-call | bytes 262144 | tf_op jit(solution)/shard_map/smooth_middle/pallas_call | solution.py:26
  7.0 0.6 %collective-permute-start.2 = (bf16[16,2048]{1,0:T(8,128)(2,1)S(1)}, bf16[16,2048]{1,0:T(8,128)(2,1)S(1)}, u32[]{:S(2)}, u32[]{:S(2)}) collective-permute-start(bf16[16,2048]{1,0:T(8,128)(2,1)S(1)} %collective-permute-done.refs_1_), channel_id=1, source_target_pairs={{0,8},{8,0},{16,24},{24,16},{1,9},{9,1},{17,25},{25,17},{2,10},{10... | collective-permute-start | bytes 196616 | tf_op jit(solution)/shard_map/ppermute | solution.py:390
  7.6 1.0 %collective-permute-start.7 = (bf16[128,2048]{1,0:T(8,128)(2,1)S(1)}, bf16[128,2048]{1,0:T(8,128)(2,1)S(1)}, u32[]{:S(2)}, u32[]{:S(2)}) collective-permute-start(bf16[128,2048]{1,0:T(8,128)(2,1)S(1)} %hold.4.mid_ref), channel_id=1, source_target_pairs={{0,16},{8,24},{16,0},{24,8},{1,17},{9,25},{17,1},{25,9},{2,18},{10... | collective-permute-start | bytes 1572872 | tf_op jit(solution)/shard_map/ppermute | solution.py:390
  9.1 2.3 %smooth_edges.1 = (bf16[128,2048]{1,0:T(8,128)(2,1)S(1)}, bf16[64,2048]{1,0:T(8,128)(2,1)}, bf16[64,2048]{1,0:T(8,128)(2,1)S(1)}) custom-call(bf16[160,2048]{1,0:T(8,128)(2,1)S(1)} %get-tuple-element.41.rim_ref, bf16[16,2048]{1,0:T(8,128)(2,1)S(1)} %collective-permute-done.1.near_ref, bf16[16,2048]{1,0:T(8,128)(2,1)S(1)} %collective-permute-done.2.far_ref, ...), custom_call_target="tpu_custom_call" | custom-call | bytes 262144 | tf_op jit(solution)/shard_map/smooth_edges/pallas_call | solution.py:26
  12.1 1.1 %collective-permute-start.16 = (bf16[64,2048]{1,0:T(8,128)(2,1)}, bf16[64,2048]{1,0:T(8,128)(2,1)}, u32[]{:S(2)}, u32[]{:S(2)}) collective-permute-start(bf16[64,2048]{1,0:T(8,128)(2,1)} %get-tuple-element.60), channel_id=1, source_target_pairs={{0,16},{8,24},{16,0},{24,8},{1,17},{9,25},{17,1},{25,9},{2,18},{10... | collective-permute-start | bytes 786440 | tf_op jit(solution)/shard_map/ppermute | solution.py:390
  13.5 2.2 %gram_own.1 = (bf16[8,72,512]{2,1,0:T(8,128)(2,1)S(1)}, bf16[544,2048]{1,0:T(8,128)(2,1)S(1)}, f32[544,128]{1,0:T(8,128)S(1)}) custom-call(s32[2048]{0:T(1024)S(1)} %copy-done.4, s32[2048]{0:T(1024)S(1)} %copy-done.5, bf16[128,2048]{1,0:T(8,128)(2,1)S(1)} %hold.4.mid_ref, bf16[128,2048]{1,0:T(8,128)(2,1)S(1)} %get-tuple-element.43.edge_ref, ...), custom_call_target="tpu_custom_call" | custom-call | bytes 262144 | tf_op jit(solution)/shard_map/gram_own/pallas_call | solution.py:26
  15.7 0.8 %copy-done.1 = bf16[8,72,512]{2,1,0:T(8,128)(2,1)} copy-done((bf16[8,72,512]{2,1,0:T(8,128)(2,1)}, bf16[8,72,512]{2,1,0:T(8,128)(2,1)S(1)}, u32[]{:S(2)}) %copy-start.1) | copy-done | bytes 589848
  16.5 5.8 %all-to-all-start = ((bf16[8,72,512]{2,1,0:T(8,128)(2,1)}), bf16[8,72,512]{2,1,0:T(8,128)(2,1)}, u32[]{:S(2)}, u32[]{:S(2)}) async-start(bf16[8,72,512]{2,1,0:T(8,128)(2,1)} %copy-done.1), calls=%async_computation | async-start | bytes 1179648 | tf_op jit(solution)/shard_map/all_to_all | solution.py:430
  22.6 0.5 collective-permute-start.11
  23.9 1.0 %collective-permute-start.15 = (bf16[64,2048]{1,0:T(8,128)(2,1)S(1)}, bf16[64,2048]{1,0:T(8,128)(2,1)S(1)}, u32[]{:S(2)}, u32[]{:S(2)}) collective-permute-start(bf16[64,2048]{1,0:T(8,128)(2,1)S(1)} %copy-done.7), channel_id=1, source_target_pairs={{0,16},{8,24},{16,0},{24,8},{1,17},{9,25},{17,1},{25,9},{2,18},{10... | collective-permute-start | bytes 786440 | tf_op jit(solution)/shard_map/ppermute | solution.py:390
  24.9 0.9 %gram_cross.3 = (bf16[256,256]{1,0:T(8,128)(2,1)S(1)}, bf16[264,256]{1,0:T(8,128)(2,1)S(1)}, bf16[8,256]{1,0:T(8,128)(2,1)S(1)}) custom-call(bf16[544,2048]{1,0:T(8,128)(2,1)S(1)} %get-tuple-element.48.left_ref, f32[544,128]{1,0:T(8,128)S(1)} %get-tuple-element.49.refs_1_.total_ref, bf16[128,2048]{1,0:T(8,128)(2,1)S(1)} %hold.5.refs_0_, ...), custom_call_target="tpu_custom_call" | custom-call | bytes 262144 | tf_op jit(solution)/shard_map/gram_cross/pallas_call | solution.py:26
  25.8 1.9 %collective-permute-done.16.refs_0_ = bf16[64,2048]{1,0:T(8,128)(2,1)} collective-permute-done((bf16[64,2048]{1,0:T(8,128)(2,1)}, bf16[64,2048]{1,0:T(8,128)(2,1)}, u32[]{:S(2)}, u32[]{:S(2)}) %collective-permute-start.16) | collective-permute-done | bytes 262176 | tf_op jit(solution)/shard_map/ppermute | solution.py:390
  27.6 0.9 %slice.46 = bf16[48,2048]{1,0:T(8,128)(2,1)S(1)} slice(bf16[64,2048]{1,0:T(8,128)(2,1)} %hold.6.refs_0_), slice={[0:48], [0:2048]} | slice | bytes 393216 | tf_op jit(solution)/shard_map/slice | solution.py:395
  28.7 0.8 %slice.47 = bf16[16,2048]{1,0:T(8,128)(2,1)S(1)} slice(bf16[64,2048]{1,0:T(8,128)(2,1)} %hold.6.refs_0_), slice={[48:64], [0:2048]} | slice | bytes 131072 | tf_op jit(solution)/shard_map/slice | solution.py:395
  30.0 0.9 %collective-permute-done.18.refs_2_ = bf16[16,2048]{1,0:T(8,128)(2,1)S(1)} collective-permute-done((bf16[16,2048]{1,0:T(8,128)(2,1)S(1)}, bf16[16,2048]{1,0:T(8,128)(2,1)S(1)}, u32[]{:S(2)}, u32[]{:S(2)}) %collective-permute-start.18) | collective-permute-done | bytes 65568 | tf_op jit(solution)/shard_map/ppermute | solution.py:390
  30.9 1.7 %gram_cross.4 = (bf16[256,256]{1,0:T(8,128)(2,1)S(1)}, bf16[264,256]{1,0:T(8,128)(2,1)S(1)}, bf16[8,256]{1,0:T(8,128)(2,1)S(1)}) custom-call(bf16[544,2048]{1,0:T(8,128)(2,1)S(1)} %get-tuple-element.48.left_ref, f32[544,128]{1,0:T(8,128)S(1)} %get-tuple-element.49.refs_1_.total_ref, bf16[64,2048]{1,0:T(8,128)(2,1)} %hold.6.refs_0_, ...), custom_call_target="tpu_custom_call" | custom-call | bytes 262144 | tf_op jit(solution)/shard_map/gram_cross/pallas_call | solution.py:26
  33.1 1.2 %collective-permute-start.12 = (bf16[264,256]{1,0:T(8,128)(2,1)S(1)}, bf16[264,256]{1,0:T(8,128)(2,1)S(1)}, u32[]{:S(2)}, u32[]{:S(2)}) collective-permute-start(bf16[264,256]{1,0:T(8,128)(2,1)S(1)} %get-tuple-element.51), channel_id=1, source_target_pairs={{0,1},{1,0},{2,3},{3,2},{4,5},{5,4},{6,7},{7,6},{8,9},{9,8},{10,11... | collective-permute-start | bytes 405512 | tf_op jit(solution)/shard_map/ppermute | solution.py:390
  34.3 0.8 %gram_cross.5 = (bf16[256,256]{1,0:T(8,128)(2,1)S(1)}, bf16[264,256]{1,0:T(8,128)(2,1)S(1)}, bf16[8,256]{1,0:T(8,128)(2,1)S(1)}) custom-call(bf16[544,2048]{1,0:T(8,128)(2,1)S(1)} %get-tuple-element.48.left_ref, f32[544,128]{1,0:T(8,128)S(1)} %get-tuple-element.49.refs_1_.total_ref, ...), custom_call_target="tpu_custom_call", output_to_operand_aliasing={{0}: (4, {}), {1}: (5, {}), {2}: (6, {})} | custom-call | bytes 262144 | tf_op jit(solution)/shard_map/gram_cross/pallas_call | solution.py:26
  35.1 1.7 %collective-permute-start.20 = (bf16[264,256]{1,0:T(8,128)(2,1)S(1)}, bf16[264,256]{1,0:T(8,128)(2,1)S(1)}, u32[]{:S(2)}, u32[]{:S(2)}) collective-permute-start(bf16[264,256]{1,0:T(8,128)(2,1)S(1)} %get-tuple-element.65), channel_id=1, source_target_pairs={{0,2},{1,3},{2,0},{3,1},{4,6},{5,7},{6,4},{7,5},{8,10},{9,11},{10,... | collective-permute-start | bytes 405512 | tf_op jit(solution)/shard_map/ppermute | solution.py:390
  36.7 2.4 %collective-permute-done.12.got_ref = bf16[264,256]{1,0:T(8,128)(2,1)S(1)} collective-permute-done((bf16[264,256]{1,0:T(8,128)(2,1)S(1)}, bf16[264,256]{1,0:T(8,128)(2,1)S(1)}, u32[]{:S(2)}, u32[]{:S(2)}) %collective-permute-start.12) | collective-permute-done | bytes 135200 | tf_op jit(solution)/shard_map/ppermute | solution.py:390
  39.2 2.0 %collective-permute-start.13 = (bf16[144,256]{1,0:T(8,128)(2,1)S(1)}, bf16[144,256]{1,0:T(8,128)(2,1)S(1)}, u32[]{:S(2)}, u32[]{:S(2)}) collective-permute-start(bf16[144,256]{1,0:T(8,128)(2,1)S(1)} %get-tuple-element.54), channel_id=1, source_target_pairs={{0,2},{1,3},{2,0},{3,1},{4,6},{5,7},{6,4},{7,5},{8,10},{9,11},{10,... | collective-permute-start | bytes 221192 | tf_op jit(solution)/shard_map/ppermute | solution.py:390
  41.6 1.5 %collective-permute-start.21 = (bf16[144,256]{1,0:T(8,128)(2,1)S(1)}, bf16[144,256]{1,0:T(8,128)(2,1)S(1)}, u32[]{:S(2)}, u32[]{:S(2)}) collective-permute-start(bf16[144,256]{1,0:T(8,128)(2,1)S(1)} %get-tuple-element.68), channel_id=1, source_target_pairs={{0,1},{1,0},{2,3},{3,2},{4,5},{5,4},{6,7},{7,6},{8,9},{9,8},{10,11... | collective-permute-start | bytes 221192 | tf_op jit(solution)/shard_map/ppermute | solution.py:390
  43.1 0.5 %collective-permute-done.13.got_ref = bf16[144,256]{1,0:T(8,128)(2,1)S(1)} collective-permute-done((bf16[144,256]{1,0:T(8,128)(2,1)S(1)}, bf16[144,256]{1,0:T(8,128)(2,1)S(1)}, u32[]{:S(2)}, u32[]{:S(2)}) %collective-permute-start.13) | collective-permute-done | bytes 73760 | tf_op jit(solution)/shard_map/ppermute | solution.py:390
  43.7 2.3 %collective-permute-start.14 = (bf16[96,256]{1,0:T(8,128)(2,1)S(1)}, bf16[96,256]{1,0:T(8,128)(2,1)S(1)}, u32[]{:S(2)}, u32[]{:S(2)}) collective-permute-start(bf16[96,256]{1,0:T(8,128)(2,1)S(1)} %get-tuple-element.57), channel_id=1, source_target_pairs={{0,4},{1,5},{2,6},{3,7},{4,0},{5,1},{6,2},{7,3},{8,12},{9,13},{10,... | collective-permute-start | bytes 147464 | tf_op jit(solution)/shard_map/ppermute | solution.py:390
  46.0 2.0 %collective-permute-start.22 = (bf16[96,256]{1,0:T(8,128)(2,1)S(1)}, bf16[96,256]{1,0:T(8,128)(2,1)S(1)}, u32[]{:S(2)}, u32[]{:S(2)}) collective-permute-start(bf16[96,256]{1,0:T(8,128)(2,1)S(1)} %get-tuple-element.71), channel_id=1, source_target_pairs={{0,4},{1,5},{2,6},{3,7},{4,0},{5,1},{6,2},{7,3},{8,12},{9,13},{10,... | collective-permute-start | bytes 147464 | tf_op jit(solution)/shard_map/ppermute | solution.py:390
  48.0 1.7 %own_part.1 = (f32[64,512]{1,0:T(8,128)S(1)}, f32[64,64]{1,0:T(8,128)S(1)}, f32[144,128]{1,0:T(8,128)S(1)}) custom-call(bf16[8,72,512]{2,1,0:T(8,128)(2,1)} %all-to-all-done.got_ref), custom_call_target="tpu_custom_call" | custom-call | bytes 262144 | tf_op jit(solution)/shard_map/own_part/pallas_call | solution.py:26
  49.7 1.3 %collective-permute-done.22.refs_4_ = bf16[96,256]{1,0:T(8,128)(2,1)S(1)} collective-permute-done((bf16[96,256]{1,0:T(8,128)(2,1)S(1)}, bf16[96,256]{1,0:T(8,128)(2,1)S(1)}, u32[]{:S(2)}, u32[]{:S(2)}) %collective-permute-start.22) | collective-permute-done | bytes 49184 | tf_op jit(solution)/shard_map/ppermute | solution.py:390
  51.1 1.2 %finish.1 = f32[32,2,1024]{2,1,0:T(2,128)} custom-call(f32[64,512]{1,0:T(8,128)S(1)} %get-tuple-element.45.own_ref, f32[64,64]{1,0:T(8,128)S(1)} %get-tuple-element.46.side_ref, f32[144,128]{1,0:T(8,128)S(1)} %get-tuple-element.47.share_ref, bf16[64,256]{1,0:T(8,128)(2,1)S(1)} %get-tuple-element.56.refs_0_, ...), custom_call_target="tpu_custom_call" | custom-call | bytes 262144 | tf_op jit(solution)/shard_map/finish/pallas_call | solution.py:26
  (54 shorter events, 4.1 us)
Async XLA Ops:
  0.0 1.2 %copy-start = (bf16[256,2048]{1,0:T(8,128)(2,1)S(1)}, bf16[256,2048]{1,0:T(8,128)(2,1)}, u32[]{:S(2)}) copy-start(bf16[256,2048]{1,0:T(8,128)(2,1)} %frames_ref.3) | copy-start | bytes 3145732
  1.2 5.7 %collective-permute-start = (bf16[16,2048]{1,0:T(8,128)(2,1)S(1)}, bf16[16,2048]{1,0:T(8,128)(2,1)S(1)}, u32[]{:S(2)}, u32[]{:S(2)}) collective-permute-start(bf16[16,2048]{1,0:T(8,128)(2,1)S(1)} %get-tuple-element.40), channel_id=1, source_target_pairs={{0,16},{8,24},{16,0},{24,8},{1,17},{9,25},{17,1},{25,9},{2,18},{10... | collective-permute-start | bytes 196616 | tf_op jit(solution)/shard_map/ppermute | solution.py:390
  4.2 4.9 %collective-permute-start.1 = (bf16[16,2048]{1,0:T(8,128)(2,1)S(1)}, bf16[16,2048]{1,0:T(8,128)(2,1)S(1)}, u32[]{:S(2)}, u32[]{:S(2)}) collective-permute-start(bf16[16,2048]{1,0:T(8,128)(2,1)S(1)} %get-tuple-element.42), channel_id=1, source_target_pairs={{0,8},{8,0},{16,24},{24,16},{1,9},{9,1},{17,25},{25,17},{2,10},{10... | collective-permute-start | bytes 196616 | tf_op jit(solution)/shard_map/ppermute | solution.py:390
  4.3 0.7 %copy-start.2 = (f32[2048]{0:T(1024)S(1)}, f32[2048]{0:T(1024)}, u32[]{:S(2)}) copy-start(f32[2048]{0:T(1024)} %dead_ref.3) | copy-start | bytes 24580
  5.0 0.7 %copy-start.3 = (s32[2048]{0:T(1024)S(1)}, s32[2048]{0:T(1024)}, u32[]{:S(2)}) copy-start(s32[2048]{0:T(1024)} %width_ref.3) | copy-start | bytes 24580
  6.9 6.5 %copy-start.4 = (s32[2048]{0:T(1024)S(1)}, s32[2048]{0:T(1024)}, u32[]{:S(2)}) copy-start(s32[2048]{0:T(1024)} %label_ref.1) | copy-start | bytes 24580
  7.0 6.5 %copy-start.5 = (s32[2048]{0:T(1024)S(1)}, s32[2048]{0:T(1024)}, u32[]{:S(2)}) copy-start(s32[2048]{0:T(1024)} %valid_ref.1) | copy-start | bytes 24580
  7.0 2.2 %collective-permute-start.2 = (bf16[16,2048]{1,0:T(8,128)(2,1)S(1)}, bf16[16,2048]{1,0:T(8,128)(2,1)S(1)}, u32[]{:S(2)}, u32[]{:S(2)}) collective-permute-start(bf16[16,2048]{1,0:T(8,128)(2,1)S(1)} %collective-permute-done.refs_1_), channel_id=1, source_target_pairs={{0,8},{8,0},{16,24},{24,16},{1,9},{9,1},{17,25},{25,17},{2,10},{10... | collective-permute-start | bytes 196616 | tf_op jit(solution)/shard_map/ppermute | solution.py:390
  7.6 14.9 %collective-permute-start.7 = (bf16[128,2048]{1,0:T(8,128)(2,1)S(1)}, bf16[128,2048]{1,0:T(8,128)(2,1)S(1)}, u32[]{:S(2)}, u32[]{:S(2)}) collective-permute-start(bf16[128,2048]{1,0:T(8,128)(2,1)S(1)} %hold.4.mid_ref), channel_id=1, source_target_pairs={{0,16},{8,24},{16,0},{24,8},{1,17},{9,25},{17,1},{25,9},{2,18},{10... | collective-permute-start | bytes 1572872 | tf_op jit(solution)/shard_map/ppermute | solution.py:390
  8.6 3.4 %collective-permute-start.3 = (bf16[64,2048]{1,0:T(8,128)(2,1)S(1)}, bf16[64,2048]{1,0:T(8,128)(2,1)S(1)}, u32[]{:S(2)}, u32[]{:S(2)}) collective-permute-start(bf16[64,2048]{1,0:T(8,128)(2,1)S(1)} %get-tuple-element.80), channel_id=1, source_target_pairs={{0,8},{8,0},{16,24},{24,16},{1,9},{9,1},{17,25},{25,17},{2,10},{10... | collective-permute-start | bytes 786440 | tf_op jit(solution)/shard_map/ppermute | solution.py:390
  8.9 4.3 %collective-permute-start.4 = (bf16[64,2048]{1,0:T(8,128)(2,1)S(1)}, bf16[64,2048]{1,0:T(8,128)(2,1)S(1)}, u32[]{:S(2)}, u32[]{:S(2)}) collective-permute-start(bf16[64,2048]{1,0:T(8,128)(2,1)S(1)} %get-tuple-element.79), channel_id=1, source_target_pairs={{0,8},{8,0},{16,24},{24,16},{1,9},{9,1},{17,25},{25,17},{2,10},{10... | collective-permute-start | bytes 786440 | tf_op jit(solution)/shard_map/ppermute | solution.py:390
  11.4 1.7 %copy-start.6 = (bf16[64,2048]{1,0:T(8,128)(2,1)}, bf16[64,2048]{1,0:T(8,128)(2,1)S(1)}, u32[]{:S(2)}) copy-start(bf16[64,2048]{1,0:T(8,128)(2,1)S(1)} %get-tuple-element.59) | copy-start | bytes 786436
  11.5 1.6 %collective-permute-start.5 = (bf16[64,2048]{1,0:T(8,128)(2,1)S(1)}, bf16[64,2048]{1,0:T(8,128)(2,1)S(1)}, u32[]{:S(2)}, u32[]{:S(2)}) collective-permute-start(bf16[64,2048]{1,0:T(8,128)(2,1)S(1)} %get-tuple-element.78), channel_id=1, source_target_pairs={{0,8},{8,0},{16,24},{24,16},{1,9},{9,1},{17,25},{25,17},{2,10},{10... | collective-permute-start | bytes 786440 | tf_op jit(solution)/shard_map/ppermute | solution.py:390
  11.8 1.7 %collective-permute-start.6 = (bf16[64,2048]{1,0:T(8,128)(2,1)S(1)}, bf16[64,2048]{1,0:T(8,128)(2,1)S(1)}, u32[]{:S(2)}, u32[]{:S(2)}) collective-permute-start(bf16[64,2048]{1,0:T(8,128)(2,1)S(1)} %get-tuple-element.77), channel_id=1, source_target_pairs={{0,8},{8,0},{16,24},{24,16},{1,9},{9,1},{17,25},{25,17},{2,10},{10... | collective-permute-start | bytes 786440 | tf_op jit(solution)/shard_map/ppermute | solution.py:390
  12.1 15.6 %collective-permute-start.16 = (bf16[64,2048]{1,0:T(8,128)(2,1)}, bf16[64,2048]{1,0:T(8,128)(2,1)}, u32[]{:S(2)}, u32[]{:S(2)}) collective-permute-start(bf16[64,2048]{1,0:T(8,128)(2,1)} %get-tuple-element.60), channel_id=1, source_target_pairs={{0,16},{8,24},{16,0},{24,8},{1,17},{9,25},{17,1},{25,9},{2,18},{10... | collective-permute-start | bytes 786440 | tf_op jit(solution)/shard_map/ppermute | solution.py:390
  15.7 0.8 %copy-start.1 = (bf16[8,72,512]{2,1,0:T(8,128)(2,1)}, bf16[8,72,512]{2,1,0:T(8,128)(2,1)S(1)}, u32[]{:S(2)}) copy-start(bf16[8,72,512]{2,1,0:T(8,128)(2,1)S(1)} %get-tuple-element.44) | copy-start | bytes 1769476
  16.5 31.5 %all-to-all-start = ((bf16[8,72,512]{2,1,0:T(8,128)(2,1)}), bf16[8,72,512]{2,1,0:T(8,128)(2,1)}, u32[]{:S(2)}, u32[]{:S(2)}) async-start(bf16[8,72,512]{2,1,0:T(8,128)(2,1)} %copy-done.1), calls=%async_computation | async-start | bytes 1179648 | tf_op jit(solution)/shard_map/all_to_all | solution.py:430
  22.3 1.6 %copy-start.7 = (bf16[64,2048]{1,0:T(8,128)(2,1)S(1)}, bf16[64,2048]{1,0:T(8,128)(2,1)}, u32[]{:S(2)}) copy-start(bf16[64,2048]{1,0:T(8,128)(2,1)} %copy-done.6) | copy-start | bytes 786436
  22.5 1.4 %collective-permute-start.10 = (bf16[32,2048]{1,0:T(8,128)(2,1)S(1)}, bf16[32,2048]{1,0:T(8,128)(2,1)S(1)}, u32[]{:S(2)}, u32[]{:S(2)}) collective-permute-start(bf16[32,2048]{1,0:T(8,128)(2,1)S(1)} %get-tuple-element.74), channel_id=1, source_target_pairs={{0,8},{8,0},{16,24},{24,16},{1,9},{9,1},{17,25},{25,17},{2,10},{10... | collective-permute-start | bytes 393224 | tf_op jit(solution)/shard_map/ppermute | solution.py:390
  22.6 2.3 %collective-permute-start.11 = (bf16[32,2048]{1,0:T(8,128)(2,1)S(1)}, bf16[32,2048]{1,0:T(8,128)(2,1)S(1)}, u32[]{:S(2)}, u32[]{:S(2)}) collective-permute-start(bf16[32,2048]{1,0:T(8,128)(2,1)S(1)} %get-tuple-element.73), channel_id=1, source_target_pairs={{0,8},{8,0},{16,24},{24,16},{1,9},{9,1},{17,25},{25,17},{2,10},{10... | collective-permute-start | bytes 393224 | tf_op jit(solution)/shard_map/ppermute | solution.py:390
  23.1 1.8 %collective-permute-start.8 = (bf16[32,2048]{1,0:T(8,128)(2,1)S(1)}, bf16[32,2048]{1,0:T(8,128)(2,1)S(1)}, u32[]{:S(2)}, u32[]{:S(2)}) collective-permute-start(bf16[32,2048]{1,0:T(8,128)(2,1)S(1)} %get-tuple-element.76), channel_id=1, source_target_pairs={{0,8},{8,0},{16,24},{24,16},{1,9},{9,1},{17,25},{25,17},{2,10},{10... | collective-permute-start | bytes 393224 | tf_op jit(solution)/shard_map/ppermute | solution.py:390
  23.1 1.8 %collective-permute-start.9 = (bf16[32,2048]{1,0:T(8,128)(2,1)S(1)}, bf16[32,2048]{1,0:T(8,128)(2,1)S(1)}, u32[]{:S(2)}, u32[]{:S(2)}) collective-permute-start(bf16[32,2048]{1,0:T(8,128)(2,1)S(1)} %get-tuple-element.75), channel_id=1, source_target_pairs={{0,8},{8,0},{16,24},{24,16},{1,9},{9,1},{17,25},{25,17},{2,10},{10... | collective-permute-start | bytes 393224 | tf_op jit(solution)/shard_map/ppermute | solution.py:390
  23.9 8.8 %collective-permute-start.15 = (bf16[64,2048]{1,0:T(8,128)(2,1)S(1)}, bf16[64,2048]{1,0:T(8,128)(2,1)S(1)}, u32[]{:S(2)}, u32[]{:S(2)}) collective-permute-start(bf16[64,2048]{1,0:T(8,128)(2,1)S(1)} %copy-done.7), channel_id=1, source_target_pairs={{0,16},{8,24},{16,0},{24,8},{1,17},{9,25},{17,1},{25,9},{2,18},{10... | collective-permute-start | bytes 786440 | tf_op jit(solution)/shard_map/ppermute | solution.py:390
  28.6 2.3 %collective-permute-start.17 = (bf16[48,2048]{1,0:T(8,128)(2,1)S(1)}, bf16[48,2048]{1,0:T(8,128)(2,1)S(1)}, u32[]{:S(2)}, u32[]{:S(2)}) collective-permute-start(bf16[48,2048]{1,0:T(8,128)(2,1)S(1)} %slice.46), channel_id=1, source_target_pairs={{0,8},{8,0},{16,24},{24,16},{1,9},{9,1},{17,25},{25,17},{2,10},{10... | collective-permute-start | bytes 589832 | tf_op jit(solution)/shard_map/ppermute | solution.py:390
  29.5 1.4 %collective-permute-start.18 = (bf16[16,2048]{1,0:T(8,128)(2,1)S(1)}, bf16[16,2048]{1,0:T(8,128)(2,1)S(1)}, u32[]{:S(2)}, u32[]{:S(2)}) collective-permute-start(bf16[16,2048]{1,0:T(8,128)(2,1)S(1)} %slice.47), channel_id=1, source_target_pairs={{0,8},{8,0},{16,24},{24,16},{1,9},{9,1},{17,25},{25,17},{2,10},{10... | collective-permute-start | bytes 196616 | tf_op jit(solution)/shard_map/ppermute | solution.py:390
  32.7 1.5 %collective-permute-start.19 = (bf16[64,2048]{1,0:T(8,128)(2,1)S(1)}, bf16[64,2048]{1,0:T(8,128)(2,1)S(1)}, u32[]{:S(2)}, u32[]{:S(2)}) collective-permute-start(bf16[64,2048]{1,0:T(8,128)(2,1)S(1)} %hold.7.refs_0_), channel_id=1, source_target_pairs={{0,8},{8,0},{16,24},{24,16},{1,9},{9,1},{17,25},{25,17},{2,10},{10... | collective-permute-start | bytes 786440 | tf_op jit(solution)/shard_map/ppermute | solution.py:390
  33.1 6.1 %collective-permute-start.12 = (bf16[264,256]{1,0:T(8,128)(2,1)S(1)}, bf16[264,256]{1,0:T(8,128)(2,1)S(1)}, u32[]{:S(2)}, u32[]{:S(2)}) collective-permute-start(bf16[264,256]{1,0:T(8,128)(2,1)S(1)} %get-tuple-element.51), channel_id=1, source_target_pairs={{0,1},{1,0},{2,3},{3,2},{4,5},{5,4},{6,7},{7,6},{8,9},{9,8},{10,11... | collective-permute-start | bytes 405512 | tf_op jit(solution)/shard_map/ppermute | solution.py:390
  35.1 6.5 %collective-permute-start.20 = (bf16[264,256]{1,0:T(8,128)(2,1)S(1)}, bf16[264,256]{1,0:T(8,128)(2,1)S(1)}, u32[]{:S(2)}, u32[]{:S(2)}) collective-permute-start(bf16[264,256]{1,0:T(8,128)(2,1)S(1)} %get-tuple-element.65), channel_id=1, source_target_pairs={{0,2},{1,3},{2,0},{3,1},{4,6},{5,7},{6,4},{7,5},{8,10},{9,11},{10,... | collective-permute-start | bytes 405512 | tf_op jit(solution)/shard_map/ppermute | solution.py:390
  39.2 4.4 %collective-permute-start.13 = (bf16[144,256]{1,0:T(8,128)(2,1)S(1)}, bf16[144,256]{1,0:T(8,128)(2,1)S(1)}, u32[]{:S(2)}, u32[]{:S(2)}) collective-permute-start(bf16[144,256]{1,0:T(8,128)(2,1)S(1)} %get-tuple-element.54), channel_id=1, source_target_pairs={{0,2},{1,3},{2,0},{3,1},{4,6},{5,7},{6,4},{7,5},{8,10},{9,11},{10,... | collective-permute-start | bytes 221192 | tf_op jit(solution)/shard_map/ppermute | solution.py:390
  41.6 4.4 %collective-permute-start.21 = (bf16[144,256]{1,0:T(8,128)(2,1)S(1)}, bf16[144,256]{1,0:T(8,128)(2,1)S(1)}, u32[]{:S(2)}, u32[]{:S(2)}) collective-permute-start(bf16[144,256]{1,0:T(8,128)(2,1)S(1)} %get-tuple-element.68), channel_id=1, source_target_pairs={{0,1},{1,0},{2,3},{3,2},{4,5},{5,4},{6,7},{7,6},{8,9},{9,8},{10,11... | collective-permute-start | bytes 221192 | tf_op jit(solution)/shard_map/ppermute | solution.py:390
  43.7 6.1 %collective-permute-start.14 = (bf16[96,256]{1,0:T(8,128)(2,1)S(1)}, bf16[96,256]{1,0:T(8,128)(2,1)S(1)}, u32[]{:S(2)}, u32[]{:S(2)}) collective-permute-start(bf16[96,256]{1,0:T(8,128)(2,1)S(1)} %get-tuple-element.57), channel_id=1, source_target_pairs={{0,4},{1,5},{2,6},{3,7},{4,0},{5,1},{6,2},{7,3},{8,12},{9,13},{10,... | collective-permute-start | bytes 147464 | tf_op jit(solution)/shard_map/ppermute | solution.py:390
  46.0 5.1 %collective-permute-start.22 = (bf16[96,256]{1,0:T(8,128)(2,1)S(1)}, bf16[96,256]{1,0:T(8,128)(2,1)S(1)}, u32[]{:S(2)}, u32[]{:S(2)}) collective-permute-start(bf16[96,256]{1,0:T(8,128)(2,1)S(1)} %get-tuple-element.71), channel_id=1, source_target_pairs={{0,4},{1,5},{2,6},{3,7},{4,0},{5,1},{6,2},{7,3},{8,12},{9,13},{10,... | collective-permute-start | bytes 147464 | tf_op jit(solution)/shard_map/ppermute | solution.py:390

commit v5 on v4

--- a/solution.py
+++ b/solution.py
@@ -12,6 +12,7 @@
 EDGE_PART = 4
 FORWARDS = ((4, 8, 12), (12,), ())
 STAT = 8
+SENT = 4
 STAT_ROWS = 8
 LANE = 128
 f32 = jnp.float32
@@ -189,11 +190,9 @@
 
 def stat_rows(mean, count=None):
     width = mean[0].shape[1]
-    rows = [piece for m in zip(*[split(m, 3) for m in mean]) for piece in m]
+    rows = [piece for m in zip(*[split(m, 2 if count is None else 3) for m in mean]) for piece in m]
     zero = jnp.zeros((1, width), f32)
-    if count is None:
-        rows += [zero] * 2
-    else:
+    if count is not None:
         lane = lax.broadcasted_iota(jnp.int32, (1, width), 1) // (LANE // 2)
         for part in zip(*[split(c, 2) for c in count]):
             rows.append(sum(jnp.where(lane == q, p, 0.0) for q, p in enumerate(part)))
@@ -276,7 +275,7 @@
 def join_stats(mine_ref, got_ref, groups):
     mine = mine_ref[...].astype(f32)
     got = got_ref[pl.ds(got_ref.shape[0] - mine.shape[0], mine.shape[0]), :].astype(f32)
-    return jnp.concatenate([mine[: groups * STAT], got[: groups * STAT]], axis=0)
+    return jnp.concatenate([mine[: groups * SENT], got[: groups * SENT]], axis=0)
 
 
 def merge_kernel(keep_ref, got_ref, stat_ref, next_keep_ref, next_send_ref, next_stat_ref, *, groups):
@@ -290,7 +289,7 @@
 
 
 def merge(keep, got, stat, groups):
-    outs = part_outs(keep.shape[0] // 2, keep.shape[1], 2 * groups * STAT)
+    outs = part_outs(keep.shape[0] // 2, keep.shape[1], 2 * groups * SENT)
     return kernel_call(functools.partial(merge_kernel, groups=groups), "merge", (keep, got, stat), outs)
 
 
@@ -346,9 +345,11 @@
 def part_sums(keep_ref, got_ref, stat_ref, side_ref, share_ref, bits):
     stats = join_stats(stat_ref, got_ref, 2 ** len(bits) // 2)
     spots = [sum((group >> bit & 1) << level for level, bit in enumerate(bits)) for group in range(2 ** len(bits))]
-    stats = jnp.concatenate([stats[STAT * spot : STAT * (spot + 1)] for spot in spots], axis=0)
+    stats = stats + pltpu.roll(stats, stats.shape[0] - CYCLES, 0)
+    zero = jnp.zeros((STAT - SENT, stats.shape[1]), f32)
+    stats = jnp.concatenate([x for spot in spots for x in (stats[SENT * spot : SENT * (spot + 1)], zero)], axis=0)
     entries = stats.shape[0]
-    mean = whole_means(stats)
+    mean = stats
     size = keep_ref.shape[0] // CYCLES
     return [
         part_sum(
@@ -416,7 +417,7 @@
     mid = hold(mid, halo)
     far_mid = {j: swap(mid, "frame", j) for j in range(2, nblocks, 2)}
     near_halo = swap(near_halo, "frame", 1)
-    halo = swap(halo, "frame", 1)
+    halo = swap(hold(halo, mid), "frame", 1)
     near = swap_pieces(mid, 8)
     edge, top, bottom = smooth_edges(rim, near_halo, halo, dead_time, band_width, nframes)
     far_ends = {j: [swap(x, "frame", j) for x in (top, bottom)] for j in range(2, nblocks, 2)}

time: 52.7 us -> 52.6 us (level)
  no operation moved by 1% of the time
where the time goes in v5:
time: 52.6 us; the launch traced here: 52.1 us
  starting transfers between devices  26.2 us (50%)
  Pallas kernels  12.2 us (23%)
  waiting for transfers between devices  8.16 us (16%)
  local copies, waits for them, and re-layouts  5.37 us (10%)
    ppermute x23, starting transfers between devices, swap(): lax.ppermute(x, axis, [(i, i ^ bit) for i in range(lax.axis_size(axis))])  20.4 us
    pallas_call x13, Pallas kernels, kernel_call(): pl.pallas_call(body, in_specs=in_specs or [vmem] * len(args), out_specs=[...  12.2 us
    ppermute x23, waiting for transfers between devices, swap(): lax.ppermute(x, axis, [(i, i ^ bit) for i in range(lax.axis_size(axis))])  8.16 us
    all_to_all x1, starting transfers between devices, shards(): lax.all_to_all(own, 'pixel', 0, 0, tiled=True)  5.84 us
    unnamed x16, local copies, waits for them, and re-layouts  3.47 us
    slice x5, local copies, waits for them, and re-layouts, swap_pieces(): return [swap(x[i:j], 'frame', 1) for i, j in zip(at, at[1:])]  1.9 us
  transfers between devices with their start and end apart: 24, of which 10 were waited for; matrix products, arithmetic and copies ran while one was open for 4% of the time, Pallas kernels for 21%

profile of v5, /device:TPU:0, one launch (start us, length us, event | category | flops | bytes accessed | tf_op | source)
XLA Modules:
  0.0 52.1 jit_solution(3869629032251693501)
XLA Ops:
  0.0 1.2 %copy-done = bf16[256,2048]{1,0:T(8,128)(2,1)S(1)} copy-done((bf16[256,2048]{1,0:T(8,128)(2,1)S(1)}, bf16[256,2048]{1,0:T(8,128)(2,1)}, u32[]{:S(2)}) %copy-start) | copy-done | bytes 1048600
  1.2 3.0 %collective-permute-start = (bf16[16,2048]{1,0:T(8,128)(2,1)S(1)}, bf16[16,2048]{1,0:T(8,128)(2,1)S(1)}, u32[]{:S(2)}, u32[]{:S(2)}) collective-permute-start(bf16[16,2048]{1,0:T(8,128)(2,1)S(1)} %get-tuple-element.40), channel_id=1, source_target_pairs={{0,16},{8,24},{16,0},{24,8},{1,17},{9,25},{17,1},{25,9},{2,18},{10... | collective-permute-start | bytes 196616 | tf_op jit(solution)/shard_map/ppermute | solution.py:391
  4.3 0.7 %copy-done.2 = f32[2048]{0:T(1024)S(1)} copy-done((f32[2048]{0:T(1024)S(1)}, f32[2048]{0:T(1024)}, u32[]{:S(2)}) %copy-start.2) | copy-done | bytes 8216
  5.0 0.7 %copy-done.3 = s32[2048]{0:T(1024)S(1)} copy-done((s32[2048]{0:T(1024)S(1)}, s32[2048]{0:T(1024)}, u32[]{:S(2)}) %copy-start.3) | copy-done | bytes 8216
  5.6 1.3 %smooth_middle.1 = (bf16[128,2048]{1,0:T(8,128)(2,1)S(1)}, bf16[160,2048]{1,0:T(8,128)(2,1)S(1)}) custom-call(bf16[256,2048]{1,0:T(8,128)(2,1)S(1)} %copy-done, f32[2048]{0:T(1024)S(1)} %copy-done.2, s32[2048]{0:T(1024)S(1)} %copy-done.3), custom_call_target="tpu_custom_call" | custom-call | bytes 262144 | tf_op jit(solution)/shard_map/smooth_middle/pallas_call | solution.py:27
  7.0 0.6 %collective-permute-start.2 = (bf16[16,2048]{1,0:T(8,128)(2,1)S(1)}, bf16[16,2048]{1,0:T(8,128)(2,1)S(1)}, u32[]{:S(2)}, u32[]{:S(2)}) collective-permute-start(bf16[16,2048]{1,0:T(8,128)(2,1)S(1)} %hold.6), channel_id=1, source_target_pairs={{0,8},{8,0},{16,24},{24,16},{1,9},{9,1},{17,25},{25,17},{2,10},{10... | collective-permute-start | bytes 196616 | tf_op jit(solution)/shard_map/ppermute | solution.py:391
  7.6 1.0 %collective-permute-start.7 = (bf16[128,2048]{1,0:T(8,128)(2,1)S(1)}, bf16[128,2048]{1,0:T(8,128)(2,1)S(1)}, u32[]{:S(2)}, u32[]{:S(2)}) collective-permute-start(bf16[128,2048]{1,0:T(8,128)(2,1)S(1)} %hold.5.refs_1_.mid_ref), channel_id=1, source_target_pairs={{0,16},{8,24},{16,0},{24,8},{1,17},{9,25},{17,1},{25,9},{2,18},{10... | collective-permute-start | bytes 1572872 | tf_op jit(solution)/shard_map/ppermute | solution.py:391
  9.2 2.3 %smooth_edges.1 = (bf16[128,2048]{1,0:T(8,128)(2,1)S(1)}, bf16[64,2048]{1,0:T(8,128)(2,1)}, bf16[64,2048]{1,0:T(8,128)(2,1)S(1)}) custom-call(bf16[160,2048]{1,0:T(8,128)(2,1)S(1)} %get-tuple-element.41.rim_ref, bf16[16,2048]{1,0:T(8,128)(2,1)S(1)} %collective-permute-done.1.near_ref, bf16[16,2048]{1,0:T(8,128)(2,1)S(1)} %collective-permute-done.2.far_ref, ...), custom_call_target="tpu_custom_call" | custom-call | bytes 262144 | tf_op jit(solution)/shard_map/smooth_edges/pallas_call | solution.py:27
  12.1 1.1 %collective-permute-start.16 = (bf16[64,2048]{1,0:T(8,128)(2,1)}, bf16[64,2048]{1,0:T(8,128)(2,1)}, u32[]{:S(2)}, u32[]{:S(2)}) collective-permute-start(bf16[64,2048]{1,0:T(8,128)(2,1)} %get-tuple-element.60), channel_id=1, source_target_pairs={{0,16},{8,24},{16,0},{24,8},{1,17},{9,25},{17,1},{25,9},{2,18},{10... | collective-permute-start | bytes 786440 | tf_op jit(solution)/shard_map/ppermute | solution.py:391
  13.5 2.2 %gram_own.1 = (bf16[8,72,512]{2,1,0:T(8,128)(2,1)S(1)}, bf16[544,2048]{1,0:T(8,128)(2,1)S(1)}, f32[544,128]{1,0:T(8,128)S(1)}) custom-call(s32[2048]{0:T(1024)S(1)} %copy-done.4, s32[2048]{0:T(1024)S(1)} %copy-done.5, bf16[128,2048]{1,0:T(8,128)(2,1)S(1)} %hold.5.refs_1_.mid_ref, bf16[128,2048]{1,0:T(8,128)(2,1)S(1)} %get-tuple-element.43.edge_ref, ...), custom_call_target="tpu_custom_call" | custom-call | bytes 262144 | tf_op jit(solution)/shard_map/gram_own/pallas_call | solution.py:27
  15.7 0.8 %copy-done.1 = bf16[8,72,512]{2,1,0:T(8,128)(2,1)} copy-done((bf16[8,72,512]{2,1,0:T(8,128)(2,1)}, bf16[8,72,512]{2,1,0:T(8,128)(2,1)S(1)}, u32[]{:S(2)}) %copy-start.1) | copy-done | bytes 589848
  16.5 5.8 %all-to-all-start = ((bf16[8,72,512]{2,1,0:T(8,128)(2,1)}), bf16[8,72,512]{2,1,0:T(8,128)(2,1)}, u32[]{:S(2)}, u32[]{:S(2)}) async-start(bf16[8,72,512]{2,1,0:T(8,128)(2,1)} %copy-done.1), calls=%async_computation | async-start | bytes 1179648 | tf_op jit(solution)/shard_map/all_to_all | solution.py:431
  22.6 0.5 collective-permute-start.11
  23.9 1.0 %collective-permute-start.15 = (bf16[64,2048]{1,0:T(8,128)(2,1)S(1)}, bf16[64,2048]{1,0:T(8,128)(2,1)S(1)}, u32[]{:S(2)}, u32[]{:S(2)}) collective-permute-start(bf16[64,2048]{1,0:T(8,128)(2,1)S(1)} %copy-done.7), channel_id=1, source_target_pairs={{0,16},{8,24},{16,0},{24,8},{1,17},{9,25},{17,1},{25,9},{2,18},{10... | collective-permute-start | bytes 786440 | tf_op jit(solution)/shard_map/ppermute | solution.py:391
  24.9 0.8 %gram_cross.3 = (bf16[256,256]{1,0:T(8,128)(2,1)S(1)}, bf16[264,256]{1,0:T(8,128)(2,1)S(1)}, bf16[8,256]{1,0:T(8,128)(2,1)S(1)}) custom-call(bf16[544,2048]{1,0:T(8,128)(2,1)S(1)} %get-tuple-element.48.left_ref, f32[544,128]{1,0:T(8,128)S(1)} %get-tuple-element.49.refs_1_.total_ref, bf16[128,2048]{1,0:T(8,128)(2,1)S(1)} %hold.7.refs_0_, ...), custom_call_target="tpu_custom_call" | custom-call | bytes 262144 | tf_op jit(solution)/shard_map/gram_cross/pallas_call | solution.py:27
  25.8 1.9 %collective-permute-done.16.refs_0_ = bf16[64,2048]{1,0:T(8,128)(2,1)} collective-permute-done((bf16[64,2048]{1,0:T(8,128)(2,1)}, bf16[64,2048]{1,0:T(8,128)(2,1)}, u32[]{:S(2)}, u32[]{:S(2)}) %collective-permute-start.16) | collective-permute-done | bytes 262176 | tf_op jit(solution)/shard_map/ppermute | solution.py:391
  27.6 0.9 %slice.46 = bf16[48,2048]{1,0:T(8,128)(2,1)S(1)} slice(bf16[64,2048]{1,0:T(8,128)(2,1)} %hold.8.refs_0_), slice={[0:48], [0:2048]} | slice | bytes 393216 | tf_op jit(solution)/shard_map/slice | solution.py:396
  28.7 0.8 %slice.47 = bf16[16,2048]{1,0:T(8,128)(2,1)S(1)} slice(bf16[64,2048]{1,0:T(8,128)(2,1)} %hold.8.refs_0_), slice={[48:64], [0:2048]} | slice | bytes 131072 | tf_op jit(solution)/shard_map/slice | solution.py:396
  30.0 0.9 %collective-permute-done.18.refs_2_ = bf16[16,2048]{1,0:T(8,128)(2,1)S(1)} collective-permute-done((bf16[16,2048]{1,0:T(8,128)(2,1)S(1)}, bf16[16,2048]{1,0:T(8,128)(2,1)S(1)}, u32[]{:S(2)}, u32[]{:S(2)}) %collective-permute-start.18) | collective-permute-done | bytes 65568 | tf_op jit(solution)/shard_map/ppermute | solution.py:391
  30.9 1.7 %gram_cross.4 = (bf16[256,256]{1,0:T(8,128)(2,1)S(1)}, bf16[264,256]{1,0:T(8,128)(2,1)S(1)}, bf16[8,256]{1,0:T(8,128)(2,1)S(1)}) custom-call(bf16[544,2048]{1,0:T(8,128)(2,1)S(1)} %get-tuple-element.48.left_ref, f32[544,128]{1,0:T(8,128)S(1)} %get-tuple-element.49.refs_1_.total_ref, bf16[64,2048]{1,0:T(8,128)(2,1)} %hold.8.refs_0_, ...), custom_call_target="tpu_custom_call" | custom-call | bytes 262144 | tf_op jit(solution)/shard_map/gram_cross/pallas_call | solution.py:27
  33.1 1.2 %collective-permute-start.12 = (bf16[264,256]{1,0:T(8,128)(2,1)S(1)}, bf16[264,256]{1,0:T(8,128)(2,1)S(1)}, u32[]{:S(2)}, u32[]{:S(2)}) collective-permute-start(bf16[264,256]{1,0:T(8,128)(2,1)S(1)} %get-tuple-element.51), channel_id=1, source_target_pairs={{0,1},{1,0},{2,3},{3,2},{4,5},{5,4},{6,7},{7,6},{8,9},{9,8},{10,11... | collective-permute-start | bytes 405512 | tf_op jit(solution)/shard_map/ppermute | solution.py:391
  34.3 0.8 %gram_cross.5 = (bf16[256,256]{1,0:T(8,128)(2,1)S(1)}, bf16[264,256]{1,0:T(8,128)(2,1)S(1)}, bf16[8,256]{1,0:T(8,128)(2,1)S(1)}) custom-call(bf16[544,2048]{1,0:T(8,128)(2,1)S(1)} %get-tuple-element.48.left_ref, f32[544,128]{1,0:T(8,128)S(1)} %get-tuple-element.49.refs_1_.total_ref, ...), custom_call_target="tpu_custom_call", output_to_operand_aliasing={{0}: (4, {}), {1}: (5, {}), {2}: (6, {})} | custom-call | bytes 262144 | tf_op jit(solution)/shard_map/gram_cross/pallas_call | solution.py:27
  35.1 1.7 %collective-permute-start.20 = (bf16[264,256]{1,0:T(8,128)(2,1)S(1)}, bf16[264,256]{1,0:T(8,128)(2,1)S(1)}, u32[]{:S(2)}, u32[]{:S(2)}) collective-permute-start(bf16[264,256]{1,0:T(8,128)(2,1)S(1)} %get-tuple-element.65), channel_id=1, source_target_pairs={{0,2},{1,3},{2,0},{3,1},{4,6},{5,7},{6,4},{7,5},{8,10},{9,11},{10,... | collective-permute-start | bytes 405512 | tf_op jit(solution)/shard_map/ppermute | solution.py:391
  36.7 2.4 %collective-permute-done.12.got_ref = bf16[264,256]{1,0:T(8,128)(2,1)S(1)} collective-permute-done((bf16[264,256]{1,0:T(8,128)(2,1)S(1)}, bf16[264,256]{1,0:T(8,128)(2,1)S(1)}, u32[]{:S(2)}, u32[]{:S(2)}) %collective-permute-start.12) | collective-permute-done | bytes 135200 | tf_op jit(solution)/shard_map/ppermute | solution.py:391
  39.2 2.0 %collective-permute-start.13 = (bf16[136,256]{1,0:T(8,128)(2,1)S(1)}, bf16[136,256]{1,0:T(8,128)(2,1)S(1)}, u32[]{:S(2)}, u32[]{:S(2)}) collective-permute-start(bf16[136,256]{1,0:T(8,128)(2,1)S(1)} %get-tuple-element.54), channel_id=1, source_target_pairs={{0,2},{1,3},{2,0},{3,1},{4,6},{5,7},{6,4},{7,5},{8,10},{9,11},{10,... | collective-permute-start | bytes 208904 | tf_op jit(solution)/shard_map/ppermute | solution.py:391
  41.6 1.5 %collective-permute-start.21 = (bf16[136,256]{1,0:T(8,128)(2,1)S(1)}, bf16[136,256]{1,0:T(8,128)(2,1)S(1)}, u32[]{:S(2)}, u32[]{:S(2)}) collective-permute-start(bf16[136,256]{1,0:T(8,128)(2,1)S(1)} %get-tuple-element.68), channel_id=1, source_target_pairs={{0,1},{1,0},{2,3},{3,2},{4,5},{5,4},{6,7},{7,6},{8,9},{9,8},{10,11... | collective-permute-start | bytes 208904 | tf_op jit(solution)/shard_map/ppermute | solution.py:391
  43.1 0.5 collective-permute-done.13.got_ref
  43.6 2.3 %collective-permute-start.14 = (bf16[80,256]{1,0:T(8,128)(2,1)S(1)}, bf16[80,256]{1,0:T(8,128)(2,1)S(1)}, u32[]{:S(2)}, u32[]{:S(2)}) collective-permute-start(bf16[80,256]{1,0:T(8,128)(2,1)S(1)} %get-tuple-element.57), channel_id=1, source_target_pairs={{0,4},{1,5},{2,6},{3,7},{4,0},{5,1},{6,2},{7,3},{8,12},{9,13},{10,... | collective-permute-start | bytes 122888 | tf_op jit(solution)/shard_map/ppermute | solution.py:391
  46.0 2.0 %collective-permute-start.22 = (bf16[80,256]{1,0:T(8,128)(2,1)S(1)}, bf16[80,256]{1,0:T(8,128)(2,1)S(1)}, u32[]{:S(2)}, u32[]{:S(2)}) collective-permute-start(bf16[80,256]{1,0:T(8,128)(2,1)S(1)} %get-tuple-element.71), channel_id=1, source_target_pairs={{0,4},{1,5},{2,6},{3,7},{4,0},{5,1},{6,2},{7,3},{8,12},{9,13},{10,... | collective-permute-start | bytes 122888 | tf_op jit(solution)/shard_map/ppermute | solution.py:391
  48.0 1.7 %own_part.1 = (f32[64,512]{1,0:T(8,128)S(1)}, f32[64,64]{1,0:T(8,128)S(1)}, f32[144,128]{1,0:T(8,128)S(1)}) custom-call(bf16[8,72,512]{2,1,0:T(8,128)(2,1)} %all-to-all-done.got_ref), custom_call_target="tpu_custom_call" | custom-call | bytes 262144 | tf_op jit(solution)/shard_map/own_part/pallas_call | solution.py:27
  49.7 1.2 %collective-permute-done.22.refs_4_ = bf16[80,256]{1,0:T(8,128)(2,1)S(1)} collective-permute-done((bf16[80,256]{1,0:T(8,128)(2,1)S(1)}, bf16[80,256]{1,0:T(8,128)(2,1)S(1)}, u32[]{:S(2)}, u32[]{:S(2)}) %collective-permute-start.22) | collective-permute-done | bytes 40992 | tf_op jit(solution)/shard_map/ppermute | solution.py:391
  50.9 1.2 %finish.1 = f32[32,2,1024]{2,1,0:T(2,128)} custom-call(f32[64,512]{1,0:T(8,128)S(1)} %get-tuple-element.45.own_ref, f32[64,64]{1,0:T(8,128)S(1)} %get-tuple-element.46.side_ref, f32[144,128]{1,0:T(8,128)S(1)} %get-tuple-element.47.share_ref, bf16[64,256]{1,0:T(8,128)(2,1)S(1)} %get-tuple-element.56.refs_0_, ...), custom_call_target="tpu_custom_call" | custom-call | bytes 262144 | tf_op jit(solution)/shard_map/finish/pallas_call | solution.py:27
  (55 shorter events, 4.0 us)
Async XLA Ops:
  0.0 1.2 %copy-start = (bf16[256,2048]{1,0:T(8,128)(2,1)S(1)}, bf16[256,2048]{1,0:T(8,128)(2,1)}, u32[]{:S(2)}) copy-start(bf16[256,2048]{1,0:T(8,128)(2,1)} %frames_ref.3) | copy-start | bytes 3145732
  1.2 5.7 %collective-permute-start = (bf16[16,2048]{1,0:T(8,128)(2,1)S(1)}, bf16[16,2048]{1,0:T(8,128)(2,1)S(1)}, u32[]{:S(2)}, u32[]{:S(2)}) collective-permute-start(bf16[16,2048]{1,0:T(8,128)(2,1)S(1)} %get-tuple-element.40), channel_id=1, source_target_pairs={{0,16},{8,24},{16,0},{24,8},{1,17},{9,25},{17,1},{25,9},{2,18},{10... | collective-permute-start | bytes 196616 | tf_op jit(solution)/shard_map/ppermute | solution.py:391
  4.2 4.9 %collective-permute-start.1 = (bf16[16,2048]{1,0:T(8,128)(2,1)S(1)}, bf16[16,2048]{1,0:T(8,128)(2,1)S(1)}, u32[]{:S(2)}, u32[]{:S(2)}) collective-permute-start(bf16[16,2048]{1,0:T(8,128)(2,1)S(1)} %get-tuple-element.42), channel_id=1, source_target_pairs={{0,8},{8,0},{16,24},{24,16},{1,9},{9,1},{17,25},{25,17},{2,10},{10... | collective-permute-start | bytes 196616 | tf_op jit(solution)/shard_map/ppermute | solution.py:391
  4.3 0.7 %copy-start.2 = (f32[2048]{0:T(1024)S(1)}, f32[2048]{0:T(1024)}, u32[]{:S(2)}) copy-start(f32[2048]{0:T(1024)} %dead_ref.3) | copy-start | bytes 24580
  5.0 0.7 %copy-start.3 = (s32[2048]{0:T(1024)S(1)}, s32[2048]{0:T(1024)}, u32[]{:S(2)}) copy-start(s32[2048]{0:T(1024)} %width_ref.3) | copy-start | bytes 24580
  7.0 6.5 %copy-start.4 = (s32[2048]{0:T(1024)S(1)}, s32[2048]{0:T(1024)}, u32[]{:S(2)}) copy-start(s32[2048]{0:T(1024)} %label_ref.1) | copy-start | bytes 24580
  7.0 6.5 %copy-start.5 = (s32[2048]{0:T(1024)S(1)}, s32[2048]{0:T(1024)}, u32[]{:S(2)}) copy-start(s32[2048]{0:T(1024)} %valid_ref.1) | copy-start | bytes 24580
  7.0 2.2 %collective-permute-start.2 = (bf16[16,2048]{1,0:T(8,128)(2,1)S(1)}, bf16[16,2048]{1,0:T(8,128)(2,1)S(1)}, u32[]{:S(2)}, u32[]{:S(2)}) collective-permute-start(bf16[16,2048]{1,0:T(8,128)(2,1)S(1)} %hold.6), channel_id=1, source_target_pairs={{0,8},{8,0},{16,24},{24,16},{1,9},{9,1},{17,25},{25,17},{2,10},{10... | collective-permute-start | bytes 196616 | tf_op jit(solution)/shard_map/ppermute | solution.py:391
  7.6 14.9 %collective-permute-start.7 = (bf16[128,2048]{1,0:T(8,128)(2,1)S(1)}, bf16[128,2048]{1,0:T(8,128)(2,1)S(1)}, u32[]{:S(2)}, u32[]{:S(2)}) collective-permute-start(bf16[128,2048]{1,0:T(8,128)(2,1)S(1)} %hold.5.refs_1_.mid_ref), channel_id=1, source_target_pairs={{0,16},{8,24},{16,0},{24,8},{1,17},{9,25},{17,1},{25,9},{2,18},{10... | collective-permute-start | bytes 1572872 | tf_op jit(solution)/shard_map/ppermute | solution.py:391
  8.6 3.4 %collective-permute-start.3 = (bf16[64,2048]{1,0:T(8,128)(2,1)S(1)}, bf16[64,2048]{1,0:T(8,128)(2,1)S(1)}, u32[]{:S(2)}, u32[]{:S(2)}) collective-permute-start(bf16[64,2048]{1,0:T(8,128)(2,1)S(1)} %get-tuple-element.80), channel_id=1, source_target_pairs={{0,8},{8,0},{16,24},{24,16},{1,9},{9,1},{17,25},{25,17},{2,10},{10... | collective-permute-start | bytes 786440 | tf_op jit(solution)/shard_map/ppermute | solution.py:391
  8.9 4.3 %collective-permute-start.4 = (bf16[64,2048]{1,0:T(8,128)(2,1)S(1)}, bf16[64,2048]{1,0:T(8,128)(2,1)S(1)}, u32[]{:S(2)}, u32[]{:S(2)}) collective-permute-start(bf16[64,2048]{1,0:T(8,128)(2,1)S(1)} %get-tuple-element.79), channel_id=1, source_target_pairs={{0,8},{8,0},{16,24},{24,16},{1,9},{9,1},{17,25},{25,17},{2,10},{10... | collective-permute-start | bytes 786440 | tf_op jit(solution)/shard_map/ppermute | solution.py:391
  11.4 1.7 %copy-start.6 = (bf16[64,2048]{1,0:T(8,128)(2,1)}, bf16[64,2048]{1,0:T(8,128)(2,1)S(1)}, u32[]{:S(2)}) copy-start(bf16[64,2048]{1,0:T(8,128)(2,1)S(1)} %get-tuple-element.59) | copy-start | bytes 786436
  11.5 1.6 %collective-permute-start.5 = (bf16[64,2048]{1,0:T(8,128)(2,1)S(1)}, bf16[64,2048]{1,0:T(8,128)(2,1)S(1)}, u32[]{:S(2)}, u32[]{:S(2)}) collective-permute-start(bf16[64,2048]{1,0:T(8,128)(2,1)S(1)} %get-tuple-element.78), channel_id=1, source_target_pairs={{0,8},{8,0},{16,24},{24,16},{1,9},{9,1},{17,25},{25,17},{2,10},{10... | collective-permute-start | bytes 786440 | tf_op jit(solution)/shard_map/ppermute | solution.py:391
  11.8 1.7 %collective-permute-start.6 = (bf16[64,2048]{1,0:T(8,128)(2,1)S(1)}, bf16[64,2048]{1,0:T(8,128)(2,1)S(1)}, u32[]{:S(2)}, u32[]{:S(2)}) collective-permute-start(bf16[64,2048]{1,0:T(8,128)(2,1)S(1)} %get-tuple-element.77), channel_id=1, source_target_pairs={{0,8},{8,0},{16,24},{24,16},{1,9},{9,1},{17,25},{25,17},{2,10},{10... | collective-permute-start | bytes 786440 | tf_op jit(solution)/shard_map/ppermute | solution.py:391
  12.1 15.6 %collective-permute-start.16 = (bf16[64,2048]{1,0:T(8,128)(2,1)}, bf16[64,2048]{1,0:T(8,128)(2,1)}, u32[]{:S(2)}, u32[]{:S(2)}) collective-permute-start(bf16[64,2048]{1,0:T(8,128)(2,1)} %get-tuple-element.60), channel_id=1, source_target_pairs={{0,16},{8,24},{16,0},{24,8},{1,17},{9,25},{17,1},{25,9},{2,18},{10... | collective-permute-start | bytes 786440 | tf_op jit(solution)/shard_map/ppermute | solution.py:391
  15.7 0.8 %copy-start.1 = (bf16[8,72,512]{2,1,0:T(8,128)(2,1)}, bf16[8,72,512]{2,1,0:T(8,128)(2,1)S(1)}, u32[]{:S(2)}) copy-start(bf16[8,72,512]{2,1,0:T(8,128)(2,1)S(1)} %get-tuple-element.44) | copy-start | bytes 1769476
  16.5 31.4 %all-to-all-start = ((bf16[8,72,512]{2,1,0:T(8,128)(2,1)}), bf16[8,72,512]{2,1,0:T(8,128)(2,1)}, u32[]{:S(2)}, u32[]{:S(2)}) async-start(bf16[8,72,512]{2,1,0:T(8,128)(2,1)} %copy-done.1), calls=%async_computation | async-start | bytes 1179648 | tf_op jit(solution)/shard_map/all_to_all | solution.py:431
  22.4 1.6 %copy-start.7 = (bf16[64,2048]{1,0:T(8,128)(2,1)S(1)}, bf16[64,2048]{1,0:T(8,128)(2,1)}, u32[]{:S(2)}) copy-start(bf16[64,2048]{1,0:T(8,128)(2,1)} %copy-done.6) | copy-start | bytes 786436
  22.5 1.4 %collective-permute-start.10 = (bf16[32,2048]{1,0:T(8,128)(2,1)S(1)}, bf16[32,2048]{1,0:T(8,128)(2,1)S(1)}, u32[]{:S(2)}, u32[]{:S(2)}) collective-permute-start(bf16[32,2048]{1,0:T(8,128)(2,1)S(1)} %get-tuple-element.74), channel_id=1, source_target_pairs={{0,8},{8,0},{16,24},{24,16},{1,9},{9,1},{17,25},{25,17},{2,10},{10... | collective-permute-start | bytes 393224 | tf_op jit(solution)/shard_map/ppermute | solution.py:391
  22.6 2.3 %collective-permute-start.11 = (bf16[32,2048]{1,0:T(8,128)(2,1)S(1)}, bf16[32,2048]{1,0:T(8,128)(2,1)S(1)}, u32[]{:S(2)}, u32[]{:S(2)}) collective-permute-start(bf16[32,2048]{1,0:T(8,128)(2,1)S(1)} %get-tuple-element.73), channel_id=1, source_target_pairs={{0,8},{8,0},{16,24},{24,16},{1,9},{9,1},{17,25},{25,17},{2,10},{10... | collective-permute-start | bytes 393224 | tf_op jit(solution)/shard_map/ppermute | solution.py:391
  23.1 1.8 %collective-permute-start.8 = (bf16[32,2048]{1,0:T(8,128)(2,1)S(1)}, bf16[32,2048]{1,0:T(8,128)(2,1)S(1)}, u32[]{:S(2)}, u32[]{:S(2)}) collective-permute-start(bf16[32,2048]{1,0:T(8,128)(2,1)S(1)} %get-tuple-element.76), channel_id=1, source_target_pairs={{0,8},{8,0},{16,24},{24,16},{1,9},{9,1},{17,25},{25,17},{2,10},{10... | collective-permute-start | bytes 393224 | tf_op jit(solution)/shard_map/ppermute | solution.py:391
  23.2 1.8 %collective-permute-start.9 = (bf16[32,2048]{1,0:T(8,128)(2,1)S(1)}, bf16[32,2048]{1,0:T(8,128)(2,1)S(1)}, u32[]{:S(2)}, u32[]{:S(2)}) collective-permute-start(bf16[32,2048]{1,0:T(8,128)(2,1)S(1)} %get-tuple-element.75), channel_id=1, source_target_pairs={{0,8},{8,0},{16,24},{24,16},{1,9},{9,1},{17,25},{25,17},{2,10},{10... | collective-permute-start | bytes 393224 | tf_op jit(solution)/shard_map/ppermute | solution.py:391
  23.9 8.8 %collective-permute-start.15 = (bf16[64,2048]{1,0:T(8,128)(2,1)S(1)}, bf16[64,2048]{1,0:T(8,128)(2,1)S(1)}, u32[]{:S(2)}, u32[]{:S(2)}) collective-permute-start(bf16[64,2048]{1,0:T(8,128)(2,1)S(1)} %copy-done.7), channel_id=1, source_target_pairs={{0,16},{8,24},{16,0},{24,8},{1,17},{9,25},{17,1},{25,9},{2,18},{10... | collective-permute-start | bytes 786440 | tf_op jit(solution)/shard_map/ppermute | solution.py:391
  28.6 2.3 %collective-permute-start.17 = (bf16[48,2048]{1,0:T(8,128)(2,1)S(1)}, bf16[48,2048]{1,0:T(8,128)(2,1)S(1)}, u32[]{:S(2)}, u32[]{:S(2)}) collective-permute-start(bf16[48,2048]{1,0:T(8,128)(2,1)S(1)} %slice.46), channel_id=1, source_target_pairs={{0,8},{8,0},{16,24},{24,16},{1,9},{9,1},{17,25},{25,17},{2,10},{10... | collective-permute-start | bytes 589832 | tf_op jit(solution)/shard_map/ppermute | solution.py:391
  29.5 1.4 %collective-permute-start.18 = (bf16[16,2048]{1,0:T(8,128)(2,1)S(1)}, bf16[16,2048]{1,0:T(8,128)(2,1)S(1)}, u32[]{:S(2)}, u32[]{:S(2)}) collective-permute-start(bf16[16,2048]{1,0:T(8,128)(2,1)S(1)} %slice.47), channel_id=1, source_target_pairs={{0,8},{8,0},{16,24},{24,16},{1,9},{9,1},{17,25},{25,17},{2,10},{10... | collective-permute-start | bytes 196616 | tf_op jit(solution)/shard_map/ppermute | solution.py:391
  32.8 1.5 %collective-permute-start.19 = (bf16[64,2048]{1,0:T(8,128)(2,1)S(1)}, bf16[64,2048]{1,0:T(8,128)(2,1)S(1)}, u32[]{:S(2)}, u32[]{:S(2)}) collective-permute-start(bf16[64,2048]{1,0:T(8,128)(2,1)S(1)} %hold.9.refs_0_), channel_id=1, source_target_pairs={{0,8},{8,0},{16,24},{24,16},{1,9},{9,1},{17,25},{25,17},{2,10},{10... | collective-permute-start | bytes 786440 | tf_op jit(solution)/shard_map/ppermute | solution.py:391
  33.1 6.1 %collective-permute-start.12 = (bf16[264,256]{1,0:T(8,128)(2,1)S(1)}, bf16[264,256]{1,0:T(8,128)(2,1)S(1)}, u32[]{:S(2)}, u32[]{:S(2)}) collective-permute-start(bf16[264,256]{1,0:T(8,128)(2,1)S(1)} %get-tuple-element.51), channel_id=1, source_target_pairs={{0,1},{1,0},{2,3},{3,2},{4,5},{5,4},{6,7},{7,6},{8,9},{9,8},{10,11... | collective-permute-start | bytes 405512 | tf_op jit(solution)/shard_map/ppermute | solution.py:391
  35.1 6.5 %collective-permute-start.20 = (bf16[264,256]{1,0:T(8,128)(2,1)S(1)}, bf16[264,256]{1,0:T(8,128)(2,1)S(1)}, u32[]{:S(2)}, u32[]{:S(2)}) collective-permute-start(bf16[264,256]{1,0:T(8,128)(2,1)S(1)} %get-tuple-element.65), channel_id=1, source_target_pairs={{0,2},{1,3},{2,0},{3,1},{4,6},{5,7},{6,4},{7,5},{8,10},{9,11},{10,... | collective-permute-start | bytes 405512 | tf_op jit(solution)/shard_map/ppermute | solution.py:391
  39.2 4.4 %collective-permute-start.13 = (bf16[136,256]{1,0:T(8,128)(2,1)S(1)}, bf16[136,256]{1,0:T(8,128)(2,1)S(1)}, u32[]{:S(2)}, u32[]{:S(2)}) collective-permute-start(bf16[136,256]{1,0:T(8,128)(2,1)S(1)} %get-tuple-element.54), channel_id=1, source_target_pairs={{0,2},{1,3},{2,0},{3,1},{4,6},{5,7},{6,4},{7,5},{8,10},{9,11},{10,... | collective-permute-start | bytes 208904 | tf_op jit(solution)/shard_map/ppermute | solution.py:391
  41.6 4.4 %collective-permute-start.21 = (bf16[136,256]{1,0:T(8,128)(2,1)S(1)}, bf16[136,256]{1,0:T(8,128)(2,1)S(1)}, u32[]{:S(2)}, u32[]{:S(2)}) collective-permute-start(bf16[136,256]{1,0:T(8,128)(2,1)S(1)} %get-tuple-element.68), channel_id=1, source_target_pairs={{0,1},{1,0},{2,3},{3,2},{4,5},{5,4},{6,7},{7,6},{8,9},{9,8},{10,11... | collective-permute-start | bytes 208904 | tf_op jit(solution)/shard_map/ppermute | solution.py:391
  43.6 6.0 %collective-permute-start.14 = (bf16[80,256]{1,0:T(8,128)(2,1)S(1)}, bf16[80,256]{1,0:T(8,128)(2,1)S(1)}, u32[]{:S(2)}, u32[]{:S(2)}) collective-permute-start(bf16[80,256]{1,0:T(8,128)(2,1)S(1)} %get-tuple-element.57), channel_id=1, source_target_pairs={{0,4},{1,5},{2,6},{3,7},{4,0},{5,1},{6,2},{7,3},{8,12},{9,13},{10,... | collective-permute-start | bytes 122888 | tf_op jit(solution)/shard_map/ppermute | solution.py:391
  46.0 5.0 %collective-permute-start.22 = (bf16[80,256]{1,0:T(8,128)(2,1)S(1)}, bf16[80,256]{1,0:T(8,128)(2,1)S(1)}, u32[]{:S(2)}, u32[]{:S(2)}) collective-permute-start(bf16[80,256]{1,0:T(8,128)(2,1)S(1)} %get-tuple-element.71), channel_id=1, source_target_pairs={{0,4},{1,5},{2,6},{3,7},{4,0},{5,1},{6,2},{7,3},{8,12},{9,13},{10,... | collective-permute-start | bytes 122888 | tf_op jit(solution)/shard_map/ppermute | solution.py:391
